TPU v7x, 512 devices: a whole 4x8x8 slice. The times are simulated.
512 devices in a mesh: band: 128 (over z, y, core), chan: 4 (over x).
Axes of the slice: x: 4, y: 8, z: 8, core: 2. Of those that a mesh axis runs over, the one named last changes fastest.
Arguments:
- grid_state: bfloat16 [65536, 227], P('band'), may hold values from -8 to 8
- mesh_latent: bfloat16 [32768, 512], P('band', 'chan'), may hold values from -6 to 6
- w_in: bfloat16 [227, 512], P(None, 'chan'), may hold values from -0.375 to 0.375
- w_enc_src: bfloat16 [512, 512], P(None, 'chan'), may hold values from -0.25 to 0.25
- w_enc_dst: bfloat16 [512, 512], P(None, 'chan'), may hold values from -0.25 to 0.25
- w_enc_out: bfloat16 [512, 512], P(None, 'chan'), may hold values from -0.25 to 0.25
- w_proc: bfloat16 [2, 3, 512, 512], P(None, None, None, 'chan'), may hold values from -0.25 to 0.25
- w_dec_src: bfloat16 [512, 512], P(None, 'chan'), may hold values from -0.25 to 0.25
- w_dec_dst: bfloat16 [512, 512], P(None, 'chan'), may hold values from -0.25 to 0.25
- w_out: bfloat16 [512, 227], P('chan'), may hold values from -0.25 to 0.25
- enc_src: int32 [640, 512], P('band'), may hold values from 0 to 511
- enc_dst: int32 [640, 512], P('band'), may hold values from -1 to 255, as said below
- local_src: int32 [128, 1024], P('band'), may hold values from 0 to 255
- local_dst: int32 [128, 1024], P('band'), may hold values from 0 to 255
- proc_src: int32 [640, 128], P('band'), may hold values from 0 to 255
- proc_dst: int32 [640, 128], P('band'), may hold values from -1 to 255, as said below
- dec_src: int32 [640, 512], P('band'), may hold values from 0 to 255
- dec_dst: int32 [640, 512], P('band'), may hold values from -1 to 511, as said below
Outputs:
- increment: bfloat16 [65536, 227], P('band')
Inputs may be any that keep to these rules, and one draw needn't show every extreme that they name: `enc_dst`: row a * 5 + j lists the grid-to-mesh edges from band a to partition (a + j - 2) mod 128; the filled slots of a row come first, the others hold -1; every row fills at least a quarter of its slots. `proc_dst`: row a * 5 + j lists the mesh edges from partition a to partition (a + j - 2) mod 128; the filled slots of a row come first, the others hold -1; every row fills at least a quarter of its slots. `dec_dst`: row a * 5 + j lists the mesh-to-grid edges from partition a to band (a + j - 2) mod 128; the filled slots of a row come first, the others hold -1; every row fills at least a quarter of its slots.
All inputs are finite; a program needn't handle non-finite values.
Results may differ from a plain program's by a relative error of at most 0.015.
Values may be sent and summed in bfloat16 or wider, within the bound.
No kernel may reach another device: no remote copies, remote signals or barrier semaphores. Data moves between devices by JAX's collectives and lax.ppermute only.
A program may use at most 64 MiB of HBM per device.

v0:
```python
import jax
import jax.numpy as jnp
from jax import lax
from jax.sharding import PartitionSpec as P

EPS = 1e-05


def shifted(value, axis, steps):
    count = lax.axis_size(axis)
    pairs = [(source, (source + steps) % count) for source in range(count)]
    return lax.ppermute(value, axis, pairs)


def normalize(values):
    values = values.astype(jnp.float32)
    return values * lax.rsqrt(jnp.mean(values * values, axis=-1, keepdims=True) + EPS)


def project(row_block, weight):
    return jnp.dot(row_block, weight, preferred_element_type=jnp.float32)


def edge_terms(sent_rows, targets, receiver):
    picked = jnp.take(receiver, jnp.maximum(targets, 0), axis=0)
    return jax.nn.silu(sent_rows.astype(jnp.float32) + picked.astype(jnp.float32))


def collect(message, targets, node_count):
    channels = message.shape[-1]
    segment_ids = jnp.where(targets < 0, node_count, targets).reshape(-1)
    summed = jax.ops.segment_sum(
        message.reshape(-1, channels), segment_ids, num_segments=node_count + 1
    )
    return summed[:node_count]


def deliver(rows, targets):
    count = rows.shape[0]
    center = count // 2
    got_rows = [None] * count
    got_targets = [None] * count
    got_rows[center] = rows[center]
    got_targets[center] = targets[center]
    for index in range(count):
        offset = index - center
        if offset != 0:
            got_rows[index], got_targets[index] = shifted(
                (rows[index], targets[index]), "band", offset
            )
    return (jnp.stack(got_rows), jnp.stack(got_targets))


def gather_sum(sent_rows, sources, targets, receiver, node_count):
    arrived_rows, arrived_targets = deliver(jnp.take(sent_rows, sources, axis=0), targets)
    return collect(edge_terms(arrived_rows, arrived_targets, receiver), arrived_targets, node_count)


def on_device(
    grid_state,
    mesh_latent,
    w_in,
    w_enc_src,
    w_enc_dst,
    w_enc_out,
    w_proc,
    w_dec_src,
    w_dec_dst,
    w_out,
    enc_src,
    enc_dst,
    local_src,
    local_dst,
    proc_src,
    proc_dst,
    dec_src,
    dec_dst,
):
    grid_count = grid_state.shape[0]
    mesh_count = mesh_latent.shape[0]
    own_part = jax.nn.silu(project(grid_state, w_in)).astype(jnp.bfloat16)
    grid_latent = lax.all_gather(own_part, "chan", axis=1, tiled=True)
    grid_normed = normalize(grid_latent).astype(jnp.bfloat16)
    enc_send = project(grid_normed, w_enc_src).astype(jnp.bfloat16)
    mesh_full = lax.all_gather(mesh_latent, "chan", axis=1, tiled=True)
    mesh_normed = normalize(mesh_full).astype(jnp.bfloat16)
    enc_recv = project(mesh_normed, w_enc_dst).astype(jnp.bfloat16)
    enc_agg = gather_sum(enc_send, enc_src, enc_dst, enc_recv, mesh_count).astype(jnp.bfloat16)
    agg_full = lax.all_gather(enc_agg, "chan", axis=1, tiled=True)
    mesh_state = mesh_latent.astype(jnp.float32) + project(
        normalize(agg_full).astype(jnp.bfloat16), w_enc_out
    )
    inner_src = local_src.reshape(-1)
    inner_dst = local_dst.reshape(-1)
    for layer_index in range(w_proc.shape[0]):
        mesh_rounded = mesh_state.astype(jnp.bfloat16)
        mesh_full = lax.all_gather(mesh_rounded, "chan", axis=1, tiled=True)
        proc_normed = normalize(mesh_full).astype(jnp.bfloat16)
        proc_send = project(proc_normed, w_proc[layer_index, 0]).astype(jnp.bfloat16)
        proc_recv = project(proc_normed, w_proc[layer_index, 1]).astype(jnp.bfloat16)
        remote_sum = gather_sum(proc_send, proc_src, proc_dst, proc_recv, mesh_count)
        inside = edge_terms(jnp.take(proc_send, inner_src, axis=0), inner_dst, proc_recv)
        inside_sum = jax.ops.segment_sum(inside, inner_dst, num_segments=mesh_count)
        proc_agg = (remote_sum + inside_sum).astype(jnp.bfloat16)
        agg_full = lax.all_gather(proc_agg, "chan", axis=1, tiled=True)
        mesh_state = mesh_state + project(
            normalize(agg_full).astype(jnp.bfloat16), w_proc[layer_index, 2]
        )
    mesh_rounded = mesh_state.astype(jnp.bfloat16)
    mesh_full = lax.all_gather(mesh_rounded, "chan", axis=1, tiled=True)
    dec_normed = normalize(mesh_full).astype(jnp.bfloat16)
    dec_send = project(dec_normed, w_dec_src).astype(jnp.bfloat16)
    dec_recv = project(grid_normed, w_dec_dst).astype(jnp.bfloat16)
    dec_agg = gather_sum(dec_send, dec_src, dec_dst, dec_recv, grid_count).astype(jnp.bfloat16)
    agg_full = lax.all_gather(dec_agg, "chan", axis=1, tiled=True)
    full_out = lax.all_gather(w_out, "chan", axis=0, tiled=True)
    combined = agg_full.astype(jnp.float32) + grid_latent.astype(jnp.float32)
    increment = project(normalize(combined).astype(jnp.bfloat16), full_out).astype(jnp.bfloat16)
    return increment


def solution(mesh):
    placed = (
        P("band", None),
        P("band", "chan"),
        P(None, "chan"),
        P(None, "chan"),
        P(None, "chan"),
        P(None, "chan"),
        P(None, None, None, "chan"),
        P(None, "chan"),
        P(None, "chan"),
        P("chan", None),
        P("band", None),
        P("band", None),
        P("band", None),
        P("band", None),
        P("band", None),
        P("band", None),
        P("band", None),
        P("band", None),
    )
    return jax.shard_map(
        on_device, mesh=mesh, in_specs=placed, out_specs=P("band", None), check_vma=False
    )
```

profile of v0, /device:TPU:1, one launch (start us, length us, event | category | flops | bytes accessed | tf_op | source)
XLA Modules:
  0.0 370.3 jit_solution(5133640768847401282)
XLA Ops:
  0.9 14.4 %collective-permute-start = (s32[512]{0:T(512)S(1)}, s32[512]{0:T(512)S(1)}, u32[]{:S(2)}, u32[]{:S(2)}) collective-permute-start(s32[512]{0:T(512)S(1)} %bitcast.184), channel_id=1, source_target_pairs={{0,504},{4,508},{8,0},{12,4},{16,8},{20,12},{24,16},{28,20},{32,24... | collective-permute-start | bytes 6152 | tf_op jit(solution)/shard_map/ppermute | solution.py:12
  34.4 12.0 %all_gather.30 = bf16[512,512]{1,0:T(8,128)(2,1)S(1)} all-gather(bf16[512,128]{1,0:T(8,128)(2,1)S(1)} %multiply_convert_fusion.2), channel_id=1, replica_groups=mesh['band'=128,'chan'=4] {'chan'}, dimensions={1}, use_global_device_ids=true | all-gather | bytes 655360 | tf_op jit(solution)/shard_map/all_gather | solution.py:82
  46.7 9.2 %all_gather.31 = bf16[256,512]{1,0:T(8,128)(2,1)S(1)} all-gather(bf16[256,128]{1,0:T(8,128)(2,1)S(1)} %copy-done.1), channel_id=1, replica_groups=mesh['band'=128,'chan'=4] {'chan'}, dimensions={1}, use_global_device_ids=true | all-gather | bytes 327680 | tf_op jit(solution)/shard_map/all_gather | solution.py:85
  57.9 7.3 %collective-permute-start.1 = (s32[512]{0:T(512)S(1)}, s32[512]{0:T(512)S(1)}, u32[]{:S(2)}, u32[]{:S(2)}) collective-permute-start(s32[512]{0:T(512)S(1)} %bitcast.182), channel_id=1, source_target_pairs={{0,508},{4,0},{8,4},{12,8},{16,12},{20,16},{24,20},{28,24},{32,28}... | collective-permute-start | bytes 6152 | tf_op jit(solution)/shard_map/ppermute | solution.py:12
  77.9 9.9 %collective-permute-start.4 = (s32[512]{0:T(512)S(1)}, s32[512]{0:T(512)S(1)}, u32[]{:S(2)}, u32[]{:S(2)}) collective-permute-start(s32[512]{0:T(512)S(1)} %bitcast.178), channel_id=1, source_target_pairs={{0,504},{4,508},{8,0},{12,4},{16,8},{20,12},{24,16},{28,20},{32,24... | collective-permute-start | bytes 6152 | tf_op jit(solution)/shard_map/ppermute | solution.py:12
  87.9 5.1 %gather_fusion = bf16[2560,128]{1,0:T(8,128)(2,1)S(1)} fusion(bf16[512,128]{1,0:T(8,128)(2,1)S(1)} %convolution_convert_fusion.2, s32[3072]{0:T(1024)S(1)} %get-tuple-element.49), kind=kCustom, calls=%fused_computation.clone | custom fusion | bytes 1320960 | tf_op jit(solution)/shard_map/jit(_take)/gather | solution.py:55
  99.8 3.4 collective-permute-done.9
  105.2 5.1 %gather_fusion.1 = bf16[2560,128]{1,0:T(8,128)(2,1)S(1)} fusion(bf16[256,128]{1,0:T(8,128)(2,1)S(1)} %convolution_convert_fusion.8, s32[3072]{0:T(1024)S(1)} %pad_clamp_fusion.2), kind=kCustom, calls=%fused_computation.1.clone | custom fusion | bytes 1320960 | tf_op jit(solution)/shard_map/jit(_take)/gather | solution.py:25
  112.9 7.8 %collective-permute-done.11 = bf16[512,128]{1,0:T(8,128)(2,1)S(1)} collective-permute-done((bf16[512,128]{1,0:T(8,128)(2,1)S(1)}, bf16[512,128]{1,0:T(8,128)(2,1)S(1)}, u32[]{:S(2)}, u32[]{:S(2)}) %collective-permute-start.11) | collective-permute-done | bytes 131104 | tf_op jit(solution)/shard_map/ppermute | solution.py:12
  122.0 15.5 %scatter_custom_fusion = f32[257,128]{1,0:T(8,128)S(1)} fusion(s32[2560]{0:T(1024)} %fusion.85, f32[2560,128]{1,0:T(8,128)S(1)} %bitcast.159, f32[]{:T(128)} %constant.46.clone.1), kind=kCustom, calls=%fused_computation.149 | custom fusion | flops 327680 | bytes 132096 | tf_op jit(solution)/shard_map/scatter-add | solution.py:32
  137.5 10.0 %all_gather.32 = bf16[256,512]{1,0:T(8,128)(2,1)S(1)} all-gather(bf16[256,128]{1,0:T(8,128)(2,1)S(1)} %slice.302), channel_id=1, replica_groups=mesh['band'=128,'chan'=4] {'chan'}, dimensions={1}, use_global_device_ids=true | all-gather | bytes 327680 | tf_op jit(solution)/shard_map/all_gather | solution.py:89
  148.8 9.7 %all_gather.33 = bf16[256,512]{1,0:T(8,128)(2,1)S(1)} all-gather(bf16[256,128]{1,0:T(8,128)(2,1)S(1)} %get-tuple-element.44), channel_id=1, replica_groups=mesh['band'=128,'chan'=4] {'chan'}, dimensions={1}, use_global_device_ids=true | all-gather | bytes 327680 | tf_op jit(solution)/shard_map/all_gather | solution.py:97
  164.1 7.4 %collective-permute-start.17 = (bf16[128,128]{1,0:T(8,128)(2,1)S(1)}, bf16[128,128]{1,0:T(8,128)(2,1)S(1)}, u32[]{:S(2)}, u32[]{:S(2)}) collective-permute-start(bf16[128,128]{1,0:T(8,128)(2,1)S(1)} %get-tuple-element.27), channel_id=1, source_target_pairs={{0,508},{4,0},{8,4},{12,8},{16,12},{20,16},{24,20},{28,24},{32,28}... | collective-permute-start | bytes 98312 | tf_op jit(solution)/shard_map/ppermute | solution.py:12
  180.9 6.0 %collective-permute-done.19 = bf16[128,128]{1,0:T(8,128)(2,1)S(1)} collective-permute-done((bf16[128,128]{1,0:T(8,128)(2,1)S(1)}, bf16[128,128]{1,0:T(8,128)(2,1)S(1)}, u32[]{:S(2)}, u32[]{:S(2)}) %collective-permute-start.19) | collective-permute-done | bytes 32800 | tf_op jit(solution)/shard_map/ppermute | solution.py:12
  187.2 6.3 %scatter_custom_fusion.1 = f32[257,128]{1,0:T(8,128)S(1)} fusion(s32[640]{0:T(1024)S(1)} %fusion.89, f32[640,128]{1,0:T(8,128)S(1)} %bitcast.165, f32[]{:T(128)} %constant.46.clone.1), kind=kCustom, calls=%fused_computation.147 | custom fusion | flops 81920 | bytes 131588 | tf_op jit(solution)/shard_map/scatter-add | solution.py:32
  193.5 12.8 %scatter_custom_fusion.2 = f32[256,128]{1,0:T(8,128)S(1)} fusion(f32[256,128]{1,0:T(8,128)S(1)} %slice.222, s32[1024]{0:T(1024)} %bitcast.175, f32[]{:T(128)} %constant.57.clone.1, pred[1024]{0:T(1024)(128)(4,1)S(1)} %copy-done.10, pred[1024]{0:T(1024)(128)(4,1)S(1)} %copy-done.11, bf16[]{:T(256)} %constant.20.clone.2, ...), kind=kCustom, calls=%fused_computation.80 | custom fusion | flops 1310720 | bytes 273408 | tf_op jit(solution)/shard_map/scatter-add | solution.py:103
  206.3 9.7 %all_gather.34 = bf16[256,512]{1,0:T(8,128)(2,1)S(1)} all-gather(bf16[256,128]{1,0:T(8,128)(2,1)S(1)} %convert_element_type.162), channel_id=1, replica_groups=mesh['band'=128,'chan'=4] {'chan'}, dimensions={1}, use_global_device_ids=true | all-gather | bytes 327680 | tf_op jit(solution)/shard_map/all_gather | solution.py:105
  216.4 9.6 %all_gather.35 = bf16[256,512]{1,0:T(8,128)(2,1)S(1)} all-gather(bf16[256,128]{1,0:T(8,128)(2,1)S(1)} %get-tuple-element.46), channel_id=1, replica_groups=mesh['band'=128,'chan'=4] {'chan'}, dimensions={1}, use_global_device_ids=true | all-gather | bytes 327680 | tf_op jit(solution)/shard_map/all_gather | solution.py:97
  230.6 7.7 %collective-permute-start.21 = (bf16[128,128]{1,0:T(8,128)(2,1)S(1)}, bf16[128,128]{1,0:T(8,128)(2,1)S(1)}, u32[]{:S(2)}, u32[]{:S(2)}) collective-permute-start(bf16[128,128]{1,0:T(8,128)(2,1)S(1)} %get-tuple-element.22), channel_id=1, source_target_pairs={{0,508},{4,0},{8,4},{12,8},{16,12},{20,16},{24,20},{28,24},{32,28}... | collective-permute-start | bytes 98312 | tf_op jit(solution)/shard_map/ppermute | solution.py:12
  247.4 6.0 %collective-permute-done.23 = bf16[128,128]{1,0:T(8,128)(2,1)S(1)} collective-permute-done((bf16[128,128]{1,0:T(8,128)(2,1)S(1)}, bf16[128,128]{1,0:T(8,128)(2,1)S(1)}, u32[]{:S(2)}, u32[]{:S(2)}) %collective-permute-start.23) | collective-permute-done | bytes 32800 | tf_op jit(solution)/shard_map/ppermute | solution.py:12
  253.7 6.3 %scatter_custom_fusion.3 = f32[257,128]{1,0:T(8,128)S(1)} fusion(s32[640]{0:T(1024)S(1)} %fusion.89, f32[640,128]{1,0:T(8,128)S(1)} %bitcast.164, f32[]{:T(128)} %constant.46.clone.1), kind=kCustom, calls=%fused_computation.145 | custom fusion | flops 81920 | bytes 131588 | tf_op jit(solution)/shard_map/scatter-add | solution.py:32
  260.0 12.8 %scatter_custom_fusion.4 = f32[256,128]{1,0:T(8,128)S(1)} fusion(f32[256,128]{1,0:T(8,128)S(1)} %slice.228, s32[1024]{0:T(1024)} %bitcast.176, f32[]{:T(128)} %constant.57.clone.1, pred[1024]{0:T(1024)(128)(4,1)S(1)} %copy-done.10, pred[1024]{0:T(1024)(128)(4,1)S(1)} %copy-done.11, bf16[]{:T(256)} %constant.20.clone.2, ...), kind=kCustom, calls=%fused_computation.71 | custom fusion | flops 1310720 | bytes 273408 | tf_op jit(solution)/shard_map/scatter-add | solution.py:103
  272.8 9.6 %all_gather.36 = bf16[256,512]{1,0:T(8,128)(2,1)S(1)} all-gather(bf16[256,128]{1,0:T(8,128)(2,1)S(1)} %convert_element_type.174), channel_id=1, replica_groups=mesh['band'=128,'chan'=4] {'chan'}, dimensions={1}, use_global_device_ids=true | all-gather | bytes 327680 | tf_op jit(solution)/shard_map/all_gather | solution.py:105
  282.8 9.7 %all_gather.37 = bf16[256,512]{1,0:T(8,128)(2,1)S(1)} all-gather(bf16[256,128]{1,0:T(8,128)(2,1)S(1)} %fusion), channel_id=1, replica_groups=mesh['band'=128,'chan'=4] {'chan'}, dimensions={1}, use_global_device_ids=true | all-gather | bytes 327680 | tf_op jit(solution)/shard_map/all_gather | solution.py:110
  292.9 5.1 %gather_fusion.6 = bf16[2560,128]{1,0:T(8,128)(2,1)S(1)} fusion(bf16[256,128]{1,0:T(8,128)(2,1)S(1)} %convolution_convert_fusion.3, s32[3072]{0:T(1024)S(1)} %pad_clamp_fusion.1), kind=kCustom, calls=%fused_computation.5.clone | custom fusion | bytes 1320960 | tf_op jit(solution)/shard_map/jit(_take)/gather | solution.py:55
  300.9 9.2 %all_gather.39 = bf16[512,227]{0,1:T(8,128)(2,1)} all-gather(bf16[128,227]{0,1:T(8,128)(2,1)S(1)} %copy-done.4), channel_id=1, replica_groups=mesh['band'=128,'chan'=4] {'chan'}, dimensions={0}, use_global_device_ids=true | all-gather | bytes 290560 | tf_op jit(solution)/shard_map/all_gather | solution.py:116
  310.1 10.3 %collective-permute-start.25 = (bf16[512,128]{1,0:T(8,128)(2,1)S(1)}, bf16[512,128]{1,0:T(8,128)(2,1)S(1)}, u32[]{:S(2)}, u32[]{:S(2)}) collective-permute-start(bf16[512,128]{1,0:T(8,128)(2,1)S(1)} %get-tuple-element.12), channel_id=1, source_target_pairs={{0,508},{4,0},{8,4},{12,8},{16,12},{20,16},{24,20},{28,24},{32,28}... | collective-permute-start | bytes 393224 | tf_op jit(solution)/shard_map/ppermute | solution.py:12
  320.4 4.2 %collective-permute-done.25 = bf16[512,128]{1,0:T(8,128)(2,1)S(1)} collective-permute-done((bf16[512,128]{1,0:T(8,128)(2,1)S(1)}, bf16[512,128]{1,0:T(8,128)(2,1)S(1)}, u32[]{:S(2)}, u32[]{:S(2)}) %collective-permute-start.25) | collective-permute-done | bytes 131104 | tf_op jit(solution)/shard_map/ppermute | solution.py:12
  326.7 5.1 %gather_fusion.7 = bf16[2560,128]{1,0:T(8,128)(2,1)S(1)} fusion(bf16[512,128]{1,0:T(8,128)(2,1)S(1)} %convolution_convert_fusion.1, s32[3072]{0:T(1024)S(1)} %get-tuple-element.48), kind=kCustom, calls=%fused_computation.4.clone | custom fusion | bytes 1320960 | tf_op jit(solution)/shard_map/jit(_take)/gather | solution.py:25
  333.8 7.8 %collective-permute-done.27 = bf16[512,128]{1,0:T(8,128)(2,1)S(1)} collective-permute-done((bf16[512,128]{1,0:T(8,128)(2,1)S(1)}, bf16[512,128]{1,0:T(8,128)(2,1)S(1)}, u32[]{:S(2)}, u32[]{:S(2)}) %collective-permute-start.27) | collective-permute-done | bytes 131104 | tf_op jit(solution)/shard_map/ppermute | solution.py:12
  342.3 15.2 %scatter_custom_fusion.5 = f32[513,128]{1,0:T(8,128)S(1)} fusion(s32[2560]{0:T(1024)S(1)} %fusion.84, f32[2560,128]{1,0:T(8,128)S(1)} %bitcast.158, f32[]{:T(128)} %constant.46.clone.1), kind=kCustom, calls=%fused_computation.110 | custom fusion | flops 327680 | bytes 262660 | tf_op jit(solution)/shard_map/scatter-add | solution.py:32
  357.5 11.4 %all_gather.38 = bf16[512,512]{1,0:T(8,128)(2,1)S(1)} all-gather(bf16[512,128]{1,0:T(8,128)(2,1)S(1)} %slice.301), channel_id=1, replica_groups=mesh['band'=128,'chan'=4] {'chan'}, dimensions={1}, use_global_device_ids=true | all-gather | bytes 655360 | tf_op jit(solution)/shard_map/all_gather | solution.py:115
  (193 shorter events, 87.6 us)
Async XLA Ops:
  0.0 33.2 %copy-start = (bf16[512,227]{0,1:T(8,128)(2,1)S(1)}, bf16[512,227]{0,1:T(8,128)(2,1)}, u32[]{:S(2)}) copy-start(bf16[512,227]{0,1:T(8,128)(2,1)} %param.26) | copy-start | bytes 697348
  0.9 72.1 %collective-permute-start = (s32[512]{0:T(512)S(1)}, s32[512]{0:T(512)S(1)}, u32[]{:S(2)}, u32[]{:S(2)}) collective-permute-start(s32[512]{0:T(512)S(1)} %bitcast.184), channel_id=1, source_target_pairs={{0,504},{4,508},{8,0},{12,4},{16,8},{20,12},{24,16},{28,20},{32,24... | collective-permute-start | bytes 6152 | tf_op jit(solution)/shard_map/ppermute | solution.py:12
  16.2 41.7 %collective-permute-start.12 = (s32[128]{0:T(128)S(1)}, s32[128]{0:T(128)S(1)}, u32[]{:S(2)}, u32[]{:S(2)}) collective-permute-start(s32[128]{0:T(128)S(1)} %get-tuple-element.42), channel_id=1, source_target_pairs={{0,504},{4,508},{8,0},{12,4},{16,8},{20,12},{24,16},{28,20},{32,24... | collective-permute-start | bytes 1544 | tf_op jit(solution)/shard_map/ppermute | solution.py:12
  19.2 46.0 %collective-permute-start.13 = (s32[128]{0:T(128)S(1)}, s32[128]{0:T(128)S(1)}, u32[]{:S(2)}, u32[]{:S(2)}) collective-permute-start(s32[128]{0:T(128)S(1)} %get-tuple-element.41), channel_id=1, source_target_pairs={{0,508},{4,0},{8,4},{12,8},{16,12},{20,16},{24,20},{28,24},{32,28}... | collective-permute-start | bytes 1544 | tf_op jit(solution)/shard_map/ppermute | solution.py:12
  22.3 44.8 %collective-permute-start.14 = (s32[128]{0:T(128)S(1)}, s32[128]{0:T(128)S(1)}, u32[]{:S(2)}, u32[]{:S(2)}) collective-permute-start(s32[128]{0:T(128)S(1)} %get-tuple-element.43), channel_id=1, source_target_pairs={{0,4},{4,8},{8,12},{12,16},{16,20},{20,24},{24,28},{28,32},{32,36}... | collective-permute-start | bytes 1544 | tf_op jit(solution)/shard_map/ppermute | solution.py:12
  24.8 44.4 %collective-permute-start.15 = (s32[128]{0:T(128)S(1)}, s32[128]{0:T(128)S(1)}, u32[]{:S(2)}, u32[]{:S(2)}) collective-permute-start(s32[128]{0:T(128)S(1)} %get-tuple-element.39), channel_id=1, source_target_pairs={{0,8},{4,12},{8,16},{12,20},{16,24},{20,28},{24,32},{28,36},{32,40... | collective-permute-start | bytes 1544 | tf_op jit(solution)/shard_map/ppermute | solution.py:12
  57.9 18.0 %collective-permute-start.1 = (s32[512]{0:T(512)S(1)}, s32[512]{0:T(512)S(1)}, u32[]{:S(2)}, u32[]{:S(2)}) collective-permute-start(s32[512]{0:T(512)S(1)} %bitcast.182), channel_id=1, source_target_pairs={{0,508},{4,0},{8,4},{12,8},{16,12},{20,16},{24,20},{28,24},{32,28}... | collective-permute-start | bytes 6152 | tf_op jit(solution)/shard_map/ppermute | solution.py:12
  65.2 12.7 %collective-permute-start.2 = (s32[512]{0:T(512)S(1)}, s32[512]{0:T(512)S(1)}, u32[]{:S(2)}, u32[]{:S(2)}) collective-permute-start(s32[512]{0:T(512)S(1)} %bitcast.180), channel_id=1, source_target_pairs={{0,4},{4,8},{8,12},{12,16},{16,20},{20,24},{24,28},{28,32},{32,36}... | collective-permute-start | bytes 6152 | tf_op jit(solution)/shard_map/ppermute | solution.py:12
  67.2 20.6 %collective-permute-start.3 = (s32[512]{0:T(512)S(1)}, s32[512]{0:T(512)S(1)}, u32[]{:S(2)}, u32[]{:S(2)}) collective-permute-start(s32[512]{0:T(512)S(1)} %bitcast.177), channel_id=1, source_target_pairs={{0,8},{4,12},{8,16},{12,20},{16,24},{20,28},{24,32},{28,36},{32,40... | collective-permute-start | bytes 6152 | tf_op jit(solution)/shard_map/ppermute | solution.py:12
  69.2 27.7 %collective-permute-start.5 = (s32[512]{0:T(512)S(1)}, s32[512]{0:T(512)S(1)}, u32[]{:S(2)}, u32[]{:S(2)}) collective-permute-start(s32[512]{0:T(512)S(1)} %bitcast.183), channel_id=1, source_target_pairs={{0,508},{4,0},{8,4},{12,8},{16,12},{20,16},{24,20},{28,24},{32,28}... | collective-permute-start | bytes 6152 | tf_op jit(solution)/shard_map/ppermute | solution.py:12
  73.1 25.8 %collective-permute-start.6 = (s32[512]{0:T(512)S(1)}, s32[512]{0:T(512)S(1)}, u32[]{:S(2)}, u32[]{:S(2)}) collective-permute-start(s32[512]{0:T(512)S(1)} %bitcast.181), channel_id=1, source_target_pairs={{0,4},{4,8},{8,12},{12,16},{16,20},{20,24},{24,28},{28,32},{32,36}... | collective-permute-start | bytes 6152 | tf_op jit(solution)/shard_map/ppermute | solution.py:12
  75.9 22.9 %collective-permute-start.7 = (s32[512]{0:T(512)S(1)}, s32[512]{0:T(512)S(1)}, u32[]{:S(2)}, u32[]{:S(2)}) collective-permute-start(s32[512]{0:T(512)S(1)} %bitcast.179), channel_id=1, source_target_pairs={{0,8},{4,12},{8,16},{12,20},{16,24},{20,28},{24,32},{28,36},{32,40... | collective-permute-start | bytes 6152 | tf_op jit(solution)/shard_map/ppermute | solution.py:12
  77.9 20.9 %collective-permute-start.4 = (s32[512]{0:T(512)S(1)}, s32[512]{0:T(512)S(1)}, u32[]{:S(2)}, u32[]{:S(2)}) collective-permute-start(s32[512]{0:T(512)S(1)} %bitcast.178), channel_id=1, source_target_pairs={{0,504},{4,508},{8,0},{12,4},{16,8},{20,12},{24,16},{28,20},{32,24... | collective-permute-start | bytes 6152 | tf_op jit(solution)/shard_map/ppermute | solution.py:12
  93.5 6.3 %collective-permute-start.8 = (bf16[512,128]{1,0:T(8,128)(2,1)S(1)}, bf16[512,128]{1,0:T(8,128)(2,1)S(1)}, u32[]{:S(2)}, u32[]{:S(2)}) collective-permute-start(bf16[512,128]{1,0:T(8,128)(2,1)S(1)} %get-tuple-element.18), channel_id=1, source_target_pairs={{0,504},{4,508},{8,0},{12,4},{16,8},{20,12},{24,16},{28,20},{32,24... | collective-permute-start | bytes 393224 | tf_op jit(solution)/shard_map/ppermute | solution.py:12
  96.9 6.3 %collective-permute-start.9 = (bf16[512,128]{1,0:T(8,128)(2,1)S(1)}, bf16[512,128]{1,0:T(8,128)(2,1)S(1)}, u32[]{:S(2)}, u32[]{:S(2)}) collective-permute-start(bf16[512,128]{1,0:T(8,128)(2,1)S(1)} %get-tuple-element.17), channel_id=1, source_target_pairs={{0,508},{4,0},{8,4},{12,8},{16,12},{20,16},{24,20},{28,24},{32,28}... | collective-permute-start | bytes 393224 | tf_op jit(solution)/shard_map/ppermute | solution.py:12
  103.2 9.6 %collective-permute-start.10 = (bf16[512,128]{1,0:T(8,128)(2,1)S(1)}, bf16[512,128]{1,0:T(8,128)(2,1)S(1)}, u32[]{:S(2)}, u32[]{:S(2)}) collective-permute-start(bf16[512,128]{1,0:T(8,128)(2,1)S(1)} %get-tuple-element.15), channel_id=1, source_target_pairs={{0,4},{4,8},{8,12},{12,16},{16,20},{20,24},{24,28},{28,32},{32,36}... | collective-permute-start | bytes 393224 | tf_op jit(solution)/shard_map/ppermute | solution.py:12
  110.9 9.8 %collective-permute-start.11 = (bf16[512,128]{1,0:T(8,128)(2,1)S(1)}, bf16[512,128]{1,0:T(8,128)(2,1)S(1)}, u32[]{:S(2)}, u32[]{:S(2)}) collective-permute-start(bf16[512,128]{1,0:T(8,128)(2,1)S(1)} %get-tuple-element.14), channel_id=1, source_target_pairs={{0,8},{4,12},{8,16},{12,20},{16,24},{20,28},{24,32},{28,36},{32,40... | collective-permute-start | bytes 393224 | tf_op jit(solution)/shard_map/ppermute | solution.py:12
  122.0 38.0 %copy-start.7 = (s32[1024]{0:T(1024)S(1)}, s32[1024]{0:T(1024)}, u32[]{:S(2)}) copy-start(s32[1024]{0:T(1024)} %get-tuple-element.51) | copy-start | bytes 12292
  162.2 9.4 %collective-permute-start.16 = (bf16[128,128]{1,0:T(8,128)(2,1)S(1)}, bf16[128,128]{1,0:T(8,128)(2,1)S(1)}, u32[]{:S(2)}, u32[]{:S(2)}) collective-permute-start(bf16[128,128]{1,0:T(8,128)(2,1)S(1)} %get-tuple-element.28), channel_id=1, source_target_pairs={{0,504},{4,508},{8,0},{12,4},{16,8},{20,12},{24,16},{28,20},{32,24... | collective-permute-start | bytes 98312 | tf_op jit(solution)/shard_map/ppermute | solution.py:12
  164.1 10.6 %collective-permute-start.17 = (bf16[128,128]{1,0:T(8,128)(2,1)S(1)}, bf16[128,128]{1,0:T(8,128)(2,1)S(1)}, u32[]{:S(2)}, u32[]{:S(2)}) collective-permute-start(bf16[128,128]{1,0:T(8,128)(2,1)S(1)} %get-tuple-element.27), channel_id=1, source_target_pairs={{0,508},{4,0},{8,4},{12,8},{16,12},{20,16},{24,20},{28,24},{32,28}... | collective-permute-start | bytes 98312 | tf_op jit(solution)/shard_map/ppermute | solution.py:12
  174.8 6.2 %collective-permute-start.18 = (bf16[128,128]{1,0:T(8,128)(2,1)S(1)}, bf16[128,128]{1,0:T(8,128)(2,1)S(1)}, u32[]{:S(2)}, u32[]{:S(2)}) collective-permute-start(bf16[128,128]{1,0:T(8,128)(2,1)S(1)} %get-tuple-element.25), channel_id=1, source_target_pairs={{0,4},{4,8},{8,12},{12,16},{16,20},{20,24},{24,28},{28,32},{32,36}... | collective-permute-start | bytes 98312 | tf_op jit(solution)/shard_map/ppermute | solution.py:12
  179.0 8.0 %collective-permute-start.19 = (bf16[128,128]{1,0:T(8,128)(2,1)S(1)}, bf16[128,128]{1,0:T(8,128)(2,1)S(1)}, u32[]{:S(2)}, u32[]{:S(2)}) collective-permute-start(bf16[128,128]{1,0:T(8,128)(2,1)S(1)} %get-tuple-element.24), channel_id=1, source_target_pairs={{0,8},{4,12},{8,16},{12,20},{16,24},{20,28},{24,32},{28,36},{32,40... | collective-permute-start | bytes 98312 | tf_op jit(solution)/shard_map/ppermute | solution.py:12
  228.6 9.7 %collective-permute-start.20 = (bf16[128,128]{1,0:T(8,128)(2,1)S(1)}, bf16[128,128]{1,0:T(8,128)(2,1)S(1)}, u32[]{:S(2)}, u32[]{:S(2)}) collective-permute-start(bf16[128,128]{1,0:T(8,128)(2,1)S(1)} %get-tuple-element.23), channel_id=1, source_target_pairs={{0,504},{4,508},{8,0},{12,4},{16,8},{20,12},{24,16},{28,20},{32,24... | collective-permute-start | bytes 98312 | tf_op jit(solution)/shard_map/ppermute | solution.py:12
  230.6 10.7 %collective-permute-start.21 = (bf16[128,128]{1,0:T(8,128)(2,1)S(1)}, bf16[128,128]{1,0:T(8,128)(2,1)S(1)}, u32[]{:S(2)}, u32[]{:S(2)}) collective-permute-start(bf16[128,128]{1,0:T(8,128)(2,1)S(1)} %get-tuple-element.22), channel_id=1, source_target_pairs={{0,508},{4,0},{8,4},{12,8},{16,12},{20,16},{24,20},{28,24},{32,28}... | collective-permute-start | bytes 98312 | tf_op jit(solution)/shard_map/ppermute | solution.py:12
  241.3 6.1 %collective-permute-start.22 = (bf16[128,128]{1,0:T(8,128)(2,1)S(1)}, bf16[128,128]{1,0:T(8,128)(2,1)S(1)}, u32[]{:S(2)}, u32[]{:S(2)}) collective-permute-start(bf16[128,128]{1,0:T(8,128)(2,1)S(1)} %get-tuple-element.20), channel_id=1, source_target_pairs={{0,4},{4,8},{8,12},{12,16},{16,20},{20,24},{24,28},{28,32},{32,36}... | collective-permute-start | bytes 98312 | tf_op jit(solution)/shard_map/ppermute | solution.py:12
  245.5 8.0 %collective-permute-start.23 = (bf16[128,128]{1,0:T(8,128)(2,1)S(1)}, bf16[128,128]{1,0:T(8,128)(2,1)S(1)}, u32[]{:S(2)}, u32[]{:S(2)}) collective-permute-start(bf16[128,128]{1,0:T(8,128)(2,1)S(1)} %get-tuple-element.19), channel_id=1, source_target_pairs={{0,8},{4,12},{8,16},{12,20},{16,24},{20,28},{24,32},{28,36},{32,40... | collective-permute-start | bytes 98312 | tf_op jit(solution)/shard_map/ppermute | solution.py:12
  253.7 39.0 %copy-start.19 = (bf16[512,128]{1,0:T(8,128)(2,1)S(1)}, bf16[512,128]{1,0:T(8,128)(2,1)}, u32[]{:S(2)}) copy-start(bf16[512,128]{1,0:T(8,128)(2,1)} %param.33) | copy-start | bytes 393220
  298.6 21.8 %collective-permute-start.24 = (bf16[512,128]{1,0:T(8,128)(2,1)S(1)}, bf16[512,128]{1,0:T(8,128)(2,1)S(1)}, u32[]{:S(2)}, u32[]{:S(2)}) collective-permute-start(bf16[512,128]{1,0:T(8,128)(2,1)S(1)} %get-tuple-element.13), channel_id=1, source_target_pairs={{0,504},{4,508},{8,0},{12,4},{16,8},{20,12},{24,16},{28,20},{32,24... | collective-permute-start | bytes 393224 | tf_op jit(solution)/shard_map/ppermute | solution.py:12
  310.1 14.6 %collective-permute-start.25 = (bf16[512,128]{1,0:T(8,128)(2,1)S(1)}, bf16[512,128]{1,0:T(8,128)(2,1)S(1)}, u32[]{:S(2)}, u32[]{:S(2)}) collective-permute-start(bf16[512,128]{1,0:T(8,128)(2,1)S(1)} %get-tuple-element.12), channel_id=1, source_target_pairs={{0,508},{4,0},{8,4},{12,8},{16,12},{20,16},{24,20},{28,24},{32,28}... | collective-permute-start | bytes 393224 | tf_op jit(solution)/shard_map/ppermute | solution.py:12
  324.7 9.0 %collective-permute-start.26 = (bf16[512,128]{1,0:T(8,128)(2,1)S(1)}, bf16[512,128]{1,0:T(8,128)(2,1)S(1)}, u32[]{:S(2)}, u32[]{:S(2)}) collective-permute-start(bf16[512,128]{1,0:T(8,128)(2,1)S(1)} %get-tuple-element.8), channel_id=1, source_target_pairs={{0,4},{4,8},{8,12},{12,16},{16,20},{20,24},{24,28},{28,32},{32,36}... | collective-permute-start | bytes 393224 | tf_op jit(solution)/shard_map/ppermute | solution.py:12
  331.8 9.8 %collective-permute-start.27 = (bf16[512,128]{1,0:T(8,128)(2,1)S(1)}, bf16[512,128]{1,0:T(8,128)(2,1)S(1)}, u32[]{:S(2)}, u32[]{:S(2)}) collective-permute-start(bf16[512,128]{1,0:T(8,128)(2,1)S(1)} %get-tuple-element.6), channel_id=1, source_target_pairs={{0,8},{4,12},{8,16},{12,20},{16,24},{20,28},{24,32},{28,36},{32,40... | collective-permute-start | bytes 393224 | tf_op jit(solution)/shard_map/ppermute | solution.py:12
  342.3 26.9 %copy-start.2 = (bf16[512,227]{0,1:T(8,128)(2,1)S(1)}, bf16[512,227]{0,1:T(8,128)(2,1)}, u32[]{:S(2)}) copy-start(bf16[512,227]{0,1:T(8,128)(2,1)} %all_gather.39) | copy-start | bytes 697348
  (17 other events, 229.3 us)
where the time goes:
time: 373 us; the launch traced here: 370 us
  starting transfers between devices  106 us (28%)
  blocking collectives  100 us (27%)
  other arithmetic  83.1 us (22%)
  waiting for transfers between devices  41.7 us (11%)
  local copies, waits for them, and re-layouts  31.2 us (8%)
  matrix products  7.32 us (2%)
    ppermute x28, starting transfers between devices, shifted(): return lax.ppermute(value, axis, pairs)  106 us
    scatter-add x4, other arithmetic, collect(): jax.ops.segment_sum(message.reshape(-1, channels), segment_ids, num_segme...  43.2 us
    ppermute x28, waiting for transfers between devices, shifted(): return lax.ppermute(value, axis, pairs)  41.7 us
    all_gather x3, blocking collectives, on_device(): mesh_full = lax.all_gather(mesh_rounded, 'chan', axis=1, tiled=True)  29 us
    scatter-add x2, other arithmetic, on_device(): inside_sum = jax.ops.segment_sum(inside, inner_dst, num_segments=mesh_count)  25.5 us
    all_gather x2, blocking collectives, on_device(): agg_full = lax.all_gather(proc_agg, 'chan', axis=1, tiled=True)  19.3 us
    gather x4, local copies, waits for them, and re-layouts, edge_terms(): picked = jnp.take(receiver, jnp.maximum(targets, 0), axis=0)  14.1 us
    gather x4, local copies, waits for them, and re-layouts, gather_sum(): jnp.take(sent_rows, sources, axis=0)  14.1 us
  transfers between devices with their start and end apart: 28, of which 9 were waited for; matrix products, arithmetic and copies ran while one was open for 9% of the time, Pallas kernels for 0%

commit v1 on v0

v1 whole, which is shorter than its diff:
```python
import jax
import jax.numpy as jnp
from jax import lax
from jax.experimental import pallas as pl
from jax.experimental.pallas import tpu as pltpu
from jax.sharding import Mesh, PartitionSpec as P

EPS = 1e-05
F32 = jnp.float32
BF16 = jnp.bfloat16
I32 = jnp.int32
LANES = 128
TILE = 32
TABLES = 5


def rms(values):
    values = values.astype(F32)
    return values * lax.rsqrt(jnp.mean(values * values, axis=-1, keepdims=True) + EPS)


def silu(values):
    return 0.5 * values * (1.0 + jnp.tanh(0.5 * values))


def dot(a, b):
    return lax.dot_general(a, b, (((1,), (0,)), ((), ())), preferred_element_type=F32)


def dot_first(a, b):
    return lax.dot_general(a, b, (((0,), (0,)), ((), ())), preferred_element_type=F32)


def dot_last(a, b):
    return lax.dot_general(a, b, (((1,), (1,)), ((), ())), preferred_element_type=F32)


def wide(ref, start, size):
    return jnp.concatenate([ref[c, start : start + size, :] for c in range(ref.shape[0])], axis=1)


def one_hot(row, count):
    nodes = lax.broadcasted_iota(I32, (count, row.shape[1]), 0)
    return jnp.where(nodes == row, 1.0, 0.0).astype(BF16)


def code_table(digits, table, core, rows_used):
    width = table.shape[1]
    value = table[...] + 1
    digits[...] = jnp.zeros_like(digits)
    digits[0:5, 0:width] = (value >> 4).astype(F32)
    digits[8:13, 0:width] = (value & 15).astype(F32)
    row = lax.broadcasted_iota(I32, (TILE, 16), 0)
    col = lax.broadcasted_iota(I32, (TILE, 16), 1)
    near = row & 15
    base = jnp.where((row >> 4) == core, 3, 0)
    wanted = (near & 1) * 8 + base + ((near >> 1) & 1)
    total = None
    for k in range(width // LANES):
        pick = jnp.where((col == wanted) & ((near >> 2) == k + rows_used), 1.0, 0.0).astype(BF16)
        part = dot(pick, digits[:, k * LANES : (k + 1) * LANES].astype(BF16))
        total = part if total is None else total + part
    return total


def decode(tile, offset, second):
    row = lax.broadcasted_iota(I32, (8, TILE), 0)
    col = lax.broadcasted_iota(I32, (8, TILE), 1)
    place = offset + (row & 3) * 4 + second * 2
    weight = jnp.where(col == place, 16.0, jnp.where(col == place + 1, 1.0, 0.0))
    return dot(weight.astype(BF16), tile).astype(I32) - 1


def pre_kernel(
    grid_state, big, w_es, w_ed, w_dd, enc_src, enc_dst, dec_src, dec_dst, proc_src, proc_dst,
    payload, enc_recv, dec_recv, latent, digits,
):
    core = lax.axis_index("core")
    channels = grid_state.shape[1]
    nodes = grid_state.shape[0]
    grid_latent = silu(dot(grid_state[...], wide(big, 0, channels))).astype(BF16)
    latent[...] = grid_latent
    grid_normed = rms(grid_latent).astype(BF16)
    payload[0:nodes, :] = dot(grid_normed, w_es[...]).astype(BF16)
    dec_recv[...] = dot(grid_normed, w_dd[...]).astype(BF16)
    mesh_count = enc_recv.shape[0]
    mesh_normed = rms(wide(big, big.shape[1] - mesh_count, mesh_count)).astype(BF16)
    enc_recv[...] = dot(mesh_normed, w_ed[...]).astype(BF16)
    for t, table in enumerate((enc_src, enc_dst, dec_src, dec_dst)):
        start = nodes + t * TILE
        payload[start : start + TILE, :] = code_table(digits, table, core, 0).astype(BF16)
    start = nodes + 4 * TILE
    both = code_table(digits, proc_src, core, 0) + code_table(digits, proc_dst, core, 1)
    payload[start : start + TILE, :] = both.astype(BF16)


def add_edges(total, send_t, recv_t, src, dst, send_count, recv_count):
    to = one_hot(dst, recv_count)
    message = silu(dot(send_t, one_hot(src, send_count)) + dot(recv_t, to)).astype(BF16)
    part = dot_last(message, to)
    return part if total is None else total + part


def flat(rows, start, count):
    return jnp.concatenate([rows[start + k : start + k + 1, :] for k in range(count)], axis=1)


def places(core):
    sib = 1 - core
    return (
        ("two", 0, core * 16, 1),
        ("two", 1, 16 - core * 16, 0),
        ("pair", sib, 0, sib),
        ("far", core, 16, core),
    )


def transposed(values):
    return values.astype(F32).T.astype(BF16)


def enc_kernel(
    pair, two, recv, enc_src, enc_dst,
    agg, proc_tab, dec_tab,
):
    core = lax.axis_index("core")
    sib = 1 - core
    recv_count = recv.shape[0]
    send_count = pair.shape[1] - TABLES * TILE
    recv_t = transposed(recv[...])
    total = add_edges(
        None, transposed(pair[core, 0:send_count, :]), recv_t, enc_src[2:3, :], enc_dst[2:3, :],
        send_count, recv_count,
    )
    for v, (kind, place, offset, second) in enumerate(places(core)):
        if kind == "two":
            block = two.at[core, place]
        elif kind == "pair":
            block = pair.at[sib]
        else:
            block = two.at[sib, core]
        lists = [
            decode(block[send_count + t * TILE : send_count + (t + 1) * TILE, :], offset, second)
            for t in range(TABLES)
        ]
        total = add_edges(
            total, transposed(block[0:send_count, :]), recv_t, flat(lists[0], 0, 4), flat(lists[1], 0, 4),
            send_count, recv_count,
        )
        dec_tab[0, v] = lists[2]
        dec_tab[1, v] = lists[3]
        proc_tab[v] = lists[4]
    agg[...] = total.T.astype(BF16)


def node_kernel(has_recv, agg4, state, weights, w_send, *rest):
    if has_recv:
        w_recv, new_state, send, recv = rest
    else:
        (send,) = rest
    count = agg4.shape[1]
    agg = wide(agg4, 0, count)
    if len(state.shape) == 3:
        before = wide(state, state.shape[1] - count, count).astype(F32)
    else:
        before = state[...]
    after = before + dot(rms(agg).astype(BF16), wide(weights, 0, weights.shape[1]))
    normed = rms(after.astype(BF16)).astype(BF16)
    send[...] = dot(normed, w_send[...]).astype(BF16)
    if has_recv:
        new_state[...] = after
        recv[...] = dot(normed, w_recv[...]).astype(BF16)


def proc_kernel(pair, two, recv, local_src, local_dst, proc_src, proc_dst, tab, agg):
    core = lax.axis_index("core")
    sib = 1 - core
    count = recv.shape[0]
    recv_t = transposed(recv[...])
    own_src = jnp.concatenate([local_src[...], proc_src[2:3, :]], axis=1)
    own_dst = jnp.concatenate([local_dst[...], proc_dst[2:3, :]], axis=1)
    total = add_edges(None, transposed(pair[core]), recv_t, own_src, own_dst, count, count)
    for v, block in enumerate((two.at[core, 0], two.at[core, 1], pair.at[sib], two.at[sib, core])):
        lists = tab[v]
        total = add_edges(
            total, transposed(block[...]), recv_t, lists[0:1, :], lists[1:2, :], count, count
        )
    agg[...] = total.T.astype(BF16)


def dec_kernel(pair, two, recv, dec_src, dec_dst, tab, agg):
    core = lax.axis_index("core")
    sib = 1 - core
    recv_count = recv.shape[0]
    send_count = pair.shape[1]
    recv_t = transposed(recv[...])
    total = add_edges(
        None, transposed(pair[core]), recv_t, dec_src[2:3, :], dec_dst[2:3, :], send_count, recv_count
    )
    for v, block in enumerate((two.at[core, 0], two.at[core, 1], pair.at[sib], two.at[sib, core])):
        total = add_edges(
            total, transposed(block[...]), recv_t, flat(tab[0, v], 0, 4), flat(tab[1, v], 0, 4),
            send_count, recv_count,
        )
    agg[...] = total.T.astype(BF16)


def out_kernel(agg4, latent, weights, out):
    combined = wide(agg4, 0, agg4.shape[1]).astype(F32) + latent[...].astype(F32)
    normed = rms(combined).astype(BF16)
    rows = weights.shape[1]
    parts = weights.shape[0]
    low = jnp.concatenate([weights[c, rows - 256 : rows - 128, :] for c in range(parts)], axis=0)
    high = jnp.concatenate([weights[c, rows - 128 : rows, :] for c in range(parts)], axis=0)
    columns = out.shape[1]
    out[:, 0:LANES] = dot(normed, low).astype(BF16)
    out[:, LANES:columns] = dot(normed, high)[:, 0 : columns - LANES].astype(BF16)


def call(kernel, out_shapes, *args, scratch=()):
    return pl.pallas_call(
        kernel,
        out_shape=out_shapes,
        in_specs=[pl.BlockSpec(memory_space=pltpu.VMEM)] * len(args),
        out_specs=jax.tree.map(lambda _: pl.BlockSpec(memory_space=pltpu.VMEM), out_shapes),
        scratch_shapes=scratch,
        compiler_params=pltpu.CompilerParams(vmem_limit_bytes=40 * 1024 * 1024),
    )(*args)


def shape(dims, kind=BF16):
    return jax.ShapeDtypeStruct(dims, kind)


def chan_gather(block):
    count = lax.axis_size("chan")
    copies = jnp.broadcast_to(block[None], (count,) + block.shape)
    return lax.all_to_all(copies, "chan", 0, 0, tiled=True)


def around(block):
    pair = lax.all_gather(block, "core")
    parts = lax.axis_size(("pair", "core"))
    swap = [(s, (s + 1) % parts if s % 2 else (s - 1) % parts) for s in range(parts)]
    got = lax.ppermute(pair, ("pair", "core"), swap)
    return pair, lax.all_gather(got, "core")


def on_device(
    grid_state, mesh_latent, w_in, w_enc_src, w_enc_dst, w_enc_out, w_proc, w_dec_src, w_dec_dst, w_out,
    enc_src, enc_dst, local_src, local_dst, proc_src, proc_dst, dec_src, dec_dst,
):
    grid_count, channels = grid_state.shape
    mesh_count, width = mesh_latent.shape
    chans = lax.axis_size("chan")
    latent_width = width * chans

    w_out_pad = jnp.pad(w_out, ((0, 0), (0, 2 * LANES - channels)))
    late = jnp.concatenate(
        [w_enc_out, w_proc[0, 2], w_proc[1, 2], w_out_pad[:, :LANES], w_out_pad[:, LANES:]], axis=0
    )
    late = lax.all_gather(late, "chan")
    updates = [late[:, i * latent_width : (i + 1) * latent_width] for i in range(3)]

    early = jnp.concatenate([jnp.pad(w_in, ((0, 2 * LANES - channels), (0, 0))), mesh_latent], axis=0)
    big = chan_gather(early)

    payload, recv, dec_recv, grid_latent = call(
        pre_kernel,
        (
            shape((grid_count + TABLES * TILE, width)),
            shape((mesh_count, width)),
            shape((grid_count, width)),
            shape((grid_count, latent_width)),
        ),
        grid_state, big, w_enc_src, w_enc_dst, w_dec_dst,
        enc_src, enc_dst, dec_src, dec_dst, proc_src, proc_dst,
        scratch=[pltpu.VMEM((16, enc_src.shape[1]), F32)],
    )
    pair, two = around(payload)
    agg, proc_tab, dec_tab = call(
        enc_kernel,
        (shape((mesh_count, width)), shape((4, 8, LANES), I32), shape((2, 4, 8, LANES), I32)),
        pair, two, recv, enc_src, enc_dst,
    )
    state = big
    for layer in range(w_proc.shape[0]):
        state, send, recv = call(
            lambda *refs: node_kernel(True, *refs),
            (shape((mesh_count, latent_width), F32), shape((mesh_count, width)), shape((mesh_count, width))),
            chan_gather(agg), state, updates[layer], w_proc[layer, 0], w_proc[layer, 1],
        )
        pair, two = around(send)
        agg = call(
            proc_kernel, shape((mesh_count, width)),
            pair, two, recv, local_src, local_dst, proc_src, proc_dst, proc_tab,
        )
    send = call(
        lambda *refs: node_kernel(False, *refs[:4], refs[4]), shape((mesh_count, width)),
        chan_gather(agg), state, updates[2], w_dec_src,
    )
    pair, two = around(send)
    agg = call(
        dec_kernel, shape((grid_count, width)), pair, two, dec_recv, dec_src, dec_dst, dec_tab
    )
    return call(out_kernel, shape((grid_count, channels)), chan_gather(agg), grid_latent, late)


def solution(mesh):
    bands, chans = mesh.devices.shape
    split = Mesh(mesh.devices.reshape(bands // 2, 2, chans), ("pair", "core", "chan"))
    band = ("pair", "core")
    placed = (
        P(band, None),
        P(band, "chan"),
        P(None, "chan"),
        P(None, "chan"),
        P(None, "chan"),
        P(None, "chan"),
        P(None, None, None, "chan"),
        P(None, "chan"),
        P(None, "chan"),
        P("chan", None),
    ) + (P(band, None),) * 8
    return jax.shard_map(
        on_device, mesh=split, in_specs=placed, out_specs=P(band, None), check_vma=False
    )
```

time: 373 us -> 155 us (0.42)
  starting transfers between devices: 106 us -> 15.9 us
  other arithmetic: 83.1 us -> 0.88 us
  blocking collectives: 100 us -> 70.9 us
  local copies, waits for them, and re-layouts: 31.2 us -> 10.3 us
  between operations: 1.22 us -> 13.8 us
  Pallas kernels: 0 us -> 10.8 us
  waiting for transfers between devices: 41.7 us -> 31.5 us
  matrix products: 7.32 us -> 0 us
    ppermute x28 -> x4, starting transfers between devices: 106 us -> 7.63 us  [around(): got = lax.ppermute(pair, ('pair', 'core'), swap)]
    scatter-add x6 -> x0, other arithmetic: 68.7 us -> none  [the longest x4 43.2 us: collect(): jax.ops.segment_sum(message.reshape(-1, channels), segment_ids, num_segme...]
    all_gather x10 -> x8, blocking collectives: 100 us -> 41.6 us  [the longest x4 24.6 us: around(): return (pair, lax.all_gather(got, 'core'))]
    all_to_all x0 -> x3, blocking collectives: none -> 29.3 us  [chan_gather(): return lax.all_to_all(copies, 'chan', 0, 0, tiled=True)]
    gather x8 -> x0, local copies, waits for them, and re-layouts: 28.2 us -> none  [the longest x4 14.1 us: edge_terms(): picked = jnp.take(receiver, jnp.maximum(targets, 0), axis=0)]
    ppermute x28 -> x4, waiting for transfers between devices: 41.7 us -> 20.1 us  [around(): got = lax.ppermute(pair, ('pair', 'core'), swap)]
    all_to_all x0 -> x2, waiting for transfers between devices: none -> 11.4 us  [chan_gather(): return lax.all_to_all(copies, 'chan', 0, 0, tiled=True)]
    pallas_call x0 -> x9, Pallas kernels: none -> 10.8 us  [call(): pl.pallas_call(kernel, out_shape=out_shapes, in_specs=[pl.BlockSpec(memor...]
  transfers between devices with their start and end apart: 28 -> 7, of which waited for: 9 -> 6; matrix products, arithmetic and copies ran while one was open for 9% -> 3% of each run, Pallas kernels for 0% -> 2%
where the time goes in v1:
time: 155 us; the launch traced here: 154 us
  blocking collectives  70.9 us (46%)
  waiting for transfers between devices  31.5 us (20%)
  starting transfers between devices  15.9 us (10%)
  between operations  13.8 us (9%)
  Pallas kernels  10.8 us (7%)
  local copies, waits for them, and re-layouts  10.3 us (7%)
    all_to_all x3, blocking collectives, chan_gather(): return lax.all_to_all(copies, 'chan', 0, 0, tiled=True)  29.3 us
    all_gather x4, blocking collectives, around(): return (pair, lax.all_gather(got, 'core'))  24.6 us
    ppermute x4, waiting for transfers between devices, around(): got = lax.ppermute(pair, ('pair', 'core'), swap)  20.1 us
    all_gather x4, blocking collectives, around(): pair = lax.all_gather(block, 'core')  17 us
    all_to_all x2, waiting for transfers between devices, chan_gather(): return lax.all_to_all(copies, 'chan', 0, 0, tiled=True)  11.4 us
    pallas_call x9, Pallas kernels, call(): pl.pallas_call(kernel, out_shape=out_shapes, in_specs=[pl.BlockSpec(memor...  10.8 us
    all_to_all x2, starting transfers between devices, chan_gather(): return lax.all_to_all(copies, 'chan', 0, 0, tiled=True)  8.25 us
    ppermute x4, starting transfers between devices, around(): got = lax.ppermute(pair, ('pair', 'core'), swap)  7.63 us
  transfers between devices with their start and end apart: 7, of which 6 were waited for; matrix products, arithmetic and copies ran while one was open for 3% of the time, Pallas kernels for 2%

profile of v1, /device:TPU:1, one launch (start us, length us, event | category | flops | bytes accessed | tf_op | source)
XLA Modules:
  0.0 154.0 jit_solution(9192447247895755852)
XLA Ops:
  7.6 0.9 constant_dynamic-update-slice_fusion.2
  8.6 1.1 bitcast_dynamic-update-slice_fusion.1
  9.7 0.9 bitcast_dynamic-update-slice_fusion
  13.3 4.8 %all-to-all-start = ((bf16[4,512,128]{2,1,0:T(8,128)(2,1)}), bf16[4,512,128]{2,1,0:T(8,128)(2,1)S(1)}, u32[]{:S(2)}, u32[]{:S(2)}) async-start(bf16[4,512,128]{2,1,0:T(8,128)(2,1)} %broadcast_in_dim.10), calls=%async_computation | async-start | bytes 1048576 | tf_op jit(solution)/shard_map/all_to_all | solution.py:238
  18.2 6.8 %all-to-all-done.big.refs_1_ = bf16[4,512,128]{2,1,0:T(8,128)(2,1)S(1)} async-done(((bf16[4,512,128]{2,1,0:T(8,128)(2,1)}), bf16[4,512,128]{2,1,0:T(8,128)(2,1)S(1)}, u32[]{:S(2)}, u32[]{:S(2)}) %all-to-all-start) | async-done | bytes 524320 | tf_op jit(solution)/shard_map/all_to_all | solution.py:238
  25.1 1.1 shard_map.172
  26.2 8.3 %all-gather = bf16[1344,128]{1,0:T(8,128)(2,1)S(1)} all-gather(bf16[672,128]{1,0:T(8,128)(2,1)S(1)} %get-tuple-element.18), channel_id=2, replica_groups=mesh['pair'=64,'core'=2,'chan'=4] {'core'}, dimensions={0}, use_global_device_ids=true | all-gather | bytes 516096 | tf_op jit(solution)/shard_map/all_gather | solution.py:242
  34.5 1.9 %collective-permute-start = (bf16[2,672,128]{2,1,0:T(8,128)(2,1)S(1)}, bf16[2,672,128]{2,1,0:T(8,128)(2,1)S(1)}, u32[]{:S(2)}, u32[]{:S(2)}) collective-permute-start(bf16[2,672,128]{2,1,0:T(8,128)(2,1)S(1)} %bitcast.24), channel_id=1, source_target_pairs={{0,508},{4,8},{8,4},{12,16},{16,12},{20,24},{24,20},{28,32},{32,28... | collective-permute-start | bytes 1032200 | tf_op jit(solution)/shard_map/ppermute | solution.py:245
  36.4 7.0 %collective-permute-done = bf16[2,672,128]{2,1,0:T(8,128)(2,1)S(1)} collective-permute-done((bf16[2,672,128]{2,1,0:T(8,128)(2,1)S(1)}, bf16[2,672,128]{2,1,0:T(8,128)(2,1)S(1)}, u32[]{:S(2)}, u32[]{:S(2)}) %collective-permute-start) | collective-permute-done | bytes 344096 | tf_op jit(solution)/shard_map/ppermute | solution.py:245
  43.4 8.7 %all-gather.1 = bf16[4,672,128]{2,1,0:T(8,128)(2,1)S(1)} all-gather(bf16[2,672,128]{2,1,0:T(8,128)(2,1)S(1)} %collective-permute-done), channel_id=3, replica_groups=mesh['pair'=64,'core'=2,'chan'=4] {'core'}, dimensions={0}, use_global_device_ids=true | all-gather | bytes 1032192 | tf_op jit(solution)/shard_map/all_gather | solution.py:246
  52.1 2.3 %shard_map.173 = (bf16[256,128]{1,0:T(8,128)(2,1)S(1)}, s32[4,8,128]{2,1,0:T(8,128)S(1)}, s32[2,4,8,128]{3,2,1,0:T(8,128)S(1)}) custom-call(bf16[2,672,128]{2,1,0:T(8,128)(2,1)S(1)} %bitcast.25, bf16[2,2,672,128]{3,2,1,0:T(8,128)(2,1)S(1)} %bitcast.23, bf16[256,128]{1,0:T(8,128)(2,1)S(1)} %get-tuple-element.19.recv, s32[5,512]{1,0:T(8,128)S(1)} %copy-done.5, ...), custom_call_target="tpu_custom_call" | custom-call | tf_op jit(solution)/shard_map/pallas_call | solution.py:221
  56.4 3.4 %all-to-all-start.1 = ((bf16[4,256,128]{2,1,0:T(8,128)(2,1)}), bf16[4,256,128]{2,1,0:T(8,128)(2,1)S(1)}, u32[]{:S(2)}, u32[]{:S(2)}) async-start(bf16[4,256,128]{2,1,0:T(8,128)(2,1)} %broadcast_in_dim.11), calls=%async_computation.1 | async-start | bytes 524288 | tf_op jit(solution)/shard_map/all_to_all | solution.py:238
  59.8 1.5 fusion.2
  61.3 4.6 %all-to-all-done.1.refs_0_ = bf16[4,256,128]{2,1,0:T(8,128)(2,1)S(1)} async-done(((bf16[4,256,128]{2,1,0:T(8,128)(2,1)}), bf16[4,256,128]{2,1,0:T(8,128)(2,1)S(1)}, u32[]{:S(2)}, u32[]{:S(2)}) %all-to-all-start.1) | async-done | bytes 262176 | tf_op jit(solution)/shard_map/all_to_all | solution.py:238
  66.6 3.0 %all-gather.3 = bf16[512,128]{1,0:T(8,128)(2,1)S(1)} all-gather(bf16[256,128]{1,0:T(8,128)(2,1)S(1)} %get-tuple-element.21), channel_id=5, replica_groups=mesh['pair'=64,'core'=2,'chan'=4] {'core'}, dimensions={0}, use_global_device_ids=true | all-gather | bytes 196608 | tf_op jit(solution)/shard_map/all_gather | solution.py:242
  69.7 1.9 %collective-permute-start.1 = (bf16[2,256,128]{2,1,0:T(8,128)(2,1)S(1)}, bf16[2,256,128]{2,1,0:T(8,128)(2,1)S(1)}, u32[]{:S(2)}, u32[]{:S(2)}) collective-permute-start(bf16[2,256,128]{2,1,0:T(8,128)(2,1)S(1)} %bitcast.31), channel_id=1, source_target_pairs={{0,508},{4,8},{8,4},{12,16},{16,12},{20,24},{24,20},{28,32},{32,28... | collective-permute-start | bytes 393224 | tf_op jit(solution)/shard_map/ppermute | solution.py:245
  71.6 4.4 %collective-permute-done.1 = bf16[2,256,128]{2,1,0:T(8,128)(2,1)S(1)} collective-permute-done((bf16[2,256,128]{2,1,0:T(8,128)(2,1)S(1)}, bf16[2,256,128]{2,1,0:T(8,128)(2,1)S(1)}, u32[]{:S(2)}, u32[]{:S(2)}) %collective-permute-start.1) | collective-permute-done | bytes 131104 | tf_op jit(solution)/shard_map/ppermute | solution.py:245
  76.0 5.3 %all-gather.4 = bf16[4,256,128]{2,1,0:T(8,128)(2,1)S(1)} all-gather(bf16[2,256,128]{2,1,0:T(8,128)(2,1)S(1)} %collective-permute-done.1), channel_id=6, replica_groups=mesh['pair'=64,'core'=2,'chan'=4] {'core'}, dimensions={0}, use_global_device_ids=true | all-gather | bytes 393216 | tf_op jit(solution)/shard_map/all_gather | solution.py:246
  81.3 1.2 shard_map.175
  82.5 8.8 %all_to_all.25.refs_0_ = bf16[4,256,128]{2,1,0:T(8,128)(2,1)S(1)} all-to-all(bf16[4,256,128]{2,1,0:T(8,128)(2,1)S(1)} %broadcast_in_dim.12), channel_id=1, replica_groups=mesh['pair'=64,'core'=2,'chan'=4] {'chan'}, dimensions={0} | all-to-all | bytes 524288 | tf_op jit(solution)/shard_map/all_to_all | solution.py:238
  92.1 2.8 %all-gather.5 = bf16[512,128]{1,0:T(8,128)(2,1)S(1)} all-gather(bf16[256,128]{1,0:T(8,128)(2,1)S(1)} %get-tuple-element.25), channel_id=7, replica_groups=mesh['pair'=64,'core'=2,'chan'=4] {'core'}, dimensions={0}, use_global_device_ids=true | all-gather | bytes 196608 | tf_op jit(solution)/shard_map/all_gather | solution.py:242
  94.8 1.9 %collective-permute-start.2 = (bf16[2,256,128]{2,1,0:T(8,128)(2,1)S(1)}, bf16[2,256,128]{2,1,0:T(8,128)(2,1)S(1)}, u32[]{:S(2)}, u32[]{:S(2)}) collective-permute-start(bf16[2,256,128]{2,1,0:T(8,128)(2,1)S(1)} %bitcast.29), channel_id=1, source_target_pairs={{0,508},{4,8},{8,4},{12,16},{16,12},{20,24},{24,20},{28,32},{32,28... | collective-permute-start | bytes 393224 | tf_op jit(solution)/shard_map/ppermute | solution.py:245
  96.7 4.4 %collective-permute-done.2 = bf16[2,256,128]{2,1,0:T(8,128)(2,1)S(1)} collective-permute-done((bf16[2,256,128]{2,1,0:T(8,128)(2,1)S(1)}, bf16[2,256,128]{2,1,0:T(8,128)(2,1)S(1)}, u32[]{:S(2)}, u32[]{:S(2)}) %collective-permute-start.2) | collective-permute-done | bytes 131104 | tf_op jit(solution)/shard_map/ppermute | solution.py:245
  101.1 5.3 %all-gather.6 = bf16[4,256,128]{2,1,0:T(8,128)(2,1)S(1)} all-gather(bf16[2,256,128]{2,1,0:T(8,128)(2,1)S(1)} %collective-permute-done.2), channel_id=8, replica_groups=mesh['pair'=64,'core'=2,'chan'=4] {'core'}, dimensions={0}, use_global_device_ids=true | all-gather | bytes 393216 | tf_op jit(solution)/shard_map/all_gather | solution.py:246
  106.4 1.2 shard_map.177
  107.6 8.8 %all_to_all.26.refs_0_ = bf16[4,256,128]{2,1,0:T(8,128)(2,1)S(1)} all-to-all(bf16[4,256,128]{2,1,0:T(8,128)(2,1)S(1)} %broadcast_in_dim.13), channel_id=1, replica_groups=mesh['pair'=64,'core'=2,'chan'=4] {'chan'}, dimensions={0} | all-to-all | bytes 524288 | tf_op jit(solution)/shard_map/all_to_all | solution.py:238
  117.1 2.9 %all-gather.7 = bf16[512,128]{1,0:T(8,128)(2,1)S(1)} all-gather(bf16[256,128]{1,0:T(8,128)(2,1)S(1)} %shard_map.178), channel_id=9, replica_groups=mesh['pair'=64,'core'=2,'chan'=4] {'core'}, dimensions={0}, use_global_device_ids=true | all-gather | bytes 196608 | tf_op jit(solution)/shard_map/all_gather | solution.py:242
  120.0 1.9 %collective-permute-start.3 = (bf16[2,256,128]{2,1,0:T(8,128)(2,1)S(1)}, bf16[2,256,128]{2,1,0:T(8,128)(2,1)S(1)}, u32[]{:S(2)}, u32[]{:S(2)}) collective-permute-start(bf16[2,256,128]{2,1,0:T(8,128)(2,1)S(1)} %bitcast.33), channel_id=1, source_target_pairs={{0,508},{4,8},{8,4},{12,16},{16,12},{20,24},{24,20},{28,32},{32,28... | collective-permute-start | bytes 393224 | tf_op jit(solution)/shard_map/ppermute | solution.py:245
  121.9 4.4 %collective-permute-done.3 = bf16[2,256,128]{2,1,0:T(8,128)(2,1)S(1)} collective-permute-done((bf16[2,256,128]{2,1,0:T(8,128)(2,1)S(1)}, bf16[2,256,128]{2,1,0:T(8,128)(2,1)S(1)}, u32[]{:S(2)}, u32[]{:S(2)}) %collective-permute-start.3) | collective-permute-done | bytes 131104 | tf_op jit(solution)/shard_map/ppermute | solution.py:245
  126.3 5.3 %all-gather.8 = bf16[4,256,128]{2,1,0:T(8,128)(2,1)S(1)} all-gather(bf16[2,256,128]{2,1,0:T(8,128)(2,1)S(1)} %collective-permute-done.3), channel_id=10, replica_groups=mesh['pair'=64,'core'=2,'chan'=4] {'core'}, dimensions={0}, use_global_device_ids=true | all-gather | bytes 393216 | tf_op jit(solution)/shard_map/all_gather | solution.py:246
  131.6 2.4 %shard_map.179 = bf16[512,128]{1,0:T(8,128)(2,1)S(1)} custom-call(bf16[2,256,128]{2,1,0:T(8,128)(2,1)S(1)} %bitcast.34, bf16[2,2,256,128]{3,2,1,0:T(8,128)(2,1)S(1)} %bitcast.28, bf16[512,128]{1,0:T(8,128)(2,1)S(1)} %get-tuple-element.28.recv, s32[5,512]{1,0:T(8,128)S(1)} %copy-done.7, s32[5,512]{1,0:T(8,128)S(1)} %copy-done.9, s32[2,4,8,128]{3,2,1,0:T(8,128)S(1)} %copy-done.17), custom_call_target="tpu_custom_call" | custom-call | tf_op jit(solution)/shard_map/pallas_call | solution.py:221
  134.1 11.6 %all_to_all.27.agg4 = bf16[4,512,128]{2,1,0:T(8,128)(2,1)S(1)} all-to-all(bf16[4,512,128]{2,1,0:T(8,128)(2,1)S(1)} %broadcast_in_dim.14), channel_id=1, replica_groups=mesh['pair'=64,'core'=2,'chan'=4] {'chan'}, dimensions={0} | all-to-all | bytes 1048576 | tf_op jit(solution)/shard_map/all_to_all | solution.py:238
  (67 shorter events, 9.5 us)
Async XLA Ops:
  6.5 11.6 %copy-start.22 = (bf16[512,227]{0,1:T(8,128)(2,1)S(1)}, bf16[512,227]{0,1:T(8,128)(2,1)}, u32[]{:S(2)}) copy-start(bf16[512,227]{0,1:T(8,128)(2,1)} %param.18) | copy-start | bytes 697348
  6.5 53.3 %all-gather.11.cloned.1.call-start = ((), (), s32[]{:S(2)}) async-start(), calls=%async_computation.5 | async-start | bytes 2293760 | tf_op jit(solution)/shard_map/all_gather | solution.py:262
  8.5 16.5 %copy-start.1 = (bf16[512,128]{1,0:T(8,128)(2,1)S(1)}, bf16[512,128]{1,0:T(8,128)(2,1)}, u32[]{:S(2)}) copy-start(bf16[512,128]{1,0:T(8,128)(2,1)} %w_es.1) | copy-start | bytes 393220
  8.5 16.5 %copy-start.2 = (bf16[512,128]{1,0:T(8,128)(2,1)S(1)}, bf16[512,128]{1,0:T(8,128)(2,1)}, u32[]{:S(2)}) copy-start(bf16[512,128]{1,0:T(8,128)(2,1)} %w_ed.1) | copy-start | bytes 393220
  8.6 16.5 %copy-start.3 = (bf16[512,128]{1,0:T(8,128)(2,1)S(1)}, bf16[512,128]{1,0:T(8,128)(2,1)}, u32[]{:S(2)}) copy-start(bf16[512,128]{1,0:T(8,128)(2,1)} %w_dd.1) | copy-start | bytes 393220
  8.6 16.5 %copy-start.5 = (s32[5,512]{1,0:T(8,128)S(1)}, s32[5,512]{1,0:T(8,128)}, u32[]{:S(2)}) copy-start(s32[5,512]{1,0:T(8,128)} %enc_src.3) | copy-start | bytes 30724
  8.6 16.5 %copy-start.6 = (s32[5,512]{1,0:T(8,128)S(1)}, s32[5,512]{1,0:T(8,128)}, u32[]{:S(2)}) copy-start(s32[5,512]{1,0:T(8,128)} %enc_dst.3) | copy-start | bytes 30724
  8.6 16.5 %copy-start.7 = (s32[5,512]{1,0:T(8,128)S(1)}, s32[5,512]{1,0:T(8,128)}, u32[]{:S(2)}) copy-start(s32[5,512]{1,0:T(8,128)} %dec_src.3) | copy-start | bytes 30724
  8.6 16.5 %copy-start.8 = (s32[5,512]{1,0:T(8,128)S(1)}, s32[5,512]{1,0:T(8,128)}, u32[]{:S(2)}) copy-start(s32[5,512]{1,0:T(8,128)} %dec_dst.3) | copy-start | bytes 30724
  8.6 16.5 %copy-start.12 = (s32[5,128]{1,0:T(8,128)S(1)}, s32[5,128]{1,0:T(8,128)}, u32[]{:S(2)}) copy-start(s32[5,128]{1,0:T(8,128)} %proc_src.5) | copy-start | bytes 7684
  8.6 16.5 %copy-start.14 = (s32[5,128]{1,0:T(8,128)S(1)}, s32[5,128]{1,0:T(8,128)}, u32[]{:S(2)}) copy-start(s32[5,128]{1,0:T(8,128)} %proc_dst.5) | copy-start | bytes 7684
  10.7 0.8 copy-start.21
  12.4 24.0 %copy-start.20 = (bf16[2,3,512,128]{3,2,1,0:T(8,128)(2,1)S(1)}, bf16[2,3,512,128]{3,2,1,0:T(8,128)(2,1)}, u32[]{:S(2)}) copy-start(bf16[2,3,512,128]{3,2,1,0:T(8,128)(2,1)} %param.24) | copy-start | bytes 2359300
  13.3 11.8 %all-to-all-start = ((bf16[4,512,128]{2,1,0:T(8,128)(2,1)}), bf16[4,512,128]{2,1,0:T(8,128)(2,1)S(1)}, u32[]{:S(2)}, u32[]{:S(2)}) async-start(bf16[4,512,128]{2,1,0:T(8,128)(2,1)} %broadcast_in_dim.10), calls=%async_computation | async-start | bytes 1048576 | tf_op jit(solution)/shard_map/all_to_all | solution.py:238
  34.5 9.0 %collective-permute-start = (bf16[2,672,128]{2,1,0:T(8,128)(2,1)S(1)}, bf16[2,672,128]{2,1,0:T(8,128)(2,1)S(1)}, u32[]{:S(2)}, u32[]{:S(2)}) collective-permute-start(bf16[2,672,128]{2,1,0:T(8,128)(2,1)S(1)} %bitcast.24), channel_id=1, source_target_pairs={{0,508},{4,8},{8,4},{12,16},{16,12},{20,24},{24,20},{28,32},{32,28... | collective-permute-start | bytes 1032200 | tf_op jit(solution)/shard_map/ppermute | solution.py:245
  54.4 0.6 copy-start.10
  55.0 0.6 copy-start.16
  56.4 9.5 %all-to-all-start.1 = ((bf16[4,256,128]{2,1,0:T(8,128)(2,1)}), bf16[4,256,128]{2,1,0:T(8,128)(2,1)S(1)}, u32[]{:S(2)}, u32[]{:S(2)}) async-start(bf16[4,256,128]{2,1,0:T(8,128)(2,1)} %broadcast_in_dim.11), calls=%async_computation.1 | async-start | bytes 524288 | tf_op jit(solution)/shard_map/all_to_all | solution.py:238
  65.9 15.4 %copy-start.11 = (s32[4,8,128]{2,1,0:T(8,128)S(1)}, s32[4,8,128]{2,1,0:T(8,128)}, u32[]{:S(2)}) copy-start(s32[4,8,128]{2,1,0:T(8,128)} %copy-done.10) | copy-start | bytes 49156
  65.9 15.4 %copy-start.13 = (s32[5,128]{1,0:T(8,128)S(1)}, s32[5,128]{1,0:T(8,128)}, u32[]{:S(2)}) copy-start(s32[5,128]{1,0:T(8,128)} %proc_src.5) | copy-start | bytes 7684
  65.9 15.4 %copy-start.15 = (s32[5,128]{1,0:T(8,128)S(1)}, s32[5,128]{1,0:T(8,128)}, u32[]{:S(2)}) copy-start(s32[5,128]{1,0:T(8,128)} %proc_dst.5) | copy-start | bytes 7684
  65.9 15.4 %copy-start.18 = (s32[1,1024]{1,0:T(1,128)S(1)}, s32[1,1024]{1,0:T(1,128)}, u32[]{:S(2)}) copy-start(s32[1,1024]{1,0:T(1,128)} %local_src.3) | copy-start | bytes 12292
  65.9 15.4 %copy-start.19 = (s32[1,1024]{1,0:T(1,128)S(1)}, s32[1,1024]{1,0:T(1,128)}, u32[]{:S(2)}) copy-start(s32[1,1024]{1,0:T(1,128)} %local_dst.3) | copy-start | bytes 12292
  69.7 6.3 %collective-permute-start.1 = (bf16[2,256,128]{2,1,0:T(8,128)(2,1)S(1)}, bf16[2,256,128]{2,1,0:T(8,128)(2,1)S(1)}, u32[]{:S(2)}, u32[]{:S(2)}) collective-permute-start(bf16[2,256,128]{2,1,0:T(8,128)(2,1)S(1)} %bitcast.31), channel_id=1, source_target_pairs={{0,508},{4,8},{8,4},{12,16},{16,12},{20,24},{24,20},{28,32},{32,28... | collective-permute-start | bytes 393224 | tf_op jit(solution)/shard_map/ppermute | solution.py:245
  91.3 25.1 %copy-start.4 = (bf16[512,128]{1,0:T(8,128)(2,1)S(1)}, bf16[512,128]{1,0:T(8,128)(2,1)}, u32[]{:S(2)}) copy-start(bf16[512,128]{1,0:T(8,128)(2,1)} %refs_3_.1) | copy-start | bytes 393220
  94.8 6.3 %collective-permute-start.2 = (bf16[2,256,128]{2,1,0:T(8,128)(2,1)S(1)}, bf16[2,256,128]{2,1,0:T(8,128)(2,1)S(1)}, u32[]{:S(2)}, u32[]{:S(2)}) collective-permute-start(bf16[2,256,128]{2,1,0:T(8,128)(2,1)S(1)} %bitcast.29), channel_id=1, source_target_pairs={{0,508},{4,8},{8,4},{12,16},{16,12},{20,24},{24,20},{28,32},{32,28... | collective-permute-start | bytes 393224 | tf_op jit(solution)/shard_map/ppermute | solution.py:245
  106.4 25.2 %copy-start.9 = (s32[5,512]{1,0:T(8,128)S(1)}, s32[5,512]{1,0:T(8,128)}, u32[]{:S(2)}) copy-start(s32[5,512]{1,0:T(8,128)} %dec_dst.3) | copy-start | bytes 30724
  106.4 25.2 %copy-start.17 = (s32[2,4,8,128]{3,2,1,0:T(8,128)S(1)}, s32[2,4,8,128]{3,2,1,0:T(8,128)}, u32[]{:S(2)}) copy-start(s32[2,4,8,128]{3,2,1,0:T(8,128)} %copy-done.16) | copy-start | bytes 98308
  117.1 28.6 %copy-start = (bf16[7168,128]{1,0:T(8,128)(2,1)S(1)}, bf16[7168,128]{1,0:T(8,128)(2,1)}, u32[]{:S(2)}) copy-start(bf16[7168,128]{1,0:T(8,128)(2,1)} %all-gather.11.cloned.1.call-done) | copy-start | bytes 5505028
  120.0 6.3 %collective-permute-start.3 = (bf16[2,256,128]{2,1,0:T(8,128)(2,1)S(1)}, bf16[2,256,128]{2,1,0:T(8,128)(2,1)S(1)}, u32[]{:S(2)}, u32[]{:S(2)}) collective-permute-start(bf16[2,256,128]{2,1,0:T(8,128)(2,1)S(1)} %bitcast.33), channel_id=1, source_target_pairs={{0,508},{4,8},{8,4},{12,16},{16,12},{20,24},{24,20},{28,32},{32,28... | collective-permute-start | bytes 393224 | tf_op jit(solution)/shard_map/ppermute | solution.py:245
Sparse Core Ops, SparseCore 0:
  11.6 39.4 all-gather.10

commit v2 on v1

--- a/solution.py
+++ b/solution.py
@@ -1,9 +1,11 @@
+import functools
+
 import jax
 import jax.numpy as jnp
 from jax import lax
 from jax.experimental import pallas as pl
 from jax.experimental.pallas import tpu as pltpu
-from jax.sharding import Mesh, PartitionSpec as P
+from jax.sharding import PartitionSpec as P
 
 EPS = 1e-05
 F32 = jnp.float32
@@ -37,6 +39,10 @@
 
 def wide(ref, start, size):
     return jnp.concatenate([ref[c, start : start + size, :] for c in range(ref.shape[0])], axis=1)
+
+
+def core_index():
+    return lax.axis_index("band") & 1
 
 
 def one_hot(row, count):
@@ -75,10 +81,9 @@
     grid_state, big, w_es, w_ed, w_dd, enc_src, enc_dst, dec_src, dec_dst, proc_src, proc_dst,
     payload, enc_recv, dec_recv, latent, digits,
 ):
-    core = lax.axis_index("core")
-    channels = grid_state.shape[1]
-    nodes = grid_state.shape[0]
-    grid_latent = silu(dot(grid_state[...], wide(big, 0, channels))).astype(BF16)
+    core = core_index()
+    channels, nodes = grid_state.shape
+    grid_latent = silu(dot_first(grid_state[...], wide(big, 0, channels))).astype(BF16)
     latent[...] = grid_latent
     grid_normed = rms(grid_latent).astype(BF16)
     payload[0:nodes, :] = dot(grid_normed, w_es[...]).astype(BF16)
@@ -120,10 +125,10 @@
 
 
 def enc_kernel(
-    pair, two, recv, enc_src, enc_dst,
+    pair, two, far, recv, enc_src, enc_dst,
     agg, proc_tab, dec_tab,
 ):
-    core = lax.axis_index("core")
+    core = core_index()
     sib = 1 - core
     recv_count = recv.shape[0]
     send_count = pair.shape[1] - TABLES * TILE
@@ -138,7 +143,7 @@
         elif kind == "pair":
             block = pair.at[sib]
         else:
-            block = two.at[sib, core]
+            block = far.at[sib]
         lists = [
             decode(block[send_count + t * TILE : send_count + (t + 1) * TILE, :], offset, second)
             for t in range(TABLES)
@@ -150,10 +155,49 @@
         dec_tab[0, v] = lists[2]
         dec_tab[1, v] = lists[3]
         proc_tab[v] = lists[4]
-    agg[...] = total.T.astype(BF16)
-
-
-def node_kernel(has_recv, agg4, state, weights, w_send, *rest):
+    agg[...] = jnp.broadcast_to(total.T.astype(BF16)[None], agg.shape)
+
+
+def rows_of(late, start, size):
+    half = late.shape[2]
+    parts = []
+    while size > 0:
+        k, low = start // half, start % half
+        take = min(size, half - low)
+        parts.append(
+            jnp.concatenate([late[k, c, low : low + take, :] for c in range(late.shape[1])], axis=1)
+        )
+        start, size = start + take, size - take
+    return parts[0] if len(parts) == 1 else jnp.concatenate(parts, axis=0)
+
+
+def early_kernel(w_in, mesh_latent, out):
+    channels = w_in.shape[0]
+    start = out.shape[1] - mesh_latent.shape[0]
+    for c in range(out.shape[0]):
+        out[c, 0:channels, :] = w_in[...]
+        out[c, start:, :] = mesh_latent[...]
+
+
+def late_kernel(w_enc_out, w_proc, w_out, out):
+    core = core_index()
+    half = out.shape[1]
+    depth = w_enc_out.shape[0]
+    for k in range(2):
+
+        @pl.when(core == k)
+        def _():
+            for i in range(4):
+                block = (w_enc_out, w_proc.at[0, 2], w_proc.at[1, 2], w_out)[i]
+                low = max(i * depth, k * half)
+                high = min(i * depth + block.shape[0], (k + 1) * half)
+                if low < high:
+                    rows = block[low - i * depth : high - i * depth, :]
+                    for c in range(out.shape[0]):
+                        out[c, low - k * half : high - k * half, :] = rows
+
+
+def node_kernel(index, has_recv, agg4, state, weights, w_send, *rest):
     if has_recv:
         w_recv, new_state, send, recv = rest
     else:
@@ -164,7 +208,7 @@
         before = wide(state, state.shape[1] - count, count).astype(F32)
     else:
         before = state[...]
-    after = before + dot(rms(agg).astype(BF16), wide(weights, 0, weights.shape[1]))
+    after = before + dot(rms(agg).astype(BF16), rows_of(weights, index * agg.shape[1], agg.shape[1]))
     normed = rms(after.astype(BF16)).astype(BF16)
     send[...] = dot(normed, w_send[...]).astype(BF16)
     if has_recv:
@@ -172,24 +216,24 @@
         recv[...] = dot(normed, w_recv[...]).astype(BF16)
 
 
-def proc_kernel(pair, two, recv, local_src, local_dst, proc_src, proc_dst, tab, agg):
-    core = lax.axis_index("core")
+def proc_kernel(pair, two, far, recv, local_src, local_dst, proc_src, proc_dst, tab, agg):
+    core = core_index()
     sib = 1 - core
     count = recv.shape[0]
     recv_t = transposed(recv[...])
     own_src = jnp.concatenate([local_src[...], proc_src[2:3, :]], axis=1)
     own_dst = jnp.concatenate([local_dst[...], proc_dst[2:3, :]], axis=1)
     total = add_edges(None, transposed(pair[core]), recv_t, own_src, own_dst, count, count)
-    for v, block in enumerate((two.at[core, 0], two.at[core, 1], pair.at[sib], two.at[sib, core])):
+    for v, block in enumerate((two.at[core, 0], two.at[core, 1], pair.at[sib], far.at[sib])):
         lists = tab[v]
         total = add_edges(
             total, transposed(block[...]), recv_t, lists[0:1, :], lists[1:2, :], count, count
         )
-    agg[...] = total.T.astype(BF16)
-
-
-def dec_kernel(pair, two, recv, dec_src, dec_dst, tab, agg):
-    core = lax.axis_index("core")
+    agg[...] = jnp.broadcast_to(total.T.astype(BF16)[None], agg.shape)
+
+
+def dec_kernel(pair, two, far, recv, dec_src, dec_dst, tab, agg):
+    core = core_index()
     sib = 1 - core
     recv_count = recv.shape[0]
     send_count = pair.shape[1]
@@ -197,24 +241,18 @@
     total = add_edges(
         None, transposed(pair[core]), recv_t, dec_src[2:3, :], dec_dst[2:3, :], send_count, recv_count
     )
-    for v, block in enumerate((two.at[core, 0], two.at[core, 1], pair.at[sib], two.at[sib, core])):
+    for v, block in enumerate((two.at[core, 0], two.at[core, 1], pair.at[sib], far.at[sib])):
         total = add_edges(
             total, transposed(block[...]), recv_t, flat(tab[0, v], 0, 4), flat(tab[1, v], 0, 4),
             send_count, recv_count,
         )
-    agg[...] = total.T.astype(BF16)
+    agg[...] = jnp.broadcast_to(total.T.astype(BF16)[None], agg.shape)
 
 
 def out_kernel(agg4, latent, weights, out):
     combined = wide(agg4, 0, agg4.shape[1]).astype(F32) + latent[...].astype(F32)
     normed = rms(combined).astype(BF16)
-    rows = weights.shape[1]
-    parts = weights.shape[0]
-    low = jnp.concatenate([weights[c, rows - 256 : rows - 128, :] for c in range(parts)], axis=0)
-    high = jnp.concatenate([weights[c, rows - 128 : rows, :] for c in range(parts)], axis=0)
-    columns = out.shape[1]
-    out[:, 0:LANES] = dot(normed, low).astype(BF16)
-    out[:, LANES:columns] = dot(normed, high)[:, 0 : columns - LANES].astype(BF16)
+    out[...] = dot_last(rows_of(weights, 3 * normed.shape[1], out.shape[0]), normed).astype(BF16)
 
 
 def call(kernel, out_shapes, *args, scratch=()):
@@ -232,18 +270,22 @@
     return jax.ShapeDtypeStruct(dims, kind)
 
 
-def chan_gather(block):
-    count = lax.axis_size("chan")
-    copies = jnp.broadcast_to(block[None], (count,) + block.shape)
+def exchange(copies):
     return lax.all_to_all(copies, "chan", 0, 0, tiled=True)
 
 
+def core_gather(block):
+    parts = lax.axis_size("band")
+    return lax.all_gather(block, "band", axis_index_groups=[[s, s + 1] for s in range(0, parts, 2)])
+
+
 def around(block):
-    pair = lax.all_gather(block, "core")
-    parts = lax.axis_size(("pair", "core"))
-    swap = [(s, (s + 1) % parts if s % 2 else (s - 1) % parts) for s in range(parts)]
-    got = lax.ppermute(pair, ("pair", "core"), swap)
-    return pair, lax.all_gather(got, "core")
+    parts = lax.axis_size("band")
+    pair = core_gather(block)
+    sides = [[s, (s + 1) % parts] for s in range(1, parts, 2)]
+    two = lax.all_gather(pair, "band", axis_index_groups=sides)
+    near = jnp.where(core_index() == 0, two[0, 1], two[1, 0])
+    return pair, two, core_gather(near)
 
 
 def on_device(
@@ -255,15 +297,14 @@
     chans = lax.axis_size("chan")
     latent_width = width * chans
 
-    w_out_pad = jnp.pad(w_out, ((0, 0), (0, 2 * LANES - channels)))
-    late = jnp.concatenate(
-        [w_enc_out, w_proc[0, 2], w_proc[1, 2], w_out_pad[:, :LANES], w_out_pad[:, LANES:]], axis=0
-    )
-    late = lax.all_gather(late, "chan")
-    updates = [late[:, i * latent_width : (i + 1) * latent_width] for i in range(3)]
-
-    early = jnp.concatenate([jnp.pad(w_in, ((0, 2 * LANES - channels), (0, 0))), mesh_latent], axis=0)
-    big = chan_gather(early)
+    channel_rows = -(-channels // LANES) * LANES
+    late_rows = 3 * latent_width + channel_rows
+    big = exchange(call(
+        early_kernel, shape((chans, channel_rows + mesh_count, width)), w_in, mesh_latent
+    ))
+    late = core_gather(exchange(call(
+        late_kernel, shape((chans, late_rows // 2, width)), w_enc_out, w_proc, w_out.T
+    )))
 
     payload, recv, dec_recv, grid_latent = call(
         pre_kernel,
@@ -273,46 +314,43 @@
             shape((grid_count, width)),
             shape((grid_count, latent_width)),
         ),
-        grid_state, big, w_enc_src, w_enc_dst, w_dec_dst,
+        grid_state.T, big, w_enc_src, w_enc_dst, w_dec_dst,
         enc_src, enc_dst, dec_src, dec_dst, proc_src, proc_dst,
         scratch=[pltpu.VMEM((16, enc_src.shape[1]), F32)],
     )
-    pair, two = around(payload)
+    pair, two, far = around(payload)
     agg, proc_tab, dec_tab = call(
         enc_kernel,
-        (shape((mesh_count, width)), shape((4, 8, LANES), I32), shape((2, 4, 8, LANES), I32)),
-        pair, two, recv, enc_src, enc_dst,
+        (shape((chans, mesh_count, width)), shape((4, 8, LANES), I32), shape((2, 4, 8, LANES), I32)),
+        pair, two, far, recv, enc_src, enc_dst,
     )
     state = big
     for layer in range(w_proc.shape[0]):
         state, send, recv = call(
-            lambda *refs: node_kernel(True, *refs),
+            functools.partial(node_kernel, layer, True),
             (shape((mesh_count, latent_width), F32), shape((mesh_count, width)), shape((mesh_count, width))),
-            chan_gather(agg), state, updates[layer], w_proc[layer, 0], w_proc[layer, 1],
-        )
-        pair, two = around(send)
+            exchange(agg), state, late, w_proc[layer, 0], w_proc[layer, 1],
+        )
+        pair, two, far = around(send)
         agg = call(
-            proc_kernel, shape((mesh_count, width)),
-            pair, two, recv, local_src, local_dst, proc_src, proc_dst, proc_tab,
+            proc_kernel, shape((chans, mesh_count, width)),
+            pair, two, far, recv, local_src, local_dst, proc_src, proc_dst, proc_tab,
         )
     send = call(
-        lambda *refs: node_kernel(False, *refs[:4], refs[4]), shape((mesh_count, width)),
-        chan_gather(agg), state, updates[2], w_dec_src,
-    )
-    pair, two = around(send)
+        functools.partial(node_kernel, w_proc.shape[0], False), shape((mesh_count, width)),
+        exchange(agg), state, late, w_dec_src,
+    )
+    pair, two, far = around(send)
     agg = call(
-        dec_kernel, shape((grid_count, width)), pair, two, dec_recv, dec_src, dec_dst, dec_tab
-    )
-    return call(out_kernel, shape((grid_count, channels)), chan_gather(agg), grid_latent, late)
+        dec_kernel, shape((chans, grid_count, width)), pair, two, far, dec_recv, dec_src, dec_dst, dec_tab
+    )
+    return call(out_kernel, shape((channels, grid_count)), exchange(agg), grid_latent, late).T
 
 
 def solution(mesh):
-    bands, chans = mesh.devices.shape
-    split = Mesh(mesh.devices.reshape(bands // 2, 2, chans), ("pair", "core", "chan"))
-    band = ("pair", "core")
     placed = (
-        P(band, None),
-        P(band, "chan"),
+        P("band", None),
+        P("band", "chan"),
         P(None, "chan"),
         P(None, "chan"),
         P(None, "chan"),
@@ -321,7 +359,7 @@
         P(None, "chan"),
         P(None, "chan"),
         P("chan", None),
-    ) + (P(band, None),) * 8
+    ) + (P("band", None),) * 8
     return jax.shard_map(
-        on_device, mesh=split, in_specs=placed, out_specs=P(band, None), check_vma=False
-    )
+        on_device, mesh=mesh, in_specs=placed, out_specs=P("band", None), check_vma=False
+    )

time: 155 us -> 163 us (1.052)
  blocking collectives: 70.9 us -> 111 us
  waiting for transfers between devices: 31.5 us -> 12.9 us
  starting transfers between devices: 15.9 us -> 6.88 us
  local copies, waits for them, and re-layouts: 10.3 us -> 4.49 us
  Pallas kernels: 10.8 us -> 13.2 us
    all_gather x8 -> x12, blocking collectives: 41.6 us -> 68 us  [the longest x8 45.4 us: core_gather(): lax.all_gather(block, 'band', axis_index_groups=[[s, s + 1] for s in rang...]
    ppermute x4 -> x0, waiting for transfers between devices: 20.1 us -> none  [around(): got = lax.ppermute(pair, ('pair', 'core'), swap)]
    all_to_all x3 -> x4, blocking collectives: 29.3 us -> 43.2 us  [exchange(): return lax.all_to_all(copies, 'chan', 0, 0, tiled=True)]
    ppermute x4 -> x0, starting transfers between devices: 7.63 us -> none  [around(): got = lax.ppermute(pair, ('pair', 'core'), swap)]
    slice x4 -> x0, local copies, waits for them, and re-layouts: 2.52 us -> none  [the longest x1 1.47 us: on_device(): late[:, i * latent_width:(i + 1) * latent_width]]
    pallas_call x9 -> x11, Pallas kernels: 10.8 us -> 13.2 us  [call(): pl.pallas_call(kernel, out_shape=out_shapes, in_specs=[pl.BlockSpec(memor...]
    broadcast_in_dim x5 -> x0, local copies, waits for them, and re-layouts: 1.74 us -> none  [chan_gather(): copies = jnp.broadcast_to(block[None], (count,) + block.shape)]
    unnamed x51 -> x42, local copies, waits for them, and re-layouts: 5.16 us -> 4.46 us
  transfers between devices with their start and end apart: 7 -> 3, of which waited for: 6 -> 2; matrix products, arithmetic and copies ran while one was open for 3% -> 0% of each run, Pallas kernels for 2% -> 3%
where the time goes in v2:
time: 163 us; the launch traced here: 162 us
  blocking collectives  111 us (68%)
  between operations  13.7 us (8%)
  Pallas kernels  13.2 us (8%)
  waiting for transfers between devices  12.9 us (8%)
  starting transfers between devices  6.88 us (4%)
  local copies, waits for them, and re-layouts  4.49 us (3%)
    all_gather x8, blocking collectives, core_gather(): lax.all_gather(block, 'band', axis_index_groups=[[s, s + 1] for s in rang...  45.4 us
    all_to_all x4, blocking collectives, exchange(): return lax.all_to_all(copies, 'chan', 0, 0, tiled=True)  43.2 us
    all_gather x4, blocking collectives, around(): two = lax.all_gather(pair, 'band', axis_index_groups=sides)  22.6 us
    pallas_call x11, Pallas kernels, call(): pl.pallas_call(kernel, out_shape=out_shapes, in_specs=[pl.BlockSpec(memor...  13.2 us
    all_to_all x2, waiting for transfers between devices, exchange(): return lax.all_to_all(copies, 'chan', 0, 0, tiled=True)  12.9 us
    all_to_all x2, starting transfers between devices, exchange(): return lax.all_to_all(copies, 'chan', 0, 0, tiled=True)  6.87 us
    unnamed x42, local copies, waits for them, and re-layouts  4.46 us
  transfers between devices with their start and end apart: 3, of which 2 were waited for; matrix products, arithmetic and copies ran while one was open for 0% of the time, Pallas kernels for 3%

profile of v2, /device:TPU:1, one launch (start us, length us, event | category | flops | bytes accessed | tf_op | source)
XLA Modules:
  0.0 162.5 jit_solution(18291854288052780492)
XLA Ops:
  6.5 1.1 copy-done.2
  7.7 0.9 copy-done.5
  8.6 0.8 copy-done.15
  9.7 13.9 %all_to_all.30 = bf16[4,896,128]{2,1,0:T(8,128)(2,1)} all-to-all(bf16[4,896,128]{2,1,0:T(8,128)(2,1)S(1)} %shard_map.175), channel_id=1, replica_groups=mesh['band'=128,'chan'=4] {'chan'}, dimensions={0} | all-to-all | bytes 1835008 | tf_op jit(solution)/shard_map/all_to_all | solution.py:274
  23.6 0.9 shard_map.172
  24.5 3.5 %all-to-all-start = ((bf16[4,512,128]{2,1,0:T(8,128)(2,1)}), bf16[4,512,128]{2,1,0:T(8,128)(2,1)S(1)}, u32[]{:S(2)}, u32[]{:S(2)}) async-start(bf16[4,512,128]{2,1,0:T(8,128)(2,1)} %shard_map.172), calls=%async_computation | async-start | bytes 1048576 | tf_op jit(solution)/shard_map/all_to_all | solution.py:274
  28.0 6.9 %all-to-all-done.big.state = bf16[4,512,128]{2,1,0:T(8,128)(2,1)S(1)} async-done(((bf16[4,512,128]{2,1,0:T(8,128)(2,1)}), bf16[4,512,128]{2,1,0:T(8,128)(2,1)S(1)}, u32[]{:S(2)}, u32[]{:S(2)}) %all-to-all-start) | async-done | bytes 524320 | tf_op jit(solution)/shard_map/all_to_all | solution.py:274
  35.0 1.1 shard_map.173
  36.0 9.3 %all-gather = bf16[1344,128]{1,0:T(8,128)(2,1)S(1)} all-gather(bf16[672,128]{1,0:T(8,128)(2,1)S(1)} %get-tuple-element.18), channel_id=2, replica_groups={{0,4},{8,12},{16,20},{24,28},{32,36},{40,44},{48,52},{56,60},{64,68},{7..., dimensions={0}, use_global_device_ids=true | all-gather | bytes 516096 | tf_op jit(solution)/shard_map/all_gather | solution.py:279
  45.3 7.5 %all-gather.1 = bf16[4,672,128]{2,1,0:T(8,128)(2,1)S(1)} all-gather(bf16[2,672,128]{2,1,0:T(8,128)(2,1)S(1)} %bitcast.30), channel_id=3, replica_groups={{4,8},{12,16},{20,24},{28,32},{36,40},{44,48},{52,56},{60,64},{68,72},{..., dimensions={0}, use_global_device_ids=true | all-gather | bytes 1032192 | tf_op jit(solution)/shard_map/all_gather | solution.py:286
  52.8 11.7 %all-gather.2 = bf16[2,1,672,128]{3,2,1,0:T(8,128)(2,1)S(1)} all-gather(bf16[1,1,672,128]{3,2,1,0:T(8,128)(2,1)S(1)} %slice_select_fusion), channel_id=4, replica_groups={{0,4},{8,12},{16,20},{24,28},{32,36},{40,44},{48,52},{56,60},{64,68},{7..., dimensions={0}, use_global_device_ids=true | all-gather | bytes 516096 | tf_op jit(solution)/shard_map/all_gather | solution.py:279
  64.5 3.0 %shard_map.174 = (bf16[4,256,128]{2,1,0:T(8,128)(2,1)}, s32[4,8,128]{2,1,0:T(8,128)S(1)}, s32[2,4,8,128]{3,2,1,0:T(8,128)S(1)}) custom-call(bf16[2,672,128]{2,1,0:T(8,128)(2,1)S(1)} %bitcast.31, bf16[2,2,672,128]{3,2,1,0:T(8,128)(2,1)S(1)} %bitcast.29, bf16[2,672,128]{2,1,0:T(8,128)(2,1)S(1)} %bitcast.38, bf16[256,128]{1,0:T(8,128)(2,1)S(1)} %get-tuple-element.19.recv, ...), custom_call_target="tpu_custom_call" | custom-call | tf_op jit(solution)/shard_map/pallas_call | solution.py:259
  67.4 3.4 %all-to-all-start.1 = ((bf16[4,256,128]{2,1,0:T(8,128)(2,1)}), bf16[4,256,128]{2,1,0:T(8,128)(2,1)S(1)}, u32[]{:S(2)}, u32[]{:S(2)}) async-start(bf16[4,256,128]{2,1,0:T(8,128)(2,1)} %get-tuple-element.20), calls=%async_computation.1 | async-start | bytes 524288 | tf_op jit(solution)/shard_map/all_to_all | solution.py:274
  70.9 6.0 %all-to-all-done.1.agg4 = bf16[4,256,128]{2,1,0:T(8,128)(2,1)S(1)} async-done(((bf16[4,256,128]{2,1,0:T(8,128)(2,1)}), bf16[4,256,128]{2,1,0:T(8,128)(2,1)S(1)}, u32[]{:S(2)}, u32[]{:S(2)}) %all-to-all-start.1) | async-done | bytes 262176 | tf_op jit(solution)/shard_map/all_to_all | solution.py:274
  76.9 1.5 copy-done
  78.4 0.8 shard_map.176
  79.2 3.2 %all-gather.4 = bf16[512,128]{1,0:T(8,128)(2,1)S(1)} all-gather(bf16[256,128]{1,0:T(8,128)(2,1)S(1)} %get-tuple-element.21), channel_id=6, replica_groups={{0,4},{8,12},{16,20},{24,28},{32,36},{40,44},{48,52},{56,60},{64,68},{7..., dimensions={0}, use_global_device_ids=true | all-gather | bytes 196608 | tf_op jit(solution)/shard_map/all_gather | solution.py:279
  82.4 5.1 %all-gather.5 = bf16[4,256,128]{2,1,0:T(8,128)(2,1)S(1)} all-gather(bf16[2,256,128]{2,1,0:T(8,128)(2,1)S(1)} %bitcast.43), channel_id=7, replica_groups={{4,8},{12,16},{20,24},{28,32},{36,40},{44,48},{52,56},{60,64},{68,72},{..., dimensions={0}, use_global_device_ids=true | all-gather | bytes 393216 | tf_op jit(solution)/shard_map/all_gather | solution.py:286
  87.5 5.2 %all-gather.6 = bf16[2,1,256,128]{3,2,1,0:T(8,128)(2,1)S(1)} all-gather(bf16[1,1,256,128]{3,2,1,0:T(8,128)(2,1)S(1)} %slice_select_fusion.3), channel_id=8, replica_groups={{0,4},{8,12},{16,20},{24,28},{32,36},{40,44},{48,52},{56,60},{64,68},{7..., dimensions={0}, use_global_device_ids=true | all-gather | bytes 196608 | tf_op jit(solution)/shard_map/all_gather | solution.py:279
  92.7 1.2 shard_map.177
  93.9 8.8 %all_to_all.31.agg4 = bf16[4,256,128]{2,1,0:T(8,128)(2,1)S(1)} all-to-all(bf16[4,256,128]{2,1,0:T(8,128)(2,1)S(1)} %shard_map.177), channel_id=1, replica_groups=mesh['band'=128,'chan'=4] {'chan'}, dimensions={0} | all-to-all | bytes 524288 | tf_op jit(solution)/shard_map/all_to_all | solution.py:274
  103.5 2.9 %all-gather.7 = bf16[512,128]{1,0:T(8,128)(2,1)S(1)} all-gather(bf16[256,128]{1,0:T(8,128)(2,1)S(1)} %get-tuple-element.25), channel_id=9, replica_groups={{0,4},{8,12},{16,20},{24,28},{32,36},{40,44},{48,52},{56,60},{64,68},{7..., dimensions={0}, use_global_device_ids=true | all-gather | bytes 196608 | tf_op jit(solution)/shard_map/all_gather | solution.py:279
  106.3 5.1 %all-gather.8 = bf16[4,256,128]{2,1,0:T(8,128)(2,1)S(1)} all-gather(bf16[2,256,128]{2,1,0:T(8,128)(2,1)S(1)} %bitcast.41), channel_id=10, replica_groups={{4,8},{12,16},{20,24},{28,32},{36,40},{44,48},{52,56},{60,64},{68,72},{..., dimensions={0}, use_global_device_ids=true | all-gather | bytes 393216 | tf_op jit(solution)/shard_map/all_gather | solution.py:286
  111.4 5.2 %all-gather.9 = bf16[2,1,256,128]{3,2,1,0:T(8,128)(2,1)S(1)} all-gather(bf16[1,1,256,128]{3,2,1,0:T(8,128)(2,1)S(1)} %slice_select_fusion.2), channel_id=11, replica_groups={{0,4},{8,12},{16,20},{24,28},{32,36},{40,44},{48,52},{56,60},{64,68},{7..., dimensions={0}, use_global_device_ids=true | all-gather | bytes 196608 | tf_op jit(solution)/shard_map/all_gather | solution.py:279
  116.6 1.2 shard_map.179
  117.8 8.8 %all_to_all.32.agg4 = bf16[4,256,128]{2,1,0:T(8,128)(2,1)S(1)} all-to-all(bf16[4,256,128]{2,1,0:T(8,128)(2,1)S(1)} %shard_map.179), channel_id=1, replica_groups=mesh['band'=128,'chan'=4] {'chan'}, dimensions={0} | all-to-all | bytes 524288 | tf_op jit(solution)/shard_map/all_to_all | solution.py:274
  127.3 2.7 %all-gather.10 = bf16[512,128]{1,0:T(8,128)(2,1)S(1)} all-gather(bf16[256,128]{1,0:T(8,128)(2,1)S(1)} %shard_map.180), channel_id=12, replica_groups={{0,4},{8,12},{16,20},{24,28},{32,36},{40,44},{48,52},{56,60},{64,68},{7..., dimensions={0}, use_global_device_ids=true | all-gather | bytes 196608 | tf_op jit(solution)/shard_map/all_gather | solution.py:279
  130.0 5.1 %all-gather.11 = bf16[4,256,128]{2,1,0:T(8,128)(2,1)S(1)} all-gather(bf16[2,256,128]{2,1,0:T(8,128)(2,1)S(1)} %bitcast.39), channel_id=13, replica_groups={{4,8},{12,16},{20,24},{28,32},{36,40},{44,48},{52,56},{60,64},{68,72},{..., dimensions={0}, use_global_device_ids=true | all-gather | bytes 393216 | tf_op jit(solution)/shard_map/all_gather | solution.py:286
  135.1 5.2 %all-gather.12 = bf16[2,1,256,128]{3,2,1,0:T(8,128)(2,1)S(1)} all-gather(bf16[1,1,256,128]{3,2,1,0:T(8,128)(2,1)S(1)} %slice_select_fusion.1), channel_id=14, replica_groups={{0,4},{8,12},{16,20},{24,28},{32,36},{40,44},{48,52},{56,60},{64,68},{7..., dimensions={0}, use_global_device_ids=true | all-gather | bytes 196608 | tf_op jit(solution)/shard_map/all_gather | solution.py:279
  140.3 2.4 %shard_map.181 = bf16[4,512,128]{2,1,0:T(8,128)(2,1)S(1)} custom-call(bf16[2,256,128]{2,1,0:T(8,128)(2,1)S(1)} %bitcast.40, bf16[2,2,256,128]{3,2,1,0:T(8,128)(2,1)S(1)} %bitcast.33, bf16[2,256,128]{2,1,0:T(8,128)(2,1)S(1)} %bitcast.45, bf16[512,128]{1,0:T(8,128)(2,1)S(1)} %get-tuple-element.28.recv, s32[5,512]{1,0:T(8,128)S(1)} %copy-done.12, ...), custom_call_target="tpu_custom_call" | custom-call | tf_op jit(solution)/shard_map/pallas_call | solution.py:259
  142.8 11.6 %all_to_all.33.agg4 = bf16[4,512,128]{2,1,0:T(8,128)(2,1)S(1)} all-to-all(bf16[4,512,128]{2,1,0:T(8,128)(2,1)S(1)} %shard_map.181), channel_id=1, replica_groups=mesh['band'=128,'chan'=4] {'chan'}, dimensions={0} | all-to-all | bytes 1048576 | tf_op jit(solution)/shard_map/all_to_all | solution.py:274
  154.4 1.2 shard_map.182
  (49 shorter events, 1.8 us)
Async XLA Ops:
  6.5 70.4 %all-gather.15.cloned.1.call-start = ((), (), s32[]{:S(2)}) async-start(), calls=%async_computation.6 | async-start | bytes 2752512 | tf_op jit(solution)/shard_map/all_gather | solution.py:279
  6.5 1.1 copy-start.2
  7.7 0.9 copy-start.5
  8.6 0.8 copy-start.15
  9.5 14.1 %copy-start.14 = (bf16[256,128]{1,0:T(8,128)(2,1)S(1)}, bf16[256,128]{1,0:T(8,128)(2,1)}, u32[]{:S(2)}) copy-start(bf16[256,128]{1,0:T(8,128)(2,1)} %mesh_latent.1) | copy-start | bytes 196612
  9.5 14.1 %copy-start.16 = (bf16[227,128]{1,0:T(8,128)(2,1)S(1)}, bf16[227,128]{1,0:T(8,128)(2,1)}, u32[]{:S(2)}) copy-start(bf16[227,128]{1,0:T(8,128)(2,1)} %w_in.1) | copy-start | bytes 174340
  9.5 25.3 %copy-start.4 = (bf16[512,227]{0,1:T(8,128)(2,1)S(1)}, bf16[512,227]{0,1:T(8,128)(2,1)}, u32[]{:S(2)}) copy-start(bf16[512,227]{0,1:T(8,128)(2,1)} %param.18) | copy-start | bytes 697348
  9.6 25.3 %copy-start.6 = (bf16[512,128]{1,0:T(8,128)(2,1)S(1)}, bf16[512,128]{1,0:T(8,128)(2,1)}, u32[]{:S(2)}) copy-start(bf16[512,128]{1,0:T(8,128)(2,1)} %w_es.1) | copy-start | bytes 393220
  9.6 25.3 %copy-start.7 = (bf16[512,128]{1,0:T(8,128)(2,1)S(1)}, bf16[512,128]{1,0:T(8,128)(2,1)}, u32[]{:S(2)}) copy-start(bf16[512,128]{1,0:T(8,128)(2,1)} %w_ed.1) | copy-start | bytes 393220
  9.6 25.3 %copy-start.8 = (bf16[512,128]{1,0:T(8,128)(2,1)S(1)}, bf16[512,128]{1,0:T(8,128)(2,1)}, u32[]{:S(2)}) copy-start(bf16[512,128]{1,0:T(8,128)(2,1)} %w_dd.1) | copy-start | bytes 393220
  9.6 25.3 %copy-start.10 = (s32[5,512]{1,0:T(8,128)S(1)}, s32[5,512]{1,0:T(8,128)}, u32[]{:S(2)}) copy-start(s32[5,512]{1,0:T(8,128)} %enc_src.3) | copy-start | bytes 30724
  9.6 25.3 %copy-start.11 = (s32[5,512]{1,0:T(8,128)S(1)}, s32[5,512]{1,0:T(8,128)}, u32[]{:S(2)}) copy-start(s32[5,512]{1,0:T(8,128)} %enc_dst.3) | copy-start | bytes 30724
  9.6 25.3 %copy-start.12 = (s32[5,512]{1,0:T(8,128)S(1)}, s32[5,512]{1,0:T(8,128)}, u32[]{:S(2)}) copy-start(s32[5,512]{1,0:T(8,128)} %dec_src.3) | copy-start | bytes 30724
  9.6 25.3 %copy-start.13 = (s32[5,512]{1,0:T(8,128)S(1)}, s32[5,512]{1,0:T(8,128)}, u32[]{:S(2)}) copy-start(s32[5,512]{1,0:T(8,128)} %dec_dst.3) | copy-start | bytes 30724
  9.6 25.3 %copy-start.17 = (s32[5,128]{1,0:T(8,128)S(1)}, s32[5,128]{1,0:T(8,128)}, u32[]{:S(2)}) copy-start(s32[5,128]{1,0:T(8,128)} %proc_src.5) | copy-start | bytes 7684
  9.7 25.3 %copy-start.18 = (s32[5,128]{1,0:T(8,128)S(1)}, s32[5,128]{1,0:T(8,128)}, u32[]{:S(2)}) copy-start(s32[5,128]{1,0:T(8,128)} %proc_dst.5) | copy-start | bytes 7684
  24.5 10.4 %all-to-all-start = ((bf16[4,512,128]{2,1,0:T(8,128)(2,1)}), bf16[4,512,128]{2,1,0:T(8,128)(2,1)S(1)}, u32[]{:S(2)}, u32[]{:S(2)}) async-start(bf16[4,512,128]{2,1,0:T(8,128)(2,1)} %shard_map.172), calls=%async_computation | async-start | bytes 1048576 | tf_op jit(solution)/shard_map/all_to_all | solution.py:274
  45.3 25.5 %copy-start.3 = (bf16[2,3,512,128]{3,2,1,0:T(8,128)(2,1)S(1)}, bf16[2,3,512,128]{3,2,1,0:T(8,128)(2,1)}, u32[]{:S(2)}) copy-start(bf16[2,3,512,128]{3,2,1,0:T(8,128)(2,1)} %w_proc.1) | copy-start | bytes 2359300
  67.4 9.5 %all-to-all-start.1 = ((bf16[4,256,128]{2,1,0:T(8,128)(2,1)}), bf16[4,256,128]{2,1,0:T(8,128)(2,1)S(1)}, u32[]{:S(2)}, u32[]{:S(2)}) async-start(bf16[4,256,128]{2,1,0:T(8,128)(2,1)} %get-tuple-element.20), calls=%async_computation.1 | async-start | bytes 524288 | tf_op jit(solution)/shard_map/all_to_all | solution.py:274
  76.9 1.5 copy-start
  78.4 14.2 %copy-start.19 = (s32[1,1024]{1,0:T(1,128)S(1)}, s32[1,1024]{1,0:T(1,128)}, u32[]{:S(2)}) copy-start(s32[1,1024]{1,0:T(1,128)} %local_src.3) | copy-start | bytes 12292
  78.4 14.2 %copy-start.20 = (s32[1,1024]{1,0:T(1,128)S(1)}, s32[1,1024]{1,0:T(1,128)}, u32[]{:S(2)}) copy-start(s32[1,1024]{1,0:T(1,128)} %local_dst.3) | copy-start | bytes 12292
  79.2 23.5 %copy-start.1 = (bf16[8,896,128]{2,1,0:T(8,128)(2,1)S(1)}, bf16[8,896,128]{2,1,0:T(8,128)(2,1)}, u32[]{:S(2)}) copy-start(bf16[8,896,128]{2,1,0:T(8,128)(2,1)} %all-gather.15.cloned.1.call-done) | copy-start | bytes 5505028
  103.5 23.2 %copy-start.9 = (bf16[512,128]{1,0:T(8,128)(2,1)S(1)}, bf16[512,128]{1,0:T(8,128)(2,1)}, u32[]{:S(2)}) copy-start(bf16[512,128]{1,0:T(8,128)(2,1)} %w_send.1) | copy-start | bytes 393220
Sparse Core Ops, SparseCore 0:
  23.7 27.5 all-gather.14

commit v3 on v2

--- a/solution.py
+++ b/solution.py
@@ -158,14 +158,15 @@
     agg[...] = jnp.broadcast_to(total.T.astype(BF16)[None], agg.shape)
 
 
-def rows_of(late, start, size):
-    half = late.shape[2]
+def rows_of(mine, other, start, size):
+    core = core_index()
+    half = mine.shape[1]
     parts = []
     while size > 0:
         k, low = start // half, start % half
         take = min(size, half - low)
         parts.append(
-            jnp.concatenate([late[k, c, low : low + take, :] for c in range(late.shape[1])], axis=1)
+            jnp.where(core == k, wide(mine, low, take), wide(other, low, take))
         )
         start, size = start + take, size - take
     return parts[0] if len(parts) == 1 else jnp.concatenate(parts, axis=0)
@@ -197,7 +198,7 @@
                         out[c, low - k * half : high - k * half, :] = rows
 
 
-def node_kernel(index, has_recv, agg4, state, weights, w_send, *rest):
+def node_kernel(index, has_recv, agg4, state, mine, other, w_send, *rest):
     if has_recv:
         w_recv, new_state, send, recv = rest
     else:
@@ -208,7 +209,7 @@
         before = wide(state, state.shape[1] - count, count).astype(F32)
     else:
         before = state[...]
-    after = before + dot(rms(agg).astype(BF16), rows_of(weights, index * agg.shape[1], agg.shape[1]))
+    after = before + dot(rms(agg).astype(BF16), rows_of(mine, other, index * agg.shape[1], agg.shape[1]))
     normed = rms(after.astype(BF16)).astype(BF16)
     send[...] = dot(normed, w_send[...]).astype(BF16)
     if has_recv:
@@ -249,10 +250,10 @@
     agg[...] = jnp.broadcast_to(total.T.astype(BF16)[None], agg.shape)
 
 
-def out_kernel(agg4, latent, weights, out):
+def out_kernel(agg4, latent, mine, other, out):
     combined = wide(agg4, 0, agg4.shape[1]).astype(F32) + latent[...].astype(F32)
     normed = rms(combined).astype(BF16)
-    out[...] = dot_last(rows_of(weights, 3 * normed.shape[1], out.shape[0]), normed).astype(BF16)
+    out[...] = dot_last(rows_of(mine, other, 3 * normed.shape[1], out.shape[0]), normed).astype(BF16)
 
 
 def call(kernel, out_shapes, *args, scratch=()):
@@ -302,9 +303,12 @@
     big = exchange(call(
         early_kernel, shape((chans, channel_rows + mesh_count, width)), w_in, mesh_latent
     ))
-    late = core_gather(exchange(call(
+    copies = call(
         late_kernel, shape((chans, late_rows // 2, width)), w_enc_out, w_proc, w_out.T
-    )))
+    )
+    copies, big = lax.optimization_barrier((copies, big))
+    mine = exchange(copies)
+    other = lax.ppermute(mine, "band", [(s, s ^ 1) for s in range(lax.axis_size("band"))])
 
     payload, recv, dec_recv, grid_latent = call(
         pre_kernel,
@@ -329,7 +333,7 @@
         state, send, recv = call(
             functools.partial(node_kernel, layer, True),
             (shape((mesh_count, latent_width), F32), shape((mesh_count, width)), shape((mesh_count, width))),
-            exchange(agg), state, late, w_proc[layer, 0], w_proc[layer, 1],
+            exchange(agg), state, mine, other, w_proc[layer, 0], w_proc[layer, 1],
         )
         pair, two, far = around(send)
         agg = call(
@@ -338,13 +342,13 @@
         )
     send = call(
         functools.partial(node_kernel, w_proc.shape[0], False), shape((mesh_count, width)),
-        exchange(agg), state, late, w_dec_src,
+        exchange(agg), state, mine, other, w_dec_src,
     )
     pair, two, far = around(send)
     agg = call(
         dec_kernel, shape((chans, grid_count, width)), pair, two, far, dec_recv, dec_src, dec_dst, dec_tab
     )
-    return call(out_kernel, shape((channels, grid_count)), exchange(agg), grid_latent, late).T
+    return call(out_kernel, shape((channels, grid_count)), exchange(agg), grid_latent, mine, other).T
 
 
 def solution(mesh):

time: 163 us -> 156 us (0.957)
  between operations: 13.7 us -> 0.26 us
  starting transfers between devices: 6.88 us -> 18.1 us
  blocking collectives: 111 us -> 101 us
  local copies, waits for them, and re-layouts: 4.49 us -> 11 us
    ppermute x0 -> x1, starting transfers between devices: none -> 9.67 us  [on_device(): lax.ppermute(mine, 'band', [(s, s ^ 1) for s in range(lax.axis_size('band...]
    all_gather x8, blocking collectives: 45.4 us -> 37.5 us  [core_gather(): lax.all_gather(block, 'band', axis_index_groups=[[s, s + 1] for s in rang...]
    unnamed x42 -> x64, local copies, waits for them, and re-layouts: 4.46 us -> 10.3 us
    all_to_all x4, blocking collectives: 43.2 us -> 41.3 us  [exchange(): return lax.all_to_all(copies, 'chan', 0, 0, tiled=True)]
  transfers between devices with their start and end apart: 3 -> 3, of which waited for: 2 -> 2; matrix products, arithmetic and copies ran while one was open for 0% -> 0% of each run, Pallas kernels for 3% -> 2%
where the time goes in v3:
time: 156 us; the launch traced here: 155 us
  blocking collectives  101 us (65%)
  starting transfers between devices  18.1 us (12%)
  Pallas kernels  12.5 us (8%)
  waiting for transfers between devices  12.1 us (8%)
  local copies, waits for them, and re-layouts  11 us (7%)
    all_to_all x4, blocking collectives, exchange(): return lax.all_to_all(copies, 'chan', 0, 0, tiled=True)  41.3 us
    all_gather x8, blocking collectives, core_gather(): lax.all_gather(block, 'band', axis_index_groups=[[s, s + 1] for s in rang...  37.5 us
    all_gather x4, blocking collectives, around(): two = lax.all_gather(pair, 'band', axis_index_groups=sides)  22.5 us
    pallas_call x11, Pallas kernels, call(): pl.pallas_call(kernel, out_shape=out_shapes, in_specs=[pl.BlockSpec(memor...  12.5 us
    all_to_all x2, waiting for transfers between devices, exchange(): return lax.all_to_all(copies, 'chan', 0, 0, tiled=True)  12.1 us
    unnamed x64, local copies, waits for them, and re-layouts  10.3 us
    ppermute x1, starting transfers between devices, on_device(): lax.ppermute(mine, 'band', [(s, s ^ 1) for s in range(lax.axis_size('band...  9.67 us
    all_to_all x2, starting transfers between devices, exchange(): return lax.all_to_all(copies, 'chan', 0, 0, tiled=True)  8.38 us
  transfers between devices with their start and end apart: 3, of which 2 were waited for; matrix products, arithmetic and copies ran while one was open for 0% of the time, Pallas kernels for 2%

profile of v3, /device:TPU:1, one launch (start us, length us, event | category | flops | bytes accessed | tf_op | source)
XLA Modules:
  0.0 155.3 jit_solution(16073100393426934245)
XLA Ops:
  0.0 0.9 copy-done.23
  2.6 5.0 %all-to-all-start = ((bf16[4,512,128]{2,1,0:T(8,128)(2,1)}), bf16[4,512,128]{2,1,0:T(8,128)(2,1)S(1)}, u32[]{:S(2)}, u32[]{:S(2)}) async-start(bf16[4,512,128]{2,1,0:T(8,128)(2,1)} %shard_map.173), calls=%async_computation | async-start | bytes 1048576 | tf_op jit(solution)/shard_map/all_to_all | solution.py:275
  7.7 6.8 %all-to-all-done.big.state = bf16[4,512,128]{2,1,0:T(8,128)(2,1)S(1)} async-done(((bf16[4,512,128]{2,1,0:T(8,128)(2,1)}), bf16[4,512,128]{2,1,0:T(8,128)(2,1)S(1)}, u32[]{:S(2)}, u32[]{:S(2)}) %all-to-all-start) | async-done | bytes 524320 | tf_op jit(solution)/shard_map/all_to_all | solution.py:275
  14.5 11.6 %all_to_all.30.mine = bf16[4,896,128]{2,1,0:T(8,128)(2,1)S(1)} all-to-all(bf16[4,896,128]{2,1,0:T(8,128)(2,1)S(1)} %shard_map.172), channel_id=1, replica_groups=mesh['band'=128,'chan'=4] {'chan'}, dimensions={0} | all-to-all | bytes 1835008 | tf_op jit(solution)/shard_map/all_to_all | solution.py:275
  26.1 9.7 %collective-permute-start = (bf16[4,896,128]{2,1,0:T(8,128)(2,1)S(1)}, bf16[4,896,128]{2,1,0:T(8,128)(2,1)S(1)}, u32[]{:S(2)}, u32[]{:S(2)}) collective-permute-start(bf16[4,896,128]{2,1,0:T(8,128)(2,1)S(1)} %all_to_all.30.mine), channel_id=1, source_target_pairs={{0,4},{4,0},{8,12},{12,8},{16,20},{20,16},{24,28},{28,24},{32,36},... | collective-permute-start | bytes 2752520 | tf_op jit(solution)/shard_map/ppermute | solution.py:311
  36.5 0.9 copy-done.10
  37.4 0.9 copy-done.11
  39.7 1.1 shard_map.174
  41.6 2.0 %all-gather = bf16[1344,128]{1,0:T(8,128)(2,1)S(1)} all-gather(bf16[672,128]{1,0:T(8,128)(2,1)S(1)} %get-tuple-element.21), channel_id=2, replica_groups={{0,4},{8,12},{16,20},{24,28},{32,36},{40,44},{48,52},{56,60},{64,68},{7..., dimensions={0}, use_global_device_ids=true | all-gather | bytes 516096 | tf_op jit(solution)/shard_map/all_gather | solution.py:280
  43.6 7.3 %all-gather.1 = bf16[4,672,128]{2,1,0:T(8,128)(2,1)S(1)} all-gather(bf16[2,672,128]{2,1,0:T(8,128)(2,1)S(1)} %bitcast.25), channel_id=3, replica_groups={{4,8},{12,16},{20,24},{28,32},{36,40},{44,48},{52,56},{60,64},{68,72},{..., dimensions={0}, use_global_device_ids=true | all-gather | bytes 1032192 | tf_op jit(solution)/shard_map/all_gather | solution.py:287
  51.0 11.2 %all-gather.2 = bf16[2,1,672,128]{3,2,1,0:T(8,128)(2,1)S(1)} all-gather(bf16[1,1,672,128]{3,2,1,0:T(8,128)(2,1)S(1)} %slice_select_fusion), channel_id=4, replica_groups={{0,4},{8,12},{16,20},{24,28},{32,36},{40,44},{48,52},{56,60},{64,68},{7..., dimensions={0}, use_global_device_ids=true | all-gather | bytes 516096 | tf_op jit(solution)/shard_map/all_gather | solution.py:280
  62.2 2.3 %shard_map.175 = (bf16[4,256,128]{2,1,0:T(8,128)(2,1)S(1)}, s32[4,8,128]{2,1,0:T(8,128)S(1)}, s32[2,4,8,128]{3,2,1,0:T(8,128)S(1)}) custom-call(bf16[2,672,128]{2,1,0:T(8,128)(2,1)S(1)} %bitcast.26, bf16[2,2,672,128]{3,2,1,0:T(8,128)(2,1)S(1)} %bitcast.24, bf16[2,672,128]{2,1,0:T(8,128)(2,1)S(1)} %bitcast.33, bf16[256,128]{1,0:T(8,128)(2,1)S(1)} %get-tuple-element.22.recv, ...), custom_call_target="tpu_custom_call" | custom-call | tf_op jit(solution)/shard_map/pallas_call | solution.py:260
  65.8 3.4 %all-to-all-start.1 = ((bf16[4,256,128]{2,1,0:T(8,128)(2,1)}), bf16[4,256,128]{2,1,0:T(8,128)(2,1)S(1)}, u32[]{:S(2)}, u32[]{:S(2)}) async-start(bf16[4,256,128]{2,1,0:T(8,128)(2,1)} %copy-done.6), calls=%async_computation.1 | async-start | bytes 524288 | tf_op jit(solution)/shard_map/all_to_all | solution.py:275
  69.9 5.3 %all-to-all-done.1.agg4 = bf16[4,256,128]{2,1,0:T(8,128)(2,1)S(1)} async-done(((bf16[4,256,128]{2,1,0:T(8,128)(2,1)}), bf16[4,256,128]{2,1,0:T(8,128)(2,1)S(1)}, u32[]{:S(2)}, u32[]{:S(2)}) %all-to-all-start.1) | async-done | bytes 262176 | tf_op jit(solution)/shard_map/all_to_all | solution.py:275
  75.3 0.9 copy-done.4
  76.2 0.9 copy-done.5
  77.8 3.0 %all-gather.3 = bf16[512,128]{1,0:T(8,128)(2,1)S(1)} all-gather(bf16[256,128]{1,0:T(8,128)(2,1)S(1)} %get-tuple-element.25), channel_id=5, replica_groups={{0,4},{8,12},{16,20},{24,28},{32,36},{40,44},{48,52},{56,60},{64,68},{7..., dimensions={0}, use_global_device_ids=true | all-gather | bytes 196608 | tf_op jit(solution)/shard_map/all_gather | solution.py:280
  80.9 5.1 %all-gather.4 = bf16[4,256,128]{2,1,0:T(8,128)(2,1)S(1)} all-gather(bf16[2,256,128]{2,1,0:T(8,128)(2,1)S(1)} %bitcast.38), channel_id=6, replica_groups={{4,8},{12,16},{20,24},{28,32},{36,40},{44,48},{52,56},{60,64},{68,72},{..., dimensions={0}, use_global_device_ids=true | all-gather | bytes 393216 | tf_op jit(solution)/shard_map/all_gather | solution.py:287
  86.0 5.2 %all-gather.5 = bf16[2,1,256,128]{3,2,1,0:T(8,128)(2,1)S(1)} all-gather(bf16[1,1,256,128]{3,2,1,0:T(8,128)(2,1)S(1)} %slice_select_fusion.3), channel_id=7, replica_groups={{0,4},{8,12},{16,20},{24,28},{32,36},{40,44},{48,52},{56,60},{64,68},{7..., dimensions={0}, use_global_device_ids=true | all-gather | bytes 196608 | tf_op jit(solution)/shard_map/all_gather | solution.py:280
  91.9 1.2 shard_map.177
  93.1 9.0 %all_to_all.31.agg4 = bf16[4,256,128]{2,1,0:T(8,128)(2,1)S(1)} all-to-all(bf16[4,256,128]{2,1,0:T(8,128)(2,1)S(1)} %shard_map.177), channel_id=1, replica_groups=mesh['band'=128,'chan'=4] {'chan'}, dimensions={0} | all-to-all | bytes 524288 | tf_op jit(solution)/shard_map/all_to_all | solution.py:275
  102.8 2.7 %all-gather.6 = bf16[512,128]{1,0:T(8,128)(2,1)S(1)} all-gather(bf16[256,128]{1,0:T(8,128)(2,1)S(1)} %get-tuple-element.29), channel_id=8, replica_groups={{0,4},{8,12},{16,20},{24,28},{32,36},{40,44},{48,52},{56,60},{64,68},{7..., dimensions={0}, use_global_device_ids=true | all-gather | bytes 196608 | tf_op jit(solution)/shard_map/all_gather | solution.py:280
  105.5 5.1 %all-gather.7 = bf16[4,256,128]{2,1,0:T(8,128)(2,1)S(1)} all-gather(bf16[2,256,128]{2,1,0:T(8,128)(2,1)S(1)} %bitcast.36), channel_id=9, replica_groups={{4,8},{12,16},{20,24},{28,32},{36,40},{44,48},{52,56},{60,64},{68,72},{..., dimensions={0}, use_global_device_ids=true | all-gather | bytes 393216 | tf_op jit(solution)/shard_map/all_gather | solution.py:287
  110.6 5.2 %all-gather.8 = bf16[2,1,256,128]{3,2,1,0:T(8,128)(2,1)S(1)} all-gather(bf16[1,1,256,128]{3,2,1,0:T(8,128)(2,1)S(1)} %slice_select_fusion.2), channel_id=10, replica_groups={{0,4},{8,12},{16,20},{24,28},{32,36},{40,44},{48,52},{56,60},{64,68},{7..., dimensions={0}, use_global_device_ids=true | all-gather | bytes 196608 | tf_op jit(solution)/shard_map/all_gather | solution.py:280
  115.8 1.2 shard_map.179
  117.0 9.0 %all_to_all.32.agg4 = bf16[4,256,128]{2,1,0:T(8,128)(2,1)S(1)} all-to-all(bf16[4,256,128]{2,1,0:T(8,128)(2,1)S(1)} %shard_map.179), channel_id=1, replica_groups=mesh['band'=128,'chan'=4] {'chan'}, dimensions={0} | all-to-all | bytes 524288 | tf_op jit(solution)/shard_map/all_to_all | solution.py:275
  126.6 2.7 %all-gather.9 = bf16[512,128]{1,0:T(8,128)(2,1)S(1)} all-gather(bf16[256,128]{1,0:T(8,128)(2,1)S(1)} %shard_map.180), channel_id=11, replica_groups={{0,4},{8,12},{16,20},{24,28},{32,36},{40,44},{48,52},{56,60},{64,68},{7..., dimensions={0}, use_global_device_ids=true | all-gather | bytes 196608 | tf_op jit(solution)/shard_map/all_gather | solution.py:280
  129.4 5.1 %all-gather.10 = bf16[4,256,128]{2,1,0:T(8,128)(2,1)S(1)} all-gather(bf16[2,256,128]{2,1,0:T(8,128)(2,1)S(1)} %bitcast.34), channel_id=12, replica_groups={{4,8},{12,16},{20,24},{28,32},{36,40},{44,48},{52,56},{60,64},{68,72},{..., dimensions={0}, use_global_device_ids=true | all-gather | bytes 393216 | tf_op jit(solution)/shard_map/all_gather | solution.py:287
  134.5 5.4 %all-gather.11 = bf16[2,1,256,128]{3,2,1,0:T(8,128)(2,1)S(1)} all-gather(bf16[1,1,256,128]{3,2,1,0:T(8,128)(2,1)S(1)} %slice_select_fusion.1), channel_id=13, replica_groups={{0,4},{8,12},{16,20},{24,28},{32,36},{40,44},{48,52},{56,60},{64,68},{7..., dimensions={0}, use_global_device_ids=true | all-gather | bytes 196608 | tf_op jit(solution)/shard_map/all_gather | solution.py:280
  139.8 2.4 %shard_map.181 = bf16[4,512,128]{2,1,0:T(8,128)(2,1)S(1)} custom-call(bf16[2,256,128]{2,1,0:T(8,128)(2,1)S(1)} %bitcast.35, bf16[2,2,256,128]{3,2,1,0:T(8,128)(2,1)S(1)} %bitcast.28, bf16[2,256,128]{2,1,0:T(8,128)(2,1)S(1)} %bitcast.40, bf16[512,128]{1,0:T(8,128)(2,1)S(1)} %copy-done.14, s32[5,512]{1,0:T(8,128)S(1)} %copy-done.18, s32[5,512]{1,0:T(8,128)S(1)} %copy-done.20, ...), custom_call_target="tpu_custom_call" | custom-call | tf_op jit(solution)/shard_map/pallas_call | solution.py:260
  142.3 11.8 %all_to_all.33.agg4 = bf16[4,512,128]{2,1,0:T(8,128)(2,1)S(1)} all-to-all(bf16[4,512,128]{2,1,0:T(8,128)(2,1)S(1)} %shard_map.181), channel_id=1, replica_groups=mesh['band'=128,'chan'=4] {'chan'}, dimensions={0} | all-to-all | bytes 1048576 | tf_op jit(solution)/shard_map/all_to_all | solution.py:275
  154.1 1.2 shard_map.182
  (70 shorter events, 9.7 us)
Async XLA Ops:
  0.0 7.6 %copy-start = (bf16[2,3,512,128]{3,2,1,0:T(8,128)(2,1)S(1)}, bf16[2,3,512,128]{3,2,1,0:T(8,128)(2,1)}, u32[]{:S(2)}) copy-start(bf16[2,3,512,128]{3,2,1,0:T(8,128)(2,1)} %w_proc.1) | copy-start | bytes 2359300
  0.0 0.9 copy-start.23
  0.9 0.8 copy-start.24
  2.6 5.0 %copy-start.8 = (bf16[512,128]{1,0:T(8,128)(2,1)S(1)}, bf16[512,128]{1,0:T(8,128)(2,1)}, u32[]{:S(2)}) copy-start(bf16[512,128]{1,0:T(8,128)(2,1)} %w_enc_out.1) | copy-start | bytes 393220
  2.6 5.0 %copy-start.25 = (bf16[128,227]{0,1:T(8,128)(2,1)S(1)}, bf16[128,227]{0,1:T(8,128)(2,1)}, u32[]{:S(2)}) copy-start(bf16[128,227]{0,1:T(8,128)(2,1)} %param.27) | copy-start | bytes 174340
  2.6 11.9 %all-to-all-start = ((bf16[4,512,128]{2,1,0:T(8,128)(2,1)}), bf16[4,512,128]{2,1,0:T(8,128)(2,1)S(1)}, u32[]{:S(2)}, u32[]{:S(2)}) async-start(bf16[4,512,128]{2,1,0:T(8,128)(2,1)} %shard_map.173), calls=%async_computation | async-start | bytes 1048576 | tf_op jit(solution)/shard_map/all_to_all | solution.py:275
  7.7 28.1 %copy-start.7 = (bf16[512,227]{0,1:T(8,128)(2,1)S(1)}, bf16[512,227]{0,1:T(8,128)(2,1)}, u32[]{:S(2)}) copy-start(bf16[512,227]{0,1:T(8,128)(2,1)} %param.18) | copy-start | bytes 697348
  7.7 28.1 %copy-start.9 = (bf16[512,128]{1,0:T(8,128)(2,1)S(1)}, bf16[512,128]{1,0:T(8,128)(2,1)}, u32[]{:S(2)}) copy-start(bf16[512,128]{1,0:T(8,128)(2,1)} %w_es.1) | copy-start | bytes 393220
  14.5 21.3 %copy-start.15 = (s32[5,512]{1,0:T(8,128)S(1)}, s32[5,512]{1,0:T(8,128)}, u32[]{:S(2)}) copy-start(s32[5,512]{1,0:T(8,128)} %enc_src.3) | copy-start | bytes 30724
  14.5 21.3 %copy-start.16 = (s32[5,512]{1,0:T(8,128)S(1)}, s32[5,512]{1,0:T(8,128)}, u32[]{:S(2)}) copy-start(s32[5,512]{1,0:T(8,128)} %enc_dst.3) | copy-start | bytes 30724
  26.1 49.2 %collective-permute-start = (bf16[4,896,128]{2,1,0:T(8,128)(2,1)S(1)}, bf16[4,896,128]{2,1,0:T(8,128)(2,1)S(1)}, u32[]{:S(2)}, u32[]{:S(2)}) collective-permute-start(bf16[4,896,128]{2,1,0:T(8,128)(2,1)S(1)} %all_to_all.30.mine), channel_id=1, source_target_pairs={{0,4},{4,0},{8,12},{12,8},{16,20},{20,16},{24,28},{28,24},{32,36},... | collective-permute-start | bytes 2752520 | tf_op jit(solution)/shard_map/ppermute | solution.py:311
  35.8 0.7 copy-start.27
  35.8 0.7 copy-start.26
  36.5 0.9 copy-start.10
  37.4 0.9 copy-start.11
  38.3 0.7 copy-start.17
  39.0 0.7 copy-start.19
  40.8 0.8 copy-start.1
  41.6 2.0 %copy-start.13 = (bf16[512,128]{1,0:T(8,128)(2,1)}, bf16[512,128]{1,0:T(8,128)(2,1)S(1)}, u32[]{:S(2)}) copy-start(bf16[512,128]{1,0:T(8,128)(2,1)S(1)} %get-tuple-element.32.recv) | copy-start | bytes 393220
  64.5 0.7 copy-start.6
  65.8 9.5 %all-to-all-start.1 = ((bf16[4,256,128]{2,1,0:T(8,128)(2,1)}), bf16[4,256,128]{2,1,0:T(8,128)(2,1)S(1)}, u32[]{:S(2)}, u32[]{:S(2)}) async-start(bf16[4,256,128]{2,1,0:T(8,128)(2,1)} %copy-done.6), calls=%async_computation.1 | async-start | bytes 524288 | tf_op jit(solution)/shard_map/all_to_all | solution.py:275
  75.3 0.9 copy-start.4
  76.2 0.9 copy-start.5
  86.0 5.2 %copy-start.22 = (s32[4,8,128]{2,1,0:T(8,128)S(1)}, s32[4,8,128]{2,1,0:T(8,128)}, u32[]{:S(2)}) copy-start(s32[4,8,128]{2,1,0:T(8,128)} %copy-done.21) | copy-start | bytes 49156
  86.0 5.2 %copy-start.31 = (s32[1,1024]{1,0:T(1,128)S(1)}, s32[1,1024]{1,0:T(1,128)}, u32[]{:S(2)}) copy-start(s32[1,1024]{1,0:T(1,128)} %local_dst.3) | copy-start | bytes 12292
  93.1 9.0 %copy-start.3 = (bf16[512,128]{1,0:T(8,128)(2,1)S(1)}, bf16[512,128]{1,0:T(8,128)(2,1)}, u32[]{:S(2)}) copy-start(bf16[512,128]{1,0:T(8,128)(2,1)} %get-tuple-element.38.w_send) | copy-start | bytes 393220
  117.0 9.0 %copy-start.12 = (bf16[512,128]{1,0:T(8,128)(2,1)S(1)}, bf16[512,128]{1,0:T(8,128)(2,1)}, u32[]{:S(2)}) copy-start(bf16[512,128]{1,0:T(8,128)(2,1)} %w_send.1) | copy-start | bytes 393220
  134.4 5.4 %copy-start.18 = (s32[5,512]{1,0:T(8,128)S(1)}, s32[5,512]{1,0:T(8,128)}, u32[]{:S(2)}) copy-start(s32[5,512]{1,0:T(8,128)} %dec_src.3) | copy-start | bytes 30724
  134.4 5.4 %copy-start.20 = (s32[5,512]{1,0:T(8,128)S(1)}, s32[5,512]{1,0:T(8,128)}, u32[]{:S(2)}) copy-start(s32[5,512]{1,0:T(8,128)} %dec_dst.3) | copy-start | bytes 30724
  134.5 5.4 %copy-start.14 = (bf16[512,128]{1,0:T(8,128)(2,1)S(1)}, bf16[512,128]{1,0:T(8,128)(2,1)}, u32[]{:S(2)}) copy-start(bf16[512,128]{1,0:T(8,128)(2,1)} %copy-done.13) | copy-start | bytes 393220
  134.5 5.4 %copy-start.29 = (s32[2,4,8,128]{3,2,1,0:T(8,128)S(1)}, s32[2,4,8,128]{3,2,1,0:T(8,128)}, u32[]{:S(2)}) copy-start(s32[2,4,8,128]{3,2,1,0:T(8,128)} %copy-done.28) | copy-start | bytes 98308
  142.3 11.8 %copy-start.2 = (bf16[512,512]{1,0:T(8,128)(2,1)S(1)}, bf16[512,512]{1,0:T(8,128)(2,1)}, u32[]{:S(2)}) copy-start(bf16[512,512]{1,0:T(8,128)(2,1)} %copy-done.1) | copy-start | bytes 1572868
  (3 other events, 1.9 us)

commit v4 on v2

--- a/solution.py
+++ b/solution.py
@@ -12,6 +12,7 @@
 BF16 = jnp.bfloat16
 I32 = jnp.int32
 LANES = 128
+CHANS = 4
 TILE = 32
 TABLES = 5
 
@@ -158,17 +159,16 @@
     agg[...] = jnp.broadcast_to(total.T.astype(BF16)[None], agg.shape)
 
 
-def rows_of(late, start, size):
-    half = late.shape[2]
-    parts = []
-    while size > 0:
-        k, low = start // half, start % half
-        take = min(size, half - low)
-        parts.append(
-            jnp.concatenate([late[k, c, low : low + take, :] for c in range(late.shape[1])], axis=1)
-        )
-        start, size = start + take, size - take
-    return parts[0] if len(parts) == 1 else jnp.concatenate(parts, axis=0)
+def source(k):
+    return lax.rem(lax.axis_index("chan") + CHANS - k, CHANS)
+
+
+def arrived(blocks, start, size):
+    return jnp.concatenate([block[start : start + size, :] for block in blocks], axis=1)
+
+
+def columns_at(k):
+    return pl.ds(pl.multiple_of(source(k) * LANES, LANES), LANES)
 
 
 def early_kernel(w_in, mesh_latent, out):
@@ -180,24 +180,14 @@
 
 
 def late_kernel(w_enc_out, w_proc, w_out, out):
-    core = core_index()
-    half = out.shape[1]
     depth = w_enc_out.shape[0]
-    for k in range(2):
-
-        @pl.when(core == k)
-        def _():
-            for i in range(4):
-                block = (w_enc_out, w_proc.at[0, 2], w_proc.at[1, 2], w_out)[i]
-                low = max(i * depth, k * half)
-                high = min(i * depth + block.shape[0], (k + 1) * half)
-                if low < high:
-                    rows = block[low - i * depth : high - i * depth, :]
-                    for c in range(out.shape[0]):
-                        out[c, low - k * half : high - k * half, :] = rows
-
-
-def node_kernel(index, has_recv, agg4, state, weights, w_send, *rest):
+    out[0:depth, :] = w_enc_out[...]
+    out[depth : 2 * depth, :] = w_proc[0, 2]
+    out[2 * depth : 3 * depth, :] = w_proc[1, 2]
+    out[3 * depth : 3 * depth + w_out.shape[0], :] = w_out[...]
+
+
+def node_kernel(index, has_recv, agg4, state, b0, b1, b2, b3, w_send, *rest):
     if has_recv:
         w_recv, new_state, send, recv = rest
     else:
@@ -205,15 +195,22 @@
     count = agg4.shape[1]
     agg = wide(agg4, 0, count)
     if len(state.shape) == 3:
-        before = wide(state, state.shape[1] - count, count).astype(F32)
+        first = state.shape[1] - count
+        before = jnp.concatenate([state[source(k), first:, :] for k in range(CHANS)], axis=1).astype(F32)
     else:
         before = state[...]
-    after = before + dot(rms(agg).astype(BF16), rows_of(weights, index * agg.shape[1], agg.shape[1]))
+    depth = agg.shape[1]
+    update = arrived((b0, b1, b2, b3), index * depth, depth)
+    after = before + dot(rms(agg).astype(BF16), update)
     normed = rms(after.astype(BF16)).astype(BF16)
-    send[...] = dot(normed, w_send[...]).astype(BF16)
+
+    def turned(weight):
+        return jnp.concatenate([weight[columns_at(k), :] for k in range(CHANS)], axis=0)
+
+    send[...] = dot(normed, turned(w_send)).astype(BF16)
     if has_recv:
         new_state[...] = after
-        recv[...] = dot(normed, w_recv[...]).astype(BF16)
+        recv[...] = dot(normed, turned(w_recv)).astype(BF16)
 
 
 def proc_kernel(pair, two, far, recv, local_src, local_dst, proc_src, proc_dst, tab, agg):
@@ -249,10 +246,13 @@
     agg[...] = jnp.broadcast_to(total.T.astype(BF16)[None], agg.shape)
 
 
-def out_kernel(agg4, latent, weights, out):
-    combined = wide(agg4, 0, agg4.shape[1]).astype(F32) + latent[...].astype(F32)
+def out_kernel(agg4, latent, b0, b1, b2, b3, out):
+    combined = jnp.concatenate(
+        [agg4[source(k)].astype(F32) + latent[:, columns_at(k)].astype(F32) for k in range(CHANS)], axis=1
+    )
     normed = rms(combined).astype(BF16)
-    out[...] = dot_last(rows_of(weights, 3 * normed.shape[1], out.shape[0]), normed).astype(BF16)
+    weights = arrived((b0, b1, b2, b3), 3 * normed.shape[1], out.shape[0])
+    out[...] = dot_last(weights, normed).astype(BF16)
 
 
 def call(kernel, out_shapes, *args, scratch=()):
@@ -262,7 +262,7 @@
         in_specs=[pl.BlockSpec(memory_space=pltpu.VMEM)] * len(args),
         out_specs=jax.tree.map(lambda _: pl.BlockSpec(memory_space=pltpu.VMEM), out_shapes),
         scratch_shapes=scratch,
-        compiler_params=pltpu.CompilerParams(vmem_limit_bytes=40 * 1024 * 1024),
+        compiler_params=pltpu.CompilerParams(vmem_limit_bytes=16 * 1024 * 1024),
     )(*args)
 
 
@@ -302,9 +302,11 @@
     big = exchange(call(
         early_kernel, shape((chans, channel_rows + mesh_count, width)), w_in, mesh_latent
     ))
-    late = core_gather(exchange(call(
-        late_kernel, shape((chans, late_rows // 2, width)), w_enc_out, w_proc, w_out.T
-    )))
+    late = call(late_kernel, shape((late_rows, width)), w_enc_out, w_proc, w_out.T)
+    late, big = lax.optimization_barrier((late, big))
+    blocks = [late] + [
+        lax.ppermute(late, "chan", [(s, (s + k) % chans) for s in range(chans)]) for k in range(1, chans)
+    ]
 
     payload, recv, dec_recv, grid_latent = call(
         pre_kernel,
@@ -329,7 +331,7 @@
         state, send, recv = call(
             functools.partial(node_kernel, layer, True),
             (shape((mesh_count, latent_width), F32), shape((mesh_count, width)), shape((mesh_count, width))),
-            exchange(agg), state, late, w_proc[layer, 0], w_proc[layer, 1],
+            exchange(agg), state, *blocks, w_proc[layer, 0], w_proc[layer, 1],
         )
         pair, two, far = around(send)
         agg = call(
@@ -338,13 +340,13 @@
         )
     send = call(
         functools.partial(node_kernel, w_proc.shape[0], False), shape((mesh_count, width)),
-        exchange(agg), state, late, w_dec_src,
+        exchange(agg), state, *blocks, w_dec_src,
     )
     pair, two, far = around(send)
     agg = call(
         dec_kernel, shape((chans, grid_count, width)), pair, two, far, dec_recv, dec_src, dec_dst, dec_tab
     )
-    return call(out_kernel, shape((channels, grid_count)), exchange(agg), grid_latent, late).T
+    return call(out_kernel, shape((channels, grid_count)), exchange(agg), grid_latent, *blocks).T
 
 
 def solution(mesh):

time: 163 us -> 148 us (0.908)
  blocking collectives: 111 us -> 94.6 us
  between operations: 13.7 us -> 0.31 us
  starting transfers between devices: 6.88 us -> 17.3 us
  local copies, waits for them, and re-layouts: 4.49 us -> 10.4 us
    all_to_all x4 -> x3, blocking collectives: 43.2 us -> 29.7 us  [exchange(): return lax.all_to_all(copies, 'chan', 0, 0, tiled=True)]
    ppermute x0 -> x3, starting transfers between devices: none -> 8.4 us  [on_device(): lax.ppermute(late, 'chan', [(s, (s + k) % chans) for s in range(chans)])]
    unnamed x42 -> x64, local copies, waits for them, and re-layouts: 4.46 us -> 9.66 us
    all_gather x8, blocking collectives: 45.4 us -> 42.4 us  [core_gather(): lax.all_gather(block, 'band', axis_index_groups=[[s, s + 1] for s in rang...]
    all_to_all x2, starting transfers between devices: 6.87 us -> 8.88 us  [exchange(): return lax.all_to_all(copies, 'chan', 0, 0, tiled=True)]
  transfers between devices with their start and end apart: 3 -> 5, of which waited for: 2 -> 2; matrix products, arithmetic and copies ran while one was open for 0% -> 1% of each run, Pallas kernels for 3% -> 2%
where the time goes in v4:
time: 148 us; the launch traced here: 147 us
  blocking collectives  94.6 us (64%)
  starting transfers between devices  17.3 us (12%)
  Pallas kernels  12.4 us (8%)
  waiting for transfers between devices  11.9 us (8%)
  local copies, waits for them, and re-layouts  10.4 us (7%)
    all_gather x8, blocking collectives, core_gather(): lax.all_gather(block, 'band', axis_index_groups=[[s, s + 1] for s in rang...  42.4 us
    all_to_all x3, blocking collectives, exchange(): return lax.all_to_all(copies, 'chan', 0, 0, tiled=True)  29.7 us
    all_gather x4, blocking collectives, around(): two = lax.all_gather(pair, 'band', axis_index_groups=sides)  22.5 us
    pallas_call x11, Pallas kernels, call(): pl.pallas_call(kernel, out_shape=out_shapes, in_specs=[pl.BlockSpec(memor...  12.4 us
    all_to_all x2, waiting for transfers between devices, exchange(): return lax.all_to_all(copies, 'chan', 0, 0, tiled=True)  11.9 us
    unnamed x64, local copies, waits for them, and re-layouts  9.66 us
    all_to_all x2, starting transfers between devices, exchange(): return lax.all_to_all(copies, 'chan', 0, 0, tiled=True)  8.88 us
    ppermute x3, starting transfers between devices, on_device(): lax.ppermute(late, 'chan', [(s, (s + k) % chans) for s in range(chans)])  8.4 us
  transfers between devices with their start and end apart: 5, of which 2 were waited for; matrix products, arithmetic and copies ran while one was open for 1% of the time, Pallas kernels for 2%

profile of v4, /device:TPU:1, one launch (start us, length us, event | category | flops | bytes accessed | tf_op | source)
XLA Modules:
  0.0 146.9 jit_solution(15992141071427695700)
XLA Ops:
  0.0 0.9 copy-done.23
  2.6 5.0 %all-to-all-start = ((bf16[4,512,128]{2,1,0:T(8,128)(2,1)}), bf16[4,512,128]{2,1,0:T(8,128)(2,1)S(1)}, u32[]{:S(2)}, u32[]{:S(2)}) async-start(bf16[4,512,128]{2,1,0:T(8,128)(2,1)} %shard_map.173), calls=%async_computation | async-start | bytes 1048576 | tf_op jit(solution)/shard_map/all_to_all | solution.py:274
  7.7 6.8 %all-to-all-done.big.state = bf16[4,512,128]{2,1,0:T(8,128)(2,1)S(1)} async-done(((bf16[4,512,128]{2,1,0:T(8,128)(2,1)}), bf16[4,512,128]{2,1,0:T(8,128)(2,1)S(1)}, u32[]{:S(2)}, u32[]{:S(2)}) %all-to-all-start) | async-done | bytes 524320 | tf_op jit(solution)/shard_map/all_to_all | solution.py:274
  14.5 2.2 %collective-permute-start = (bf16[1792,128]{1,0:T(8,128)(2,1)S(1)}, bf16[1792,128]{1,0:T(8,128)(2,1)S(1)}, u32[]{:S(2)}, u32[]{:S(2)}) collective-permute-start(bf16[1792,128]{1,0:T(8,128)(2,1)S(1)} %shard_map.172.b0), channel_id=1, source_target_pairs={{0,1},{1,2},{2,3},{3,0},{4,5},{5,6},{6,7},{7,4},{8,9},{9,10},{10,1... | collective-permute-start | bytes 1376264 | tf_op jit(solution)/shard_map/ppermute | solution.py:308
  16.7 3.7 %collective-permute-start.1 = (bf16[1792,128]{1,0:T(8,128)(2,1)S(1)}, bf16[1792,128]{1,0:T(8,128)(2,1)S(1)}, u32[]{:S(2)}, u32[]{:S(2)}) collective-permute-start(bf16[1792,128]{1,0:T(8,128)(2,1)S(1)} %shard_map.172.b0), channel_id=1, source_target_pairs={{0,2},{1,3},{2,0},{3,1},{4,6},{5,7},{6,4},{7,5},{8,10},{9,11},{10,... | collective-permute-start | bytes 1376264 | tf_op jit(solution)/shard_map/ppermute | solution.py:308
  20.4 2.5 %collective-permute-start.2 = (bf16[1792,128]{1,0:T(8,128)(2,1)S(1)}, bf16[1792,128]{1,0:T(8,128)(2,1)S(1)}, u32[]{:S(2)}, u32[]{:S(2)}) collective-permute-start(bf16[1792,128]{1,0:T(8,128)(2,1)S(1)} %shard_map.172.b0), channel_id=1, source_target_pairs={{0,3},{1,0},{2,1},{3,2},{4,7},{5,4},{6,5},{7,6},{8,11},{9,8},{10,9... | collective-permute-start | bytes 1376264 | tf_op jit(solution)/shard_map/ppermute | solution.py:308
  23.0 0.9 copy-done.9
  23.9 0.9 copy-done.10
  26.2 1.1 shard_map.174
  28.1 9.8 %all-gather = bf16[1344,128]{1,0:T(8,128)(2,1)S(1)} all-gather(bf16[672,128]{1,0:T(8,128)(2,1)S(1)} %get-tuple-element.21), channel_id=2, replica_groups={{0,4},{8,12},{16,20},{24,28},{32,36},{40,44},{48,52},{56,60},{64,68},{7..., dimensions={0}, use_global_device_ids=true | all-gather | bytes 516096 | tf_op jit(solution)/shard_map/all_gather | solution.py:279
  38.0 7.3 %all-gather.1 = bf16[4,672,128]{2,1,0:T(8,128)(2,1)S(1)} all-gather(bf16[2,672,128]{2,1,0:T(8,128)(2,1)S(1)} %bitcast.25), channel_id=3, replica_groups={{4,8},{12,16},{20,24},{28,32},{36,40},{44,48},{52,56},{60,64},{68,72},{..., dimensions={0}, use_global_device_ids=true | all-gather | bytes 1032192 | tf_op jit(solution)/shard_map/all_gather | solution.py:286
  45.3 7.9 %all-gather.2 = bf16[2,1,672,128]{3,2,1,0:T(8,128)(2,1)S(1)} all-gather(bf16[1,1,672,128]{3,2,1,0:T(8,128)(2,1)S(1)} %slice_select_fusion), channel_id=4, replica_groups={{0,4},{8,12},{16,20},{24,28},{32,36},{40,44},{48,52},{56,60},{64,68},{7..., dimensions={0}, use_global_device_ids=true | all-gather | bytes 516096 | tf_op jit(solution)/shard_map/all_gather | solution.py:279
  53.2 2.3 %shard_map.175 = (bf16[4,256,128]{2,1,0:T(8,128)(2,1)S(1)}, s32[4,8,128]{2,1,0:T(8,128)S(1)}, s32[2,4,8,128]{3,2,1,0:T(8,128)S(1)}) custom-call(bf16[2,672,128]{2,1,0:T(8,128)(2,1)S(1)} %bitcast.26, bf16[2,2,672,128]{3,2,1,0:T(8,128)(2,1)S(1)} %bitcast.24, bf16[2,672,128]{2,1,0:T(8,128)(2,1)S(1)} %bitcast.33, bf16[256,128]{1,0:T(8,128)(2,1)S(1)} %get-tuple-element.22.recv, ...), custom_call_target="tpu_custom_call" | custom-call | tf_op jit(solution)/shard_map/pallas_call | solution.py:259
  56.8 3.9 %all-to-all-start.1 = ((bf16[4,256,128]{2,1,0:T(8,128)(2,1)}), bf16[4,256,128]{2,1,0:T(8,128)(2,1)S(1)}, u32[]{:S(2)}, u32[]{:S(2)}) async-start(bf16[4,256,128]{2,1,0:T(8,128)(2,1)} %copy-done.6), calls=%async_computation.1 | async-start | bytes 524288 | tf_op jit(solution)/shard_map/all_to_all | solution.py:274
  61.5 5.1 %all-to-all-done.1.agg4 = bf16[4,256,128]{2,1,0:T(8,128)(2,1)S(1)} async-done(((bf16[4,256,128]{2,1,0:T(8,128)(2,1)}), bf16[4,256,128]{2,1,0:T(8,128)(2,1)S(1)}, u32[]{:S(2)}, u32[]{:S(2)}) %all-to-all-start.1) | async-done | bytes 262176 | tf_op jit(solution)/shard_map/all_to_all | solution.py:274
  67.5 0.9 copy-done.5
  69.1 3.4 %all-gather.3 = bf16[512,128]{1,0:T(8,128)(2,1)S(1)} all-gather(bf16[256,128]{1,0:T(8,128)(2,1)S(1)} %get-tuple-element.25), channel_id=5, replica_groups={{0,4},{8,12},{16,20},{24,28},{32,36},{40,44},{48,52},{56,60},{64,68},{7..., dimensions={0}, use_global_device_ids=true | all-gather | bytes 196608 | tf_op jit(solution)/shard_map/all_gather | solution.py:279
  72.5 5.1 %all-gather.4 = bf16[4,256,128]{2,1,0:T(8,128)(2,1)S(1)} all-gather(bf16[2,256,128]{2,1,0:T(8,128)(2,1)S(1)} %bitcast.38), channel_id=6, replica_groups={{4,8},{12,16},{20,24},{28,32},{36,40},{44,48},{52,56},{60,64},{68,72},{..., dimensions={0}, use_global_device_ids=true | all-gather | bytes 393216 | tf_op jit(solution)/shard_map/all_gather | solution.py:286
  77.6 5.2 %all-gather.5 = bf16[2,1,256,128]{3,2,1,0:T(8,128)(2,1)S(1)} all-gather(bf16[1,1,256,128]{3,2,1,0:T(8,128)(2,1)S(1)} %slice_select_fusion.3), channel_id=7, replica_groups={{0,4},{8,12},{16,20},{24,28},{32,36},{40,44},{48,52},{56,60},{64,68},{7..., dimensions={0}, use_global_device_ids=true | all-gather | bytes 196608 | tf_op jit(solution)/shard_map/all_gather | solution.py:279
  83.5 1.2 shard_map.177
  84.7 9.0 %all_to_all.25.agg4 = bf16[4,256,128]{2,1,0:T(8,128)(2,1)S(1)} all-to-all(bf16[4,256,128]{2,1,0:T(8,128)(2,1)S(1)} %shard_map.177), channel_id=1, replica_groups=mesh['band'=128,'chan'=4] {'chan'}, dimensions={0} | all-to-all | bytes 524288 | tf_op jit(solution)/shard_map/all_to_all | solution.py:274
  94.4 2.7 %all-gather.6 = bf16[512,128]{1,0:T(8,128)(2,1)S(1)} all-gather(bf16[256,128]{1,0:T(8,128)(2,1)S(1)} %get-tuple-element.29), channel_id=8, replica_groups={{0,4},{8,12},{16,20},{24,28},{32,36},{40,44},{48,52},{56,60},{64,68},{7..., dimensions={0}, use_global_device_ids=true | all-gather | bytes 196608 | tf_op jit(solution)/shard_map/all_gather | solution.py:279
  97.1 5.1 %all-gather.7 = bf16[4,256,128]{2,1,0:T(8,128)(2,1)S(1)} all-gather(bf16[2,256,128]{2,1,0:T(8,128)(2,1)S(1)} %bitcast.36), channel_id=9, replica_groups={{4,8},{12,16},{20,24},{28,32},{36,40},{44,48},{52,56},{60,64},{68,72},{..., dimensions={0}, use_global_device_ids=true | all-gather | bytes 393216 | tf_op jit(solution)/shard_map/all_gather | solution.py:286
  102.2 5.2 %all-gather.8 = bf16[2,1,256,128]{3,2,1,0:T(8,128)(2,1)S(1)} all-gather(bf16[1,1,256,128]{3,2,1,0:T(8,128)(2,1)S(1)} %slice_select_fusion.2), channel_id=10, replica_groups={{0,4},{8,12},{16,20},{24,28},{32,36},{40,44},{48,52},{56,60},{64,68},{7..., dimensions={0}, use_global_device_ids=true | all-gather | bytes 196608 | tf_op jit(solution)/shard_map/all_gather | solution.py:279
  107.4 1.2 shard_map.179
  108.6 9.0 %all_to_all.26.agg4 = bf16[4,256,128]{2,1,0:T(8,128)(2,1)S(1)} all-to-all(bf16[4,256,128]{2,1,0:T(8,128)(2,1)S(1)} %shard_map.179), channel_id=1, replica_groups=mesh['band'=128,'chan'=4] {'chan'}, dimensions={0} | all-to-all | bytes 524288 | tf_op jit(solution)/shard_map/all_to_all | solution.py:274
  118.2 2.7 %all-gather.9 = bf16[512,128]{1,0:T(8,128)(2,1)S(1)} all-gather(bf16[256,128]{1,0:T(8,128)(2,1)S(1)} %shard_map.180), channel_id=11, replica_groups={{0,4},{8,12},{16,20},{24,28},{32,36},{40,44},{48,52},{56,60},{64,68},{7..., dimensions={0}, use_global_device_ids=true | all-gather | bytes 196608 | tf_op jit(solution)/shard_map/all_gather | solution.py:279
  121.0 5.1 %all-gather.10 = bf16[4,256,128]{2,1,0:T(8,128)(2,1)S(1)} all-gather(bf16[2,256,128]{2,1,0:T(8,128)(2,1)S(1)} %bitcast.34), channel_id=12, replica_groups={{4,8},{12,16},{20,24},{28,32},{36,40},{44,48},{52,56},{60,64},{68,72},{..., dimensions={0}, use_global_device_ids=true | all-gather | bytes 393216 | tf_op jit(solution)/shard_map/all_gather | solution.py:286
  126.1 5.4 %all-gather.11 = bf16[2,1,256,128]{3,2,1,0:T(8,128)(2,1)S(1)} all-gather(bf16[1,1,256,128]{3,2,1,0:T(8,128)(2,1)S(1)} %slice_select_fusion.1), channel_id=13, replica_groups={{0,4},{8,12},{16,20},{24,28},{32,36},{40,44},{48,52},{56,60},{64,68},{7..., dimensions={0}, use_global_device_ids=true | all-gather | bytes 196608 | tf_op jit(solution)/shard_map/all_gather | solution.py:279
  131.4 2.4 %shard_map.181 = bf16[4,512,128]{2,1,0:T(8,128)(2,1)S(1)} custom-call(bf16[2,256,128]{2,1,0:T(8,128)(2,1)S(1)} %bitcast.35, bf16[2,2,256,128]{3,2,1,0:T(8,128)(2,1)S(1)} %bitcast.28, bf16[2,256,128]{2,1,0:T(8,128)(2,1)S(1)} %bitcast.40, bf16[512,128]{1,0:T(8,128)(2,1)S(1)} %copy-done.13, s32[5,512]{1,0:T(8,128)S(1)} %copy-done.18, s32[5,512]{1,0:T(8,128)S(1)} %copy-done.20, ...), custom_call_target="tpu_custom_call" | custom-call | tf_op jit(solution)/shard_map/pallas_call | solution.py:259
  133.9 11.8 %all_to_all.27.agg4 = bf16[4,512,128]{2,1,0:T(8,128)(2,1)S(1)} all-to-all(bf16[4,512,128]{2,1,0:T(8,128)(2,1)S(1)} %shard_map.181), channel_id=1, replica_groups=mesh['band'=128,'chan'=4] {'chan'}, dimensions={0} | all-to-all | bytes 1048576 | tf_op jit(solution)/shard_map/all_to_all | solution.py:274
  145.6 1.2 shard_map.182
  (73 shorter events, 9.9 us)
Async XLA Ops:
  0.0 7.6 %copy-start = (bf16[2,3,512,128]{3,2,1,0:T(8,128)(2,1)S(1)}, bf16[2,3,512,128]{3,2,1,0:T(8,128)(2,1)}, u32[]{:S(2)}) copy-start(bf16[2,3,512,128]{3,2,1,0:T(8,128)(2,1)} %w_proc.1) | copy-start | bytes 2359300
  0.0 0.9 copy-start.23
  0.9 0.8 copy-start.24
  2.6 5.0 %copy-start.14 = (bf16[512,128]{1,0:T(8,128)(2,1)S(1)}, bf16[512,128]{1,0:T(8,128)(2,1)}, u32[]{:S(2)}) copy-start(bf16[512,128]{1,0:T(8,128)(2,1)} %w_enc_out.1) | copy-start | bytes 393220
  2.6 5.0 %copy-start.25 = (bf16[128,227]{0,1:T(8,128)(2,1)S(1)}, bf16[128,227]{0,1:T(8,128)(2,1)}, u32[]{:S(2)}) copy-start(bf16[128,227]{0,1:T(8,128)(2,1)} %param.27) | copy-start | bytes 174340
  2.6 11.9 %all-to-all-start = ((bf16[4,512,128]{2,1,0:T(8,128)(2,1)}), bf16[4,512,128]{2,1,0:T(8,128)(2,1)S(1)}, u32[]{:S(2)}, u32[]{:S(2)}) async-start(bf16[4,512,128]{2,1,0:T(8,128)(2,1)} %shard_map.173), calls=%async_computation | async-start | bytes 1048576 | tf_op jit(solution)/shard_map/all_to_all | solution.py:274
  7.6 15.4 %copy-start.7 = (bf16[512,227]{0,1:T(8,128)(2,1)S(1)}, bf16[512,227]{0,1:T(8,128)(2,1)}, u32[]{:S(2)}) copy-start(bf16[512,227]{0,1:T(8,128)(2,1)} %param.18) | copy-start | bytes 697348
  7.6 15.4 %copy-start.8 = (bf16[512,128]{1,0:T(8,128)(2,1)S(1)}, bf16[512,128]{1,0:T(8,128)(2,1)}, u32[]{:S(2)}) copy-start(bf16[512,128]{1,0:T(8,128)(2,1)} %w_es.1) | copy-start | bytes 393220
  7.6 15.3 %copy-start.15 = (s32[5,512]{1,0:T(8,128)S(1)}, s32[5,512]{1,0:T(8,128)}, u32[]{:S(2)}) copy-start(s32[5,512]{1,0:T(8,128)} %enc_src.3) | copy-start | bytes 30724
  7.6 15.3 %copy-start.16 = (s32[5,512]{1,0:T(8,128)S(1)}, s32[5,512]{1,0:T(8,128)}, u32[]{:S(2)}) copy-start(s32[5,512]{1,0:T(8,128)} %enc_dst.3) | copy-start | bytes 30724
  7.6 15.3 %copy-start.26 = (s32[5,128]{1,0:T(8,128)S(1)}, s32[5,128]{1,0:T(8,128)}, u32[]{:S(2)}) copy-start(s32[5,128]{1,0:T(8,128)} %proc_src.5) | copy-start | bytes 7684
  7.6 15.3 %copy-start.27 = (s32[5,128]{1,0:T(8,128)S(1)}, s32[5,128]{1,0:T(8,128)}, u32[]{:S(2)}) copy-start(s32[5,128]{1,0:T(8,128)} %proc_dst.5) | copy-start | bytes 7684
  14.5 52.0 %collective-permute-start = (bf16[1792,128]{1,0:T(8,128)(2,1)S(1)}, bf16[1792,128]{1,0:T(8,128)(2,1)S(1)}, u32[]{:S(2)}, u32[]{:S(2)}) collective-permute-start(bf16[1792,128]{1,0:T(8,128)(2,1)S(1)} %shard_map.172.b0), channel_id=1, source_target_pairs={{0,1},{1,2},{2,3},{3,0},{4,5},{5,6},{6,7},{7,4},{8,9},{9,10},{10,1... | collective-permute-start | bytes 1376264 | tf_op jit(solution)/shard_map/ppermute | solution.py:308
  16.7 49.9 %collective-permute-start.1 = (bf16[1792,128]{1,0:T(8,128)(2,1)S(1)}, bf16[1792,128]{1,0:T(8,128)(2,1)S(1)}, u32[]{:S(2)}, u32[]{:S(2)}) collective-permute-start(bf16[1792,128]{1,0:T(8,128)(2,1)S(1)} %shard_map.172.b0), channel_id=1, source_target_pairs={{0,2},{1,3},{2,0},{3,1},{4,6},{5,7},{6,4},{7,5},{8,10},{9,11},{10,... | collective-permute-start | bytes 1376264 | tf_op jit(solution)/shard_map/ppermute | solution.py:308
  20.4 46.2 %collective-permute-start.2 = (bf16[1792,128]{1,0:T(8,128)(2,1)S(1)}, bf16[1792,128]{1,0:T(8,128)(2,1)S(1)}, u32[]{:S(2)}, u32[]{:S(2)}) collective-permute-start(bf16[1792,128]{1,0:T(8,128)(2,1)S(1)} %shard_map.172.b0), channel_id=1, source_target_pairs={{0,3},{1,0},{2,1},{3,2},{4,7},{5,4},{6,5},{7,6},{8,11},{9,8},{10,9... | collective-permute-start | bytes 1376264 | tf_op jit(solution)/shard_map/ppermute | solution.py:308
  23.0 0.9 copy-start.9
  23.9 0.9 copy-start.10
  24.8 0.7 copy-start.17
  27.3 0.8 copy-start.1
  28.1 9.8 %copy-start.12 = (bf16[512,128]{1,0:T(8,128)(2,1)}, bf16[512,128]{1,0:T(8,128)(2,1)S(1)}, u32[]{:S(2)}) copy-start(bf16[512,128]{1,0:T(8,128)(2,1)S(1)} %get-tuple-element.32.recv) | copy-start | bytes 393220
  56.8 9.7 %all-to-all-start.1 = ((bf16[4,256,128]{2,1,0:T(8,128)(2,1)}), bf16[4,256,128]{2,1,0:T(8,128)(2,1)S(1)}, u32[]{:S(2)}, u32[]{:S(2)}) async-start(bf16[4,256,128]{2,1,0:T(8,128)(2,1)} %copy-done.6), calls=%async_computation.1 | async-start | bytes 524288 | tf_op jit(solution)/shard_map/all_to_all | solution.py:274
  66.5 0.9 copy-start.4
  67.5 0.9 copy-start.5
  77.5 5.3 %copy-start.22 = (s32[4,8,128]{2,1,0:T(8,128)S(1)}, s32[4,8,128]{2,1,0:T(8,128)}, u32[]{:S(2)}) copy-start(s32[4,8,128]{2,1,0:T(8,128)} %copy-done.21) | copy-start | bytes 49156
  77.6 5.2 %copy-start.31 = (s32[1,1024]{1,0:T(1,128)S(1)}, s32[1,1024]{1,0:T(1,128)}, u32[]{:S(2)}) copy-start(s32[1,1024]{1,0:T(1,128)} %local_dst.3) | copy-start | bytes 12292
  84.7 9.0 %copy-start.3 = (bf16[512,128]{1,0:T(8,128)(2,1)S(1)}, bf16[512,128]{1,0:T(8,128)(2,1)}, u32[]{:S(2)}) copy-start(bf16[512,128]{1,0:T(8,128)(2,1)} %get-tuple-element.38.w_send) | copy-start | bytes 393220
  108.6 9.0 %copy-start.11 = (bf16[512,128]{1,0:T(8,128)(2,1)S(1)}, bf16[512,128]{1,0:T(8,128)(2,1)}, u32[]{:S(2)}) copy-start(bf16[512,128]{1,0:T(8,128)(2,1)} %w_send.1) | copy-start | bytes 393220
  126.0 5.4 %copy-start.18 = (s32[5,512]{1,0:T(8,128)S(1)}, s32[5,512]{1,0:T(8,128)}, u32[]{:S(2)}) copy-start(s32[5,512]{1,0:T(8,128)} %dec_src.3) | copy-start | bytes 30724
  126.0 5.4 %copy-start.20 = (s32[5,512]{1,0:T(8,128)S(1)}, s32[5,512]{1,0:T(8,128)}, u32[]{:S(2)}) copy-start(s32[5,512]{1,0:T(8,128)} %dec_dst.3) | copy-start | bytes 30724
  126.0 5.4 %copy-start.13 = (bf16[512,128]{1,0:T(8,128)(2,1)S(1)}, bf16[512,128]{1,0:T(8,128)(2,1)}, u32[]{:S(2)}) copy-start(bf16[512,128]{1,0:T(8,128)(2,1)} %copy-done.12) | copy-start | bytes 393220
  126.1 5.4 %copy-start.29 = (s32[2,4,8,128]{3,2,1,0:T(8,128)S(1)}, s32[2,4,8,128]{3,2,1,0:T(8,128)}, u32[]{:S(2)}) copy-start(s32[2,4,8,128]{3,2,1,0:T(8,128)} %copy-done.28) | copy-start | bytes 98308
  133.9 11.8 %copy-start.2 = (bf16[512,512]{1,0:T(8,128)(2,1)S(1)}, bf16[512,512]{1,0:T(8,128)(2,1)}, u32[]{:S(2)}) copy-start(bf16[512,512]{1,0:T(8,128)(2,1)} %copy-done.1) | copy-start | bytes 1572868
  (5 other events, 3.3 us)

commit v5 on v4

--- a/solution.py
+++ b/solution.py
@@ -87,8 +87,8 @@
     grid_latent = silu(dot_first(grid_state[...], wide(big, 0, channels))).astype(BF16)
     latent[...] = grid_latent
     grid_normed = rms(grid_latent).astype(BF16)
+    dec_recv[...] = dot(grid_normed, w_dd[...]).astype(BF16)
     payload[0:nodes, :] = dot(grid_normed, w_es[...]).astype(BF16)
-    dec_recv[...] = dot(grid_normed, w_dd[...]).astype(BF16)
     mesh_count = enc_recv.shape[0]
     mesh_normed = rms(wide(big, big.shape[1] - mesh_count, mesh_count)).astype(BF16)
     enc_recv[...] = dot(mesh_normed, w_ed[...]).astype(BF16)
@@ -134,10 +134,7 @@
     recv_count = recv.shape[0]
     send_count = pair.shape[1] - TABLES * TILE
     recv_t = transposed(recv[...])
-    total = add_edges(
-        None, transposed(pair[core, 0:send_count, :]), recv_t, enc_src[2:3, :], enc_dst[2:3, :],
-        send_count, recv_count,
-    )
+    arrivals = []
     for v, (kind, place, offset, second) in enumerate(places(core)):
         if kind == "two":
             block = two.at[core, place]
@@ -149,13 +146,20 @@
             decode(block[send_count + t * TILE : send_count + (t + 1) * TILE, :], offset, second)
             for t in range(TABLES)
         ]
+        arrivals.append((block, lists))
+        dec_tab[0, v] = lists[2]
+        dec_tab[1, v] = lists[3]
+        proc_tab[v] = lists[4]
+    total = None
+    for block, lists in arrivals:
         total = add_edges(
             total, transposed(block[0:send_count, :]), recv_t, flat(lists[0], 0, 4), flat(lists[1], 0, 4),
             send_count, recv_count,
         )
-        dec_tab[0, v] = lists[2]
-        dec_tab[1, v] = lists[3]
-        proc_tab[v] = lists[4]
+    total = add_edges(
+        total, transposed(pair[core, 0:send_count, :]), recv_t, enc_src[2:3, :], enc_dst[2:3, :],
+        send_count, recv_count,
+    )
     agg[...] = jnp.broadcast_to(total.T.astype(BF16)[None], agg.shape)
 
 
@@ -171,12 +175,21 @@
     return pl.ds(pl.multiple_of(source(k) * LANES, LANES), LANES)
 
 
-def early_kernel(w_in, mesh_latent, out):
-    channels = w_in.shape[0]
-    start = out.shape[1] - mesh_latent.shape[0]
-    for c in range(out.shape[0]):
-        out[c, 0:channels, :] = w_in[...]
-        out[c, start:, :] = mesh_latent[...]
+class Rows:
+    def __init__(self, ref, start):
+        self.ref, self.start = ref, start
+
+    def __getitem__(self, index):
+        rows, columns = index
+        return self.ref[self.start + rows.start : self.start + rows.stop, columns]
+
+
+def later_kernel(kernel, start, agg4, state, b0, b1, b2, b3, *rest):
+    kernel(agg4, state, *[Rows(b, start) for b in (b0, b1, b2, b3)], *rest)
+
+
+def layer_kernel(layer, agg4, state, b0, b1, b2, b3, w_proc, *rest):
+    node_kernel(True, agg4, state, b0, b1, b2, b3, w_proc.at[layer, 0], w_proc.at[layer, 1], *rest)
 
 
 def late_kernel(w_enc_out, w_proc, w_out, out):
@@ -187,7 +200,7 @@
     out[3 * depth : 3 * depth + w_out.shape[0], :] = w_out[...]
 
 
-def node_kernel(index, has_recv, agg4, state, b0, b1, b2, b3, w_send, *rest):
+def node_kernel(has_recv, agg4, state, b0, b1, b2, b3, w_send, *rest):
     if has_recv:
         w_recv, new_state, send, recv = rest
     else:
@@ -199,9 +212,8 @@
         before = jnp.concatenate([state[source(k), first:, :] for k in range(CHANS)], axis=1).astype(F32)
     else:
         before = state[...]
-    depth = agg.shape[1]
-    update = arrived((b0, b1, b2, b3), index * depth, depth)
-    after = before + dot(rms(agg).astype(BF16), update)
+    normed = rms(agg).astype(BF16)
+    after = before + dot(normed, arrived((b0, b1, b2, b3), 0, agg.shape[1]))
     normed = rms(after.astype(BF16)).astype(BF16)
 
     def turned(weight):
@@ -218,14 +230,15 @@
     sib = 1 - core
     count = recv.shape[0]
     recv_t = transposed(recv[...])
-    own_src = jnp.concatenate([local_src[...], proc_src[2:3, :]], axis=1)
-    own_dst = jnp.concatenate([local_dst[...], proc_dst[2:3, :]], axis=1)
-    total = add_edges(None, transposed(pair[core]), recv_t, own_src, own_dst, count, count)
+    total = None
     for v, block in enumerate((two.at[core, 0], two.at[core, 1], pair.at[sib], far.at[sib])):
         lists = tab[v]
         total = add_edges(
             total, transposed(block[...]), recv_t, lists[0:1, :], lists[1:2, :], count, count
         )
+    own_src = jnp.concatenate([local_src[...], proc_src[2:3, :]], axis=1)
+    own_dst = jnp.concatenate([local_dst[...], proc_dst[2:3, :]], axis=1)
+    total = add_edges(total, transposed(pair[core]), recv_t, own_src, own_dst, count, count)
     agg[...] = jnp.broadcast_to(total.T.astype(BF16)[None], agg.shape)
 
 
@@ -251,7 +264,7 @@
         [agg4[source(k)].astype(F32) + latent[:, columns_at(k)].astype(F32) for k in range(CHANS)], axis=1
     )
     normed = rms(combined).astype(BF16)
-    weights = arrived((b0, b1, b2, b3), 3 * normed.shape[1], out.shape[0])
+    weights = arrived((b0, b1, b2, b3), 0, out.shape[0])
     out[...] = dot_last(weights, normed).astype(BF16)
 
 
@@ -299,9 +312,10 @@
 
     channel_rows = -(-channels // LANES) * LANES
     late_rows = 3 * latent_width + channel_rows
-    big = exchange(call(
-        early_kernel, shape((chans, channel_rows + mesh_count, width)), w_in, mesh_latent
-    ))
+    parts = (jnp.pad(w_in, ((0, channel_rows - channels), (0, 0))), mesh_latent)
+    big = exchange(
+        jnp.concatenate([jnp.broadcast_to(part[None], (chans,) + part.shape) for part in parts], axis=1)
+    )
     late = call(late_kernel, shape((late_rows, width)), w_enc_out, w_proc, w_out.T)
     late, big = lax.optimization_barrier((late, big))
     blocks = [late] + [
@@ -328,25 +342,25 @@
     )
     state = big
     for layer in range(w_proc.shape[0]):
+        kernel = functools.partial(layer_kernel, layer)
         state, send, recv = call(
-            functools.partial(node_kernel, layer, True),
+            functools.partial(later_kernel, kernel, layer * latent_width),
             (shape((mesh_count, latent_width), F32), shape((mesh_count, width)), shape((mesh_count, width))),
-            exchange(agg), state, *blocks, w_proc[layer, 0], w_proc[layer, 1],
+            exchange(agg), state, *blocks, w_proc,
         )
         pair, two, far = around(send)
         agg = call(
-            proc_kernel, shape((chans, mesh_count, width)),
-            pair, two, far, recv, local_src, local_dst, proc_src, proc_dst, proc_tab,
-        )
-    send = call(
-        functools.partial(node_kernel, w_proc.shape[0], False), shape((mesh_count, width)),
-        exchange(agg), state, *blocks, w_dec_src,
-    )
+            proc_kernel, shape((chans, mesh_count, width)), pair, two, far, recv,
+            local_src, local_dst, proc_src, proc_dst, proc_tab,
+        )
+    node = functools.partial(later_kernel, functools.partial(node_kernel, False), 2 * latent_width)
+    send = call(node, shape((mesh_count, width)), exchange(agg), state, *blocks, w_dec_src)
     pair, two, far = around(send)
     agg = call(
         dec_kernel, shape((chans, grid_count, width)), pair, two, far, dec_recv, dec_src, dec_dst, dec_tab
     )
-    return call(out_kernel, shape((channels, grid_count)), exchange(agg), grid_latent, *blocks).T
+    last = functools.partial(later_kernel, out_kernel, 3 * latent_width)
+    return call(last, shape((channels, grid_count)), exchange(agg), grid_latent, *blocks).T
 
 
 def solution(mesh):

time: 148 us -> 139 us (0.939)
  blocking collectives: 94.6 us -> 104 us
  local copies, waits for them, and re-layouts: 10.4 us -> 2.47 us
  waiting for transfers between devices: 11.9 us -> 6.77 us
  starting transfers between devices: 17.3 us -> 13.4 us
    all_to_all x3 -> x4, blocking collectives: 29.7 us -> 38.9 us  [exchange(): return lax.all_to_all(copies, 'chan', 0, 0, tiled=True)]
    unnamed x64 -> x34, local copies, waits for them, and re-layouts: 9.66 us -> 1.56 us
    all_to_all x2 -> x1, waiting for transfers between devices: 11.9 us -> 6.76 us  [exchange(): return lax.all_to_all(copies, 'chan', 0, 0, tiled=True)]
    all_to_all x2 -> x1, starting transfers between devices: 8.88 us -> 4.97 us  [exchange(): return lax.all_to_all(copies, 'chan', 0, 0, tiled=True)]
    pallas_call x11 -> x10, Pallas kernels: 12.4 us -> 11 us  [call(): pl.pallas_call(kernel, out_shape=out_shapes, in_specs=[pl.BlockSpec(memor...]
  transfers between devices with their start and end apart: 5 -> 4, of which waited for: 2 -> 1; matrix products, arithmetic and copies ran while one was open for 1% -> 0% of each run, Pallas kernels for 2% -> 2%
where the time goes in v5:
time: 139 us; the launch traced here: 138 us
  blocking collectives  104 us (75%)
  starting transfers between devices  13.4 us (10%)
  Pallas kernels  11 us (8%)
  waiting for transfers between devices  6.77 us (5%)
  local copies, waits for them, and re-layouts  2.47 us (2%)
    all_gather x8, blocking collectives, core_gather(): lax.all_gather(block, 'band', axis_index_groups=[[s, s + 1] for s in rang...  41.9 us
    all_to_all x4, blocking collectives, exchange(): return lax.all_to_all(copies, 'chan', 0, 0, tiled=True)  38.9 us
    all_gather x4, blocking collectives, around(): two = lax.all_gather(pair, 'band', axis_index_groups=sides)  22.8 us
    pallas_call x10, Pallas kernels, call(): pl.pallas_call(kernel, out_shape=out_shapes, in_specs=[pl.BlockSpec(memor...  11 us
    ppermute x3, starting transfers between devices, on_device(): lax.ppermute(late, 'chan', [(s, (s + k) % chans) for s in range(chans)])  8.4 us
    all_to_all x1, waiting for transfers between devices, exchange(): return lax.all_to_all(copies, 'chan', 0, 0, tiled=True)  6.76 us
    all_to_all x1, starting transfers between devices, exchange(): return lax.all_to_all(copies, 'chan', 0, 0, tiled=True)  4.97 us
  transfers between devices with their start and end apart: 4, of which 1 were waited for; matrix products, arithmetic and copies ran while one was open for 0% of the time, Pallas kernels for 2%

profile of v5, /device:TPU:1, one launch (start us, length us, event | category | flops | bytes accessed | tf_op | source)
XLA Modules:
  0.0 138.5 jit_solution(11908257738241814958)
XLA Ops:
  0.0 0.8 pad.4
  0.9 0.8 copy-done.16
  1.7 0.8 pad_maximum_fusion
  2.6 5.0 %all-to-all-start = ((bf16[4,512,128]{2,1,0:T(8,128)(2,1)}), bf16[4,512,128]{2,1,0:T(8,128)(2,1)S(1)}, u32[]{:S(2)}, u32[]{:S(2)}) async-start(bf16[4,512,128]{2,1,0:T(8,128)(2,1)} %pad_maximum_fusion), calls=%async_computation | async-start | bytes 1048576 | tf_op jit(solution)/shard_map/all_to_all | solution.py:287
  7.7 6.8 %all-to-all-done.big.state = bf16[4,512,128]{2,1,0:T(8,128)(2,1)S(1)} async-done(((bf16[4,512,128]{2,1,0:T(8,128)(2,1)}), bf16[4,512,128]{2,1,0:T(8,128)(2,1)S(1)}, u32[]{:S(2)}, u32[]{:S(2)}) %all-to-all-start) | async-done | bytes 524320 | tf_op jit(solution)/shard_map/all_to_all | solution.py:287
  14.5 2.2 %collective-permute-start = (bf16[1792,128]{1,0:T(8,128)(2,1)S(1)}, bf16[1792,128]{1,0:T(8,128)(2,1)S(1)}, u32[]{:S(2)}, u32[]{:S(2)}) collective-permute-start(bf16[1792,128]{1,0:T(8,128)(2,1)S(1)} %shard_map.172.b0), channel_id=1, source_target_pairs={{0,1},{1,2},{2,3},{3,0},{4,5},{5,6},{6,7},{7,4},{8,9},{9,10},{10,1... | collective-permute-start | bytes 1376264 | tf_op jit(solution)/shard_map/ppermute | solution.py:322
  16.7 3.7 %collective-permute-start.1 = (bf16[1792,128]{1,0:T(8,128)(2,1)S(1)}, bf16[1792,128]{1,0:T(8,128)(2,1)S(1)}, u32[]{:S(2)}, u32[]{:S(2)}) collective-permute-start(bf16[1792,128]{1,0:T(8,128)(2,1)S(1)} %shard_map.172.b0), channel_id=1, source_target_pairs={{0,2},{1,3},{2,0},{3,1},{4,6},{5,7},{6,4},{7,5},{8,10},{9,11},{10,... | collective-permute-start | bytes 1376264 | tf_op jit(solution)/shard_map/ppermute | solution.py:322
  20.4 2.5 %collective-permute-start.2 = (bf16[1792,128]{1,0:T(8,128)(2,1)S(1)}, bf16[1792,128]{1,0:T(8,128)(2,1)S(1)}, u32[]{:S(2)}, u32[]{:S(2)}) collective-permute-start(bf16[1792,128]{1,0:T(8,128)(2,1)S(1)} %shard_map.172.b0), channel_id=1, source_target_pairs={{0,3},{1,0},{2,1},{3,2},{4,7},{5,4},{6,5},{7,6},{8,11},{9,8},{10,9... | collective-permute-start | bytes 1376264 | tf_op jit(solution)/shard_map/ppermute | solution.py:322
  23.0 1.1 shard_map.173
  24.1 9.8 %all-gather = bf16[1344,128]{1,0:T(8,128)(2,1)S(1)} all-gather(bf16[672,128]{1,0:T(8,128)(2,1)S(1)} %get-tuple-element.21), channel_id=2, replica_groups={{0,4},{8,12},{16,20},{24,28},{32,36},{40,44},{48,52},{56,60},{64,68},{7..., dimensions={0}, use_global_device_ids=true | all-gather | bytes 516096 | tf_op jit(solution)/shard_map/all_gather | solution.py:292
  33.9 7.6 %all-gather.1 = bf16[4,672,128]{2,1,0:T(8,128)(2,1)S(1)} all-gather(bf16[2,672,128]{2,1,0:T(8,128)(2,1)S(1)} %bitcast.17), channel_id=3, replica_groups={{4,8},{12,16},{20,24},{28,32},{36,40},{44,48},{52,56},{60,64},{68,72},{..., dimensions={0}, use_global_device_ids=true | all-gather | bytes 1032192 | tf_op jit(solution)/shard_map/all_gather | solution.py:299
  41.6 7.6 %all-gather.2 = bf16[2,1,672,128]{3,2,1,0:T(8,128)(2,1)S(1)} all-gather(bf16[1,1,672,128]{3,2,1,0:T(8,128)(2,1)S(1)} %slice_select_fusion), channel_id=4, replica_groups={{0,4},{8,12},{16,20},{24,28},{32,36},{40,44},{48,52},{56,60},{64,68},{7..., dimensions={0}, use_global_device_ids=true | all-gather | bytes 516096 | tf_op jit(solution)/shard_map/all_gather | solution.py:292
  49.2 1.6 %shard_map.174 = (bf16[4,256,128]{2,1,0:T(8,128)(2,1)S(1)}, s32[4,8,128]{2,1,0:T(8,128)S(1)}, s32[2,4,8,128]{3,2,1,0:T(8,128)S(1)}) custom-call(bf16[2,672,128]{2,1,0:T(8,128)(2,1)S(1)} %bitcast.18, bf16[2,2,672,128]{3,2,1,0:T(8,128)(2,1)S(1)} %bitcast.16, bf16[2,672,128]{2,1,0:T(8,128)(2,1)S(1)} %bitcast.25, bf16[256,128]{1,0:T(8,128)(2,1)S(1)} %get-tuple-element.22.recv, ...), custom_call_target="tpu_custom_call" | custom-call | tf_op jit(solution)/shard_map/pallas_call | solution.py:272
  50.8 9.5 %all_to_all.25.agg4 = bf16[4,256,128]{2,1,0:T(8,128)(2,1)S(1)} all-to-all(bf16[4,256,128]{2,1,0:T(8,128)(2,1)S(1)} %get-tuple-element.23), channel_id=1, replica_groups=mesh['band'=128,'chan'=4] {'chan'}, dimensions={0} | all-to-all | bytes 524288 | tf_op jit(solution)/shard_map/all_to_all | solution.py:287
  60.4 0.8 shard_map.175
  61.1 3.4 %all-gather.3 = bf16[512,128]{1,0:T(8,128)(2,1)S(1)} all-gather(bf16[256,128]{1,0:T(8,128)(2,1)S(1)} %get-tuple-element.25), channel_id=5, replica_groups={{0,4},{8,12},{16,20},{24,28},{32,36},{40,44},{48,52},{56,60},{64,68},{7..., dimensions={0}, use_global_device_ids=true | all-gather | bytes 196608 | tf_op jit(solution)/shard_map/all_gather | solution.py:292
  64.5 5.1 %all-gather.4 = bf16[4,256,128]{2,1,0:T(8,128)(2,1)S(1)} all-gather(bf16[2,256,128]{2,1,0:T(8,128)(2,1)S(1)} %bitcast.30), channel_id=6, replica_groups={{4,8},{12,16},{20,24},{28,32},{36,40},{44,48},{52,56},{60,64},{68,72},{..., dimensions={0}, use_global_device_ids=true | all-gather | bytes 393216 | tf_op jit(solution)/shard_map/all_gather | solution.py:299
  69.6 5.2 %all-gather.5 = bf16[2,1,256,128]{3,2,1,0:T(8,128)(2,1)S(1)} all-gather(bf16[1,1,256,128]{3,2,1,0:T(8,128)(2,1)S(1)} %slice_select_fusion.3), channel_id=7, replica_groups={{0,4},{8,12},{16,20},{24,28},{32,36},{40,44},{48,52},{56,60},{64,68},{7..., dimensions={0}, use_global_device_ids=true | all-gather | bytes 196608 | tf_op jit(solution)/shard_map/all_gather | solution.py:292
  75.5 1.2 shard_map.176
  76.7 8.8 %all_to_all.26.agg4 = bf16[4,256,128]{2,1,0:T(8,128)(2,1)S(1)} all-to-all(bf16[4,256,128]{2,1,0:T(8,128)(2,1)S(1)} %shard_map.176), channel_id=1, replica_groups=mesh['band'=128,'chan'=4] {'chan'}, dimensions={0} | all-to-all | bytes 524288 | tf_op jit(solution)/shard_map/all_to_all | solution.py:287
  85.5 0.7 shard_map.177
  86.3 2.7 %all-gather.6 = bf16[512,128]{1,0:T(8,128)(2,1)S(1)} all-gather(bf16[256,128]{1,0:T(8,128)(2,1)S(1)} %get-tuple-element.29), channel_id=8, replica_groups={{0,4},{8,12},{16,20},{24,28},{32,36},{40,44},{48,52},{56,60},{64,68},{7..., dimensions={0}, use_global_device_ids=true | all-gather | bytes 196608 | tf_op jit(solution)/shard_map/all_gather | solution.py:292
  89.0 5.1 %all-gather.7 = bf16[4,256,128]{2,1,0:T(8,128)(2,1)S(1)} all-gather(bf16[2,256,128]{2,1,0:T(8,128)(2,1)S(1)} %bitcast.28), channel_id=9, replica_groups={{4,8},{12,16},{20,24},{28,32},{36,40},{44,48},{52,56},{60,64},{68,72},{..., dimensions={0}, use_global_device_ids=true | all-gather | bytes 393216 | tf_op jit(solution)/shard_map/all_gather | solution.py:299
  94.1 5.2 %all-gather.8 = bf16[2,1,256,128]{3,2,1,0:T(8,128)(2,1)S(1)} all-gather(bf16[1,1,256,128]{3,2,1,0:T(8,128)(2,1)S(1)} %slice_select_fusion.2), channel_id=10, replica_groups={{0,4},{8,12},{16,20},{24,28},{32,36},{40,44},{48,52},{56,60},{64,68},{7..., dimensions={0}, use_global_device_ids=true | all-gather | bytes 196608 | tf_op jit(solution)/shard_map/all_gather | solution.py:292
  99.3 1.2 shard_map.178
  100.5 9.0 %all_to_all.27.agg4 = bf16[4,256,128]{2,1,0:T(8,128)(2,1)S(1)} all-to-all(bf16[4,256,128]{2,1,0:T(8,128)(2,1)S(1)} %shard_map.178), channel_id=1, replica_groups=mesh['band'=128,'chan'=4] {'chan'}, dimensions={0} | all-to-all | bytes 524288 | tf_op jit(solution)/shard_map/all_to_all | solution.py:287
  110.2 2.7 %all-gather.9 = bf16[512,128]{1,0:T(8,128)(2,1)S(1)} all-gather(bf16[256,128]{1,0:T(8,128)(2,1)S(1)} %shard_map.179), channel_id=11, replica_groups={{0,4},{8,12},{16,20},{24,28},{32,36},{40,44},{48,52},{56,60},{64,68},{7..., dimensions={0}, use_global_device_ids=true | all-gather | bytes 196608 | tf_op jit(solution)/shard_map/all_gather | solution.py:292
  112.9 5.1 %all-gather.10 = bf16[4,256,128]{2,1,0:T(8,128)(2,1)S(1)} all-gather(bf16[2,256,128]{2,1,0:T(8,128)(2,1)S(1)} %bitcast.26), channel_id=12, replica_groups={{4,8},{12,16},{20,24},{28,32},{36,40},{44,48},{52,56},{60,64},{68,72},{..., dimensions={0}, use_global_device_ids=true | all-gather | bytes 393216 | tf_op jit(solution)/shard_map/all_gather | solution.py:299
  118.0 5.2 %all-gather.11 = bf16[2,1,256,128]{3,2,1,0:T(8,128)(2,1)S(1)} all-gather(bf16[1,1,256,128]{3,2,1,0:T(8,128)(2,1)S(1)} %slice_select_fusion.1), channel_id=13, replica_groups={{0,4},{8,12},{16,20},{24,28},{32,36},{40,44},{48,52},{56,60},{64,68},{7..., dimensions={0}, use_global_device_ids=true | all-gather | bytes 196608 | tf_op jit(solution)/shard_map/all_gather | solution.py:292
  123.2 2.4 %shard_map.180 = bf16[4,512,128]{2,1,0:T(8,128)(2,1)S(1)} custom-call(bf16[2,256,128]{2,1,0:T(8,128)(2,1)S(1)} %bitcast.27, bf16[2,2,256,128]{3,2,1,0:T(8,128)(2,1)S(1)} %bitcast.20, bf16[2,256,128]{2,1,0:T(8,128)(2,1)S(1)} %bitcast.32, bf16[512,128]{1,0:T(8,128)(2,1)S(1)} %get-tuple-element.32.recv, s32[5,512]{1,0:T(8,128)S(1)} %copy-done.9, ...), custom_call_target="tpu_custom_call" | custom-call | tf_op jit(solution)/shard_map/pallas_call | solution.py:272
  125.6 11.6 %all_to_all.28.agg4 = bf16[4,512,128]{2,1,0:T(8,128)(2,1)S(1)} all-to-all(bf16[4,512,128]{2,1,0:T(8,128)(2,1)S(1)} %shard_map.180), channel_id=1, replica_groups=mesh['band'=128,'chan'=4] {'chan'}, dimensions={0} | all-to-all | bytes 1048576 | tf_op jit(solution)/shard_map/all_to_all | solution.py:287
  137.3 1.2 shard_map.181
  (44 shorter events, 1.6 us)
Async XLA Ops:
  0.8 0.8 copy-start.16
  2.6 5.0 %copy-start = (bf16[2,3,512,128]{3,2,1,0:T(8,128)(2,1)S(1)}, bf16[2,3,512,128]{3,2,1,0:T(8,128)(2,1)}, u32[]{:S(2)}) copy-start(bf16[2,3,512,128]{3,2,1,0:T(8,128)(2,1)} %rest_0_.4) | copy-start | bytes 2359300
  2.6 5.0 %copy-start.6 = (bf16[512,128]{1,0:T(8,128)(2,1)S(1)}, bf16[512,128]{1,0:T(8,128)(2,1)}, u32[]{:S(2)}) copy-start(bf16[512,128]{1,0:T(8,128)(2,1)} %w_enc_out.1) | copy-start | bytes 393220
  2.6 5.0 %copy-start.11 = (bf16[128,227]{0,1:T(8,128)(2,1)S(1)}, bf16[128,227]{0,1:T(8,128)(2,1)}, u32[]{:S(2)}) copy-start(bf16[128,227]{0,1:T(8,128)(2,1)} %param.27) | copy-start | bytes 174340
  2.6 11.9 %all-to-all-start = ((bf16[4,512,128]{2,1,0:T(8,128)(2,1)}), bf16[4,512,128]{2,1,0:T(8,128)(2,1)S(1)}, u32[]{:S(2)}, u32[]{:S(2)}) async-start(bf16[4,512,128]{2,1,0:T(8,128)(2,1)} %pad_maximum_fusion), calls=%async_computation | async-start | bytes 1048576 | tf_op jit(solution)/shard_map/all_to_all | solution.py:287
  7.5 15.4 %copy-start.1 = (bf16[512,227]{0,1:T(8,128)(2,1)S(1)}, bf16[512,227]{0,1:T(8,128)(2,1)}, u32[]{:S(2)}) copy-start(bf16[512,227]{0,1:T(8,128)(2,1)} %param.18) | copy-start | bytes 697348
  7.6 15.4 %copy-start.2 = (bf16[512,128]{1,0:T(8,128)(2,1)S(1)}, bf16[512,128]{1,0:T(8,128)(2,1)}, u32[]{:S(2)}) copy-start(bf16[512,128]{1,0:T(8,128)(2,1)} %w_es.1) | copy-start | bytes 393220
  7.6 15.3 %copy-start.3 = (bf16[512,128]{1,0:T(8,128)(2,1)S(1)}, bf16[512,128]{1,0:T(8,128)(2,1)}, u32[]{:S(2)}) copy-start(bf16[512,128]{1,0:T(8,128)(2,1)} %w_ed.1) | copy-start | bytes 393220
  7.6 15.3 %copy-start.4 = (bf16[512,128]{1,0:T(8,128)(2,1)S(1)}, bf16[512,128]{1,0:T(8,128)(2,1)}, u32[]{:S(2)}) copy-start(bf16[512,128]{1,0:T(8,128)(2,1)} %w_dd.1) | copy-start | bytes 393220
  7.6 15.3 %copy-start.7 = (s32[5,512]{1,0:T(8,128)S(1)}, s32[5,512]{1,0:T(8,128)}, u32[]{:S(2)}) copy-start(s32[5,512]{1,0:T(8,128)} %enc_src.3) | copy-start | bytes 30724
  7.6 15.3 %copy-start.8 = (s32[5,512]{1,0:T(8,128)S(1)}, s32[5,512]{1,0:T(8,128)}, u32[]{:S(2)}) copy-start(s32[5,512]{1,0:T(8,128)} %enc_dst.3) | copy-start | bytes 30724
  7.6 15.3 %copy-start.9 = (s32[5,512]{1,0:T(8,128)S(1)}, s32[5,512]{1,0:T(8,128)}, u32[]{:S(2)}) copy-start(s32[5,512]{1,0:T(8,128)} %dec_src.3) | copy-start | bytes 30724
  7.6 15.3 %copy-start.10 = (s32[5,512]{1,0:T(8,128)S(1)}, s32[5,512]{1,0:T(8,128)}, u32[]{:S(2)}) copy-start(s32[5,512]{1,0:T(8,128)} %dec_dst.3) | copy-start | bytes 30724
  7.6 15.3 %copy-start.12 = (s32[5,128]{1,0:T(8,128)S(1)}, s32[5,128]{1,0:T(8,128)}, u32[]{:S(2)}) copy-start(s32[5,128]{1,0:T(8,128)} %proc_src.5) | copy-start | bytes 7684
  7.7 15.3 %copy-start.13 = (s32[5,128]{1,0:T(8,128)S(1)}, s32[5,128]{1,0:T(8,128)}, u32[]{:S(2)}) copy-start(s32[5,128]{1,0:T(8,128)} %proc_dst.5) | copy-start | bytes 7684
  14.5 45.9 %collective-permute-start = (bf16[1792,128]{1,0:T(8,128)(2,1)S(1)}, bf16[1792,128]{1,0:T(8,128)(2,1)S(1)}, u32[]{:S(2)}, u32[]{:S(2)}) collective-permute-start(bf16[1792,128]{1,0:T(8,128)(2,1)S(1)} %shard_map.172.b0), channel_id=1, source_target_pairs={{0,1},{1,2},{2,3},{3,0},{4,5},{5,6},{6,7},{7,4},{8,9},{9,10},{10,1... | collective-permute-start | bytes 1376264 | tf_op jit(solution)/shard_map/ppermute | solution.py:322
  16.7 43.7 %collective-permute-start.1 = (bf16[1792,128]{1,0:T(8,128)(2,1)S(1)}, bf16[1792,128]{1,0:T(8,128)(2,1)S(1)}, u32[]{:S(2)}, u32[]{:S(2)}) collective-permute-start(bf16[1792,128]{1,0:T(8,128)(2,1)S(1)} %shard_map.172.b0), channel_id=1, source_target_pairs={{0,2},{1,3},{2,0},{3,1},{4,6},{5,7},{6,4},{7,5},{8,10},{9,11},{10,... | collective-permute-start | bytes 1376264 | tf_op jit(solution)/shard_map/ppermute | solution.py:322
  20.4 40.0 %collective-permute-start.2 = (bf16[1792,128]{1,0:T(8,128)(2,1)S(1)}, bf16[1792,128]{1,0:T(8,128)(2,1)S(1)}, u32[]{:S(2)}, u32[]{:S(2)}) collective-permute-start(bf16[1792,128]{1,0:T(8,128)(2,1)S(1)} %shard_map.172.b0), channel_id=1, source_target_pairs={{0,3},{1,0},{2,1},{3,2},{4,7},{5,4},{6,5},{7,6},{8,11},{9,8},{10,9... | collective-permute-start | bytes 1376264 | tf_op jit(solution)/shard_map/ppermute | solution.py:322
  69.6 5.2 %copy-start.15 = (s32[1,1024]{1,0:T(1,128)S(1)}, s32[1,1024]{1,0:T(1,128)}, u32[]{:S(2)}) copy-start(s32[1,1024]{1,0:T(1,128)} %local_dst.3) | copy-start | bytes 12292
  74.8 0.7 copy-start.14
  100.5 9.0 %copy-start.5 = (bf16[512,128]{1,0:T(8,128)(2,1)S(1)}, bf16[512,128]{1,0:T(8,128)(2,1)}, u32[]{:S(2)}) copy-start(bf16[512,128]{1,0:T(8,128)(2,1)} %rest_0_.5) | copy-start | bytes 393220

commit v6 on v5

--- a/solution.py
+++ b/solution.py
@@ -14,7 +14,7 @@
 LANES = 128
 CHANS = 4
 TILE = 32
-TABLES = 5
+TABLES = 3
 
 
 def rms(values):
@@ -47,8 +47,9 @@
 
 
 def one_hot(row, count):
-    nodes = lax.broadcasted_iota(I32, (count, row.shape[1]), 0)
-    return jnp.where(nodes == row, 1.0, 0.0).astype(BF16)
+    nodes = lax.broadcasted_iota(I32, (count, row.shape[1]), 0).astype(jnp.int16)
+    hit = nodes == row.astype(jnp.int16)
+    return jnp.where(hit, jnp.ones((), BF16), jnp.zeros((), BF16))
 
 
 def code_table(digits, table, core, rows_used):
@@ -79,23 +80,23 @@
 
 
 def pre_kernel(
-    grid_state, big, w_es, w_ed, w_dd, enc_src, enc_dst, dec_src, dec_dst, proc_src, proc_dst,
+    grid_state, big, w_es, w_ed, w_dd, enc_src, enc_dst, proc_src, proc_dst,
     payload, enc_recv, dec_recv, latent, digits,
 ):
     core = core_index()
     channels, nodes = grid_state.shape
-    grid_latent = silu(dot_first(grid_state[...], wide(big, 0, channels))).astype(BF16)
+    grid_latent = silu(dot_first(grid_state[...], wide(big, enc_recv.shape[0], channels))).astype(BF16)
     latent[...] = grid_latent
     grid_normed = rms(grid_latent).astype(BF16)
     dec_recv[...] = dot(grid_normed, w_dd[...]).astype(BF16)
     payload[0:nodes, :] = dot(grid_normed, w_es[...]).astype(BF16)
     mesh_count = enc_recv.shape[0]
-    mesh_normed = rms(wide(big, big.shape[1] - mesh_count, mesh_count)).astype(BF16)
+    mesh_normed = rms(wide(big, 0, mesh_count)).astype(BF16)
     enc_recv[...] = dot(mesh_normed, w_ed[...]).astype(BF16)
-    for t, table in enumerate((enc_src, enc_dst, dec_src, dec_dst)):
+    for t, table in enumerate((enc_src, enc_dst)):
         start = nodes + t * TILE
         payload[start : start + TILE, :] = code_table(digits, table, core, 0).astype(BF16)
-    start = nodes + 4 * TILE
+    start = nodes + 2 * TILE
     both = code_table(digits, proc_src, core, 0) + code_table(digits, proc_dst, core, 1)
     payload[start : start + TILE, :] = both.astype(BF16)
 
@@ -111,13 +112,13 @@
     return jnp.concatenate([rows[start + k : start + k + 1, :] for k in range(count)], axis=1)
 
 
-def places(core):
+def places(pair, two, far, core):
     sib = 1 - core
     return (
-        ("two", 0, core * 16, 1),
-        ("two", 1, 16 - core * 16, 0),
-        ("pair", sib, 0, sib),
-        ("far", core, 16, core),
+        (two.at[core, 0], core * 16, 1),
+        (two.at[core, 1], 16 - core * 16, 0),
+        (pair.at[sib], 0, sib),
+        (far.at[sib], 16, core),
     )
 
 
@@ -127,29 +128,20 @@
 
 def enc_kernel(
     pair, two, far, recv, enc_src, enc_dst,
-    agg, proc_tab, dec_tab,
+    agg, proc_tab,
 ):
     core = core_index()
-    sib = 1 - core
     recv_count = recv.shape[0]
     send_count = pair.shape[1] - TABLES * TILE
     recv_t = transposed(recv[...])
     arrivals = []
-    for v, (kind, place, offset, second) in enumerate(places(core)):
-        if kind == "two":
-            block = two.at[core, place]
-        elif kind == "pair":
-            block = pair.at[sib]
-        else:
-            block = far.at[sib]
+    for v, (block, offset, second) in enumerate(places(pair, two, far, core)):
         lists = [
             decode(block[send_count + t * TILE : send_count + (t + 1) * TILE, :], offset, second)
             for t in range(TABLES)
         ]
         arrivals.append((block, lists))
-        dec_tab[0, v] = lists[2]
-        dec_tab[1, v] = lists[3]
-        proc_tab[v] = lists[4]
+        proc_tab[v] = lists[2]
     total = None
     for block, lists in arrivals:
         total = add_edges(
@@ -192,7 +184,8 @@
     node_kernel(True, agg4, state, b0, b1, b2, b3, w_proc.at[layer, 0], w_proc.at[layer, 1], *rest)
 
 
-def late_kernel(w_enc_out, w_proc, w_out, out):
+def late_kernel(w_enc_out, w_proc, w_out, *rest):
+    out = rest[-1]
     depth = w_enc_out.shape[0]
     out[0:depth, :] = w_enc_out[...]
     out[depth : 2 * depth, :] = w_proc[0, 2]
@@ -204,12 +197,15 @@
     if has_recv:
         w_recv, new_state, send, recv = rest
     else:
-        (send,) = rest
+        dec_src, dec_dst, send, digits = rest
+        core = core_index()
+        for t, table in enumerate((dec_src, dec_dst)):
+            start = send.shape[0] - (2 - t) * TILE
+            send[start : start + TILE, :] = code_table(digits, table, core, 0).astype(BF16)
     count = agg4.shape[1]
     agg = wide(agg4, 0, count)
     if len(state.shape) == 3:
-        first = state.shape[1] - count
-        before = jnp.concatenate([state[source(k), first:, :] for k in range(CHANS)], axis=1).astype(F32)
+        before = jnp.concatenate([state[source(k), 0:count, :] for k in range(CHANS)], axis=1).astype(F32)
     else:
         before = state[...]
     normed = rms(agg).astype(BF16)
@@ -219,7 +215,7 @@
     def turned(weight):
         return jnp.concatenate([weight[columns_at(k), :] for k in range(CHANS)], axis=0)
 
-    send[...] = dot(normed, turned(w_send)).astype(BF16)
+    send[0:count, :] = dot(normed, turned(w_send)).astype(BF16)
     if has_recv:
         new_state[...] = after
         recv[...] = dot(normed, turned(w_recv)).astype(BF16)
@@ -242,19 +238,22 @@
     agg[...] = jnp.broadcast_to(total.T.astype(BF16)[None], agg.shape)
 
 
-def dec_kernel(pair, two, far, recv, dec_src, dec_dst, tab, agg):
+def dec_kernel(pair, two, far, recv, dec_src, dec_dst, agg):
     core = core_index()
-    sib = 1 - core
     recv_count = recv.shape[0]
-    send_count = pair.shape[1]
+    send_count = pair.shape[1] - 2 * TILE
     recv_t = transposed(recv[...])
     total = add_edges(
-        None, transposed(pair[core]), recv_t, dec_src[2:3, :], dec_dst[2:3, :], send_count, recv_count
-    )
-    for v, block in enumerate((two.at[core, 0], two.at[core, 1], pair.at[sib], far.at[sib])):
+        None, transposed(pair[core, 0:send_count, :]), recv_t, dec_src[2:3, :], dec_dst[2:3, :],
+        send_count, recv_count,
+    )
+    for block, offset, second in places(pair, two, far, core):
+        src, dst = [
+            flat(decode(block[start : start + TILE, :], offset, second), 0, 4)
+            for start in (send_count, send_count + TILE)
+        ]
         total = add_edges(
-            total, transposed(block[...]), recv_t, flat(tab[0, v], 0, 4), flat(tab[1, v], 0, 4),
-            send_count, recv_count,
+            total, transposed(block[0:send_count, :]), recv_t, src, dst, send_count, recv_count
         )
     agg[...] = jnp.broadcast_to(total.T.astype(BF16)[None], agg.shape)
 
@@ -312,12 +311,13 @@
 
     channel_rows = -(-channels // LANES) * LANES
     late_rows = 3 * latent_width + channel_rows
-    parts = (jnp.pad(w_in, ((0, channel_rows - channels), (0, 0))), mesh_latent)
-    big = exchange(
-        jnp.concatenate([jnp.broadcast_to(part[None], (chans,) + part.shape) for part in parts], axis=1)
-    )
-    late = call(late_kernel, shape((late_rows, width)), w_enc_out, w_proc, w_out.T)
-    late, big = lax.optimization_barrier((late, big))
+    early = jnp.concatenate(
+        [jnp.broadcast_to(part[None], (chans,) + part.shape) for part in (mesh_latent, w_in)], axis=1
+    )
+    early, w_enc_out = lax.optimization_barrier((early, w_enc_out))
+    big = exchange(early)
+    soon = (grid_state.T, w_enc_src, w_enc_dst, w_dec_dst, enc_src, enc_dst, proc_src, proc_dst)
+    late = call(late_kernel, shape((late_rows, width)), w_enc_out, w_proc, w_out.T, *soon)
     blocks = [late] + [
         lax.ppermute(late, "chan", [(s, (s + k) % chans) for s in range(chans)]) for k in range(1, chans)
     ]
@@ -330,16 +330,16 @@
             shape((grid_count, width)),
             shape((grid_count, latent_width)),
         ),
-        grid_state.T, big, w_enc_src, w_enc_dst, w_dec_dst,
-        enc_src, enc_dst, dec_src, dec_dst, proc_src, proc_dst,
+        soon[0], big, *soon[1:],
         scratch=[pltpu.VMEM((16, enc_src.shape[1]), F32)],
     )
     pair, two, far = around(payload)
-    agg, proc_tab, dec_tab = call(
+    agg, proc_tab = call(
         enc_kernel,
-        (shape((chans, mesh_count, width)), shape((4, 8, LANES), I32), shape((2, 4, 8, LANES), I32)),
+        (shape((chans, mesh_count, width)), shape((4, 8, LANES), I32)),
         pair, two, far, recv, enc_src, enc_dst,
     )
+    agg, *blocks = lax.optimization_barrier((agg, *blocks))
     state = big
     for layer in range(w_proc.shape[0]):
         kernel = functools.partial(layer_kernel, layer)
@@ -354,10 +354,14 @@
             local_src, local_dst, proc_src, proc_dst, proc_tab,
         )
     node = functools.partial(later_kernel, functools.partial(node_kernel, False), 2 * latent_width)
-    send = call(node, shape((mesh_count, width)), exchange(agg), state, *blocks, w_dec_src)
+    send = call(
+        node, shape((mesh_count + 2 * TILE, width)),
+        exchange(agg), state, *blocks, w_dec_src, dec_src, dec_dst,
+        scratch=[pltpu.VMEM((16, dec_src.shape[1]), F32)],
+    )
     pair, two, far = around(send)
     agg = call(
-        dec_kernel, shape((chans, grid_count, width)), pair, two, far, dec_recv, dec_src, dec_dst, dec_tab
+        dec_kernel, shape((chans, grid_count, width)), pair, two, far, dec_recv, dec_src, dec_dst
     )
     last = functools.partial(later_kernel, out_kernel, 3 * latent_width)
     return call(last, shape((channels, grid_count)), exchange(agg), grid_latent, *blocks).T

time: 139 us -> 132 us (0.950)
  waiting for transfers between devices: 6.77 us -> 0.01 us
  blocking collectives: 104 us -> 100 us
  starting transfers between devices: 13.4 us -> 15.8 us
    all_to_all x1, waiting for transfers between devices: 6.76 us -> 0.01 us  [exchange(): return lax.all_to_all(copies, 'chan', 0, 0, tiled=True)]
    all_gather x8, blocking collectives: 41.9 us -> 39 us  [core_gather(): lax.all_gather(block, 'band', axis_index_groups=[[s, s + 1] for s in rang...]
    ppermute x3, starting transfers between devices: 8.4 us -> 10.8 us  [on_device(): lax.ppermute(late, 'chan', [(s, (s + k) % chans) for s in range(chans)])]
  transfers between devices with their start and end apart: 4 -> 4, of which waited for: 1 -> 0; matrix products, arithmetic and copies ran while one was open for 0% -> 0% of each run, Pallas kernels for 2% -> 2%
where the time goes in v6:
time: 132 us; the launch traced here: 131 us
  blocking collectives  100 us (76%)
  starting transfers between devices  15.8 us (12%)
  Pallas kernels  10.7 us (8%)
  local copies, waits for them, and re-layouts  3.49 us (3%)
    all_gather x8, blocking collectives, core_gather(): lax.all_gather(block, 'band', axis_index_groups=[[s, s + 1] for s in rang...  39 us
    all_to_all x4, blocking collectives, exchange(): return lax.all_to_all(copies, 'chan', 0, 0, tiled=True)  38.2 us
    all_gather x4, blocking collectives, around(): two = lax.all_gather(pair, 'band', axis_index_groups=sides)  23.1 us
    ppermute x3, starting transfers between devices, on_device(): lax.ppermute(late, 'chan', [(s, (s + k) % chans) for s in range(chans)])  10.8 us
    pallas_call x10, Pallas kernels, call(): pl.pallas_call(kernel, out_shape=out_shapes, in_specs=[pl.BlockSpec(memor...  10.7 us
    all_to_all x1, starting transfers between devices, exchange(): return lax.all_to_all(copies, 'chan', 0, 0, tiled=True)  4.99 us
  transfers between devices with their start and end apart: 4, of which 0 were waited for; matrix products, arithmetic and copies ran while one was open for 0% of the time, Pallas kernels for 2%

profile of v6, /device:TPU:1, one launch (start us, length us, event | category | flops | bytes accessed | tf_op | source)
XLA Modules:
  0.0 131.5 jit_solution(2467948846970004988)
XLA Ops:
  0.0 0.9 broadcast_in_dim.4
  0.9 0.8 pad_maximum_fusion
  1.9 5.0 %all-to-all-start = ((bf16[4,483,128]{2,1,0:T(8,128)(2,1)}), bf16[4,483,128]{2,1,0:T(8,128)(2,1)S(1)}, u32[]{:S(2)}, u32[]{:S(2)}) async-start(bf16[4,483,128]{2,1,0:T(8,128)(2,1)} %pad_maximum_fusion), calls=%async_computation | async-start | bytes 999424 | tf_op jit(solution)/shard_map/all_to_all | solution.py:286
  7.0 3.4 %collective-permute-start = (bf16[1792,128]{1,0:T(8,128)(2,1)S(1)}, bf16[1792,128]{1,0:T(8,128)(2,1)S(1)}, u32[]{:S(2)}, u32[]{:S(2)}) collective-permute-start(bf16[1792,128]{1,0:T(8,128)(2,1)S(1)} %shard_map.174.b0), channel_id=1, source_target_pairs={{0,1},{1,2},{2,3},{3,0},{4,5},{5,6},{6,7},{7,4},{8,9},{9,10},{10,1... | collective-permute-start | bytes 1376264 | tf_op jit(solution)/shard_map/ppermute | solution.py:322
  10.4 4.3 %collective-permute-start.1 = (bf16[1792,128]{1,0:T(8,128)(2,1)S(1)}, bf16[1792,128]{1,0:T(8,128)(2,1)S(1)}, u32[]{:S(2)}, u32[]{:S(2)}) collective-permute-start(bf16[1792,128]{1,0:T(8,128)(2,1)S(1)} %shard_map.174.b0), channel_id=1, source_target_pairs={{0,2},{1,3},{2,0},{3,1},{4,6},{5,7},{6,4},{7,5},{8,10},{9,11},{10,... | collective-permute-start | bytes 1376264 | tf_op jit(solution)/shard_map/ppermute | solution.py:322
  14.7 3.1 %collective-permute-start.2 = (bf16[1792,128]{1,0:T(8,128)(2,1)S(1)}, bf16[1792,128]{1,0:T(8,128)(2,1)S(1)}, u32[]{:S(2)}, u32[]{:S(2)}) collective-permute-start(bf16[1792,128]{1,0:T(8,128)(2,1)S(1)} %shard_map.174.b0), channel_id=1, source_target_pairs={{0,3},{1,0},{2,1},{3,2},{4,7},{5,4},{6,5},{7,6},{8,11},{9,8},{10,9... | collective-permute-start | bytes 1376264 | tf_op jit(solution)/shard_map/ppermute | solution.py:322
  17.8 0.9 copy-done.4
  18.7 0.9 copy-done.6
  19.6 1.0 shard_map.172
  20.6 8.3 %all-gather = bf16[1216,128]{1,0:T(8,128)(2,1)S(1)} all-gather(bf16[608,128]{1,0:T(8,128)(2,1)S(1)} %get-tuple-element.25), channel_id=2, replica_groups={{0,4},{8,12},{16,20},{24,28},{32,36},{40,44},{48,52},{56,60},{64,68},{7..., dimensions={0}, use_global_device_ids=true | all-gather | bytes 466944 | tf_op jit(solution)/shard_map/all_gather | solution.py:291
  28.9 7.3 %all-gather.1 = bf16[4,608,128]{2,1,0:T(8,128)(2,1)S(1)} all-gather(bf16[2,608,128]{2,1,0:T(8,128)(2,1)S(1)} %bitcast.17), channel_id=3, replica_groups={{4,8},{12,16},{20,24},{28,32},{36,40},{44,48},{52,56},{60,64},{68,72},{..., dimensions={0}, use_global_device_ids=true | all-gather | bytes 933888 | tf_op jit(solution)/shard_map/all_gather | solution.py:298
  36.2 7.2 %all-gather.2 = bf16[2,1,608,128]{3,2,1,0:T(8,128)(2,1)S(1)} all-gather(bf16[1,1,608,128]{3,2,1,0:T(8,128)(2,1)S(1)} %slice_select_fusion), channel_id=4, replica_groups={{0,4},{8,12},{16,20},{24,28},{32,36},{40,44},{48,52},{56,60},{64,68},{7..., dimensions={0}, use_global_device_ids=true | all-gather | bytes 466944 | tf_op jit(solution)/shard_map/all_gather | solution.py:291
  43.4 1.4 %shard_map.173 = (bf16[4,256,128]{2,1,0:T(8,128)(2,1)S(1)}, s32[4,8,128]{2,1,0:T(8,128)S(1)}) custom-call(bf16[2,608,128]{2,1,0:T(8,128)(2,1)S(1)} %bitcast.18, bf16[2,2,608,128]{3,2,1,0:T(8,128)(2,1)S(1)} %bitcast.16, bf16[2,608,128]{2,1,0:T(8,128)(2,1)S(1)} %bitcast.27, bf16[256,128]{1,0:T(8,128)(2,1)S(1)} %get-tuple-element.26.recv, ...), custom_call_target="tpu_custom_call" | custom-call | tf_op jit(solution)/shard_map/pallas_call | solution.py:271
  44.8 8.8 %all_to_all.25.agg4 = bf16[4,256,128]{2,1,0:T(8,128)(2,1)S(1)} all-to-all(bf16[4,256,128]{2,1,0:T(8,128)(2,1)S(1)} %get-tuple-element.29), channel_id=1, replica_groups=mesh['band'=128,'chan'=4] {'chan'}, dimensions={0} | all-to-all | bytes 524288 | tf_op jit(solution)/shard_map/all_to_all | solution.py:286
  53.6 0.8 shard_map.175
  54.3 2.8 %all-gather.3 = bf16[512,128]{1,0:T(8,128)(2,1)S(1)} all-gather(bf16[256,128]{1,0:T(8,128)(2,1)S(1)} %get-tuple-element.34), channel_id=5, replica_groups={{0,4},{8,12},{16,20},{24,28},{32,36},{40,44},{48,52},{56,60},{64,68},{7..., dimensions={0}, use_global_device_ids=true | all-gather | bytes 196608 | tf_op jit(solution)/shard_map/all_gather | solution.py:291
  57.1 5.1 %all-gather.4 = bf16[4,256,128]{2,1,0:T(8,128)(2,1)S(1)} all-gather(bf16[2,256,128]{2,1,0:T(8,128)(2,1)S(1)} %bitcast.28), channel_id=6, replica_groups={{4,8},{12,16},{20,24},{28,32},{36,40},{44,48},{52,56},{60,64},{68,72},{..., dimensions={0}, use_global_device_ids=true | all-gather | bytes 393216 | tf_op jit(solution)/shard_map/all_gather | solution.py:298
  62.2 5.2 %all-gather.5 = bf16[2,1,256,128]{3,2,1,0:T(8,128)(2,1)S(1)} all-gather(bf16[1,1,256,128]{3,2,1,0:T(8,128)(2,1)S(1)} %slice_select_fusion.3), channel_id=7, replica_groups={{0,4},{8,12},{16,20},{24,28},{32,36},{40,44},{48,52},{56,60},{64,68},{7..., dimensions={0}, use_global_device_ids=true | all-gather | bytes 196608 | tf_op jit(solution)/shard_map/all_gather | solution.py:291
  68.1 1.1 shard_map.176
  69.2 8.8 %all_to_all.26.agg4 = bf16[4,256,128]{2,1,0:T(8,128)(2,1)S(1)} all-to-all(bf16[4,256,128]{2,1,0:T(8,128)(2,1)S(1)} %shard_map.176), channel_id=1, replica_groups=mesh['band'=128,'chan'=4] {'chan'}, dimensions={0} | all-to-all | bytes 524288 | tf_op jit(solution)/shard_map/all_to_all | solution.py:286
  78.0 0.7 shard_map.177
  78.8 2.7 %all-gather.6 = bf16[512,128]{1,0:T(8,128)(2,1)S(1)} all-gather(bf16[256,128]{1,0:T(8,128)(2,1)S(1)} %get-tuple-element.38), channel_id=8, replica_groups={{0,4},{8,12},{16,20},{24,28},{32,36},{40,44},{48,52},{56,60},{64,68},{7..., dimensions={0}, use_global_device_ids=true | all-gather | bytes 196608 | tf_op jit(solution)/shard_map/all_gather | solution.py:291
  81.5 5.1 %all-gather.7 = bf16[4,256,128]{2,1,0:T(8,128)(2,1)S(1)} all-gather(bf16[2,256,128]{2,1,0:T(8,128)(2,1)S(1)} %bitcast.30), channel_id=9, replica_groups={{4,8},{12,16},{20,24},{28,32},{36,40},{44,48},{52,56},{60,64},{68,72},{..., dimensions={0}, use_global_device_ids=true | all-gather | bytes 393216 | tf_op jit(solution)/shard_map/all_gather | solution.py:298
  86.6 5.2 %all-gather.8 = bf16[2,1,256,128]{3,2,1,0:T(8,128)(2,1)S(1)} all-gather(bf16[1,1,256,128]{3,2,1,0:T(8,128)(2,1)S(1)} %slice_select_fusion.2), channel_id=10, replica_groups={{0,4},{8,12},{16,20},{24,28},{32,36},{40,44},{48,52},{56,60},{64,68},{7..., dimensions={0}, use_global_device_ids=true | all-gather | bytes 196608 | tf_op jit(solution)/shard_map/all_gather | solution.py:291
  91.8 1.1 shard_map.178
  92.9 9.0 %all_to_all.27.agg4 = bf16[4,256,128]{2,1,0:T(8,128)(2,1)S(1)} all-to-all(bf16[4,256,128]{2,1,0:T(8,128)(2,1)S(1)} %shard_map.178), channel_id=1, replica_groups=mesh['band'=128,'chan'=4] {'chan'}, dimensions={0} | all-to-all | bytes 524288 | tf_op jit(solution)/shard_map/all_to_all | solution.py:286
  102.6 2.8 %all-gather.9 = bf16[640,128]{1,0:T(8,128)(2,1)S(1)} all-gather(bf16[320,128]{1,0:T(8,128)(2,1)S(1)} %shard_map.179), channel_id=11, replica_groups={{0,4},{8,12},{16,20},{24,28},{32,36},{40,44},{48,52},{56,60},{64,68},{7..., dimensions={0}, use_global_device_ids=true | all-gather | bytes 245760 | tf_op jit(solution)/shard_map/all_gather | solution.py:291
  105.3 5.7 %all-gather.10 = bf16[4,320,128]{2,1,0:T(8,128)(2,1)S(1)} all-gather(bf16[2,320,128]{2,1,0:T(8,128)(2,1)S(1)} %bitcast.25), channel_id=12, replica_groups={{4,8},{12,16},{20,24},{28,32},{36,40},{44,48},{52,56},{60,64},{68,72},{..., dimensions={0}, use_global_device_ids=true | all-gather | bytes 491520 | tf_op jit(solution)/shard_map/all_gather | solution.py:298
  111.0 4.9 %all-gather.11 = bf16[2,1,320,128]{3,2,1,0:T(8,128)(2,1)S(1)} all-gather(bf16[1,1,320,128]{3,2,1,0:T(8,128)(2,1)S(1)} %slice_select_fusion.1), channel_id=13, replica_groups={{0,4},{8,12},{16,20},{24,28},{32,36},{40,44},{48,52},{56,60},{64,68},{7..., dimensions={0}, use_global_device_ids=true | all-gather | bytes 245760 | tf_op jit(solution)/shard_map/all_gather | solution.py:291
  116.0 2.6 %shard_map.180 = bf16[4,512,128]{2,1,0:T(8,128)(2,1)S(1)} custom-call(bf16[2,320,128]{2,1,0:T(8,128)(2,1)S(1)} %bitcast.26, bf16[2,2,320,128]{3,2,1,0:T(8,128)(2,1)S(1)} %bitcast.20, bf16[2,320,128]{2,1,0:T(8,128)(2,1)S(1)} %bitcast.34, bf16[512,128]{1,0:T(8,128)(2,1)S(1)} %get-tuple-element.41.recv, s32[5,512]{1,0:T(8,128)S(1)} %copy-done.11, ...), custom_call_target="tpu_custom_call" | custom-call | tf_op jit(solution)/shard_map/pallas_call | solution.py:271
  118.6 11.6 %all_to_all.28.agg4 = bf16[4,512,128]{2,1,0:T(8,128)(2,1)S(1)} all-to-all(bf16[4,512,128]{2,1,0:T(8,128)(2,1)S(1)} %shard_map.180), channel_id=1, replica_groups=mesh['band'=128,'chan'=4] {'chan'}, dimensions={0} | all-to-all | bytes 1048576 | tf_op jit(solution)/shard_map/all_to_all | solution.py:286
  130.3 1.2 shard_map.181
  (47 shorter events, 1.6 us)
Async XLA Ops:
  0.0 0.9 copy-start.18
  0.9 5.9 %copy-start = (bf16[2,3,512,128]{3,2,1,0:T(8,128)(2,1)S(1)}, bf16[2,3,512,128]{3,2,1,0:T(8,128)(2,1)}, u32[]{:S(2)}) copy-start(bf16[2,3,512,128]{3,2,1,0:T(8,128)(2,1)} %rest_0_.4) | copy-start | bytes 2359300
  1.8 5.1 %copy-start.1 = (bf16[512,227]{0,1:T(8,128)(2,1)S(1)}, bf16[512,227]{0,1:T(8,128)(2,1)}, u32[]{:S(2)}) copy-start(bf16[512,227]{0,1:T(8,128)(2,1)} %param.18) | copy-start | bytes 697348
  1.8 5.1 %copy-start.2 = (bf16[512,128]{1,0:T(8,128)(2,1)S(1)}, bf16[512,128]{1,0:T(8,128)(2,1)}, u32[]{:S(2)}) copy-start(bf16[512,128]{1,0:T(8,128)(2,1)} %rest_1_.2) | copy-start | bytes 393220
  1.8 5.1 %copy-start.3 = (bf16[512,128]{1,0:T(8,128)(2,1)S(1)}, bf16[512,128]{1,0:T(8,128)(2,1)}, u32[]{:S(2)}) copy-start(bf16[512,128]{1,0:T(8,128)(2,1)} %rest_2_.2) | copy-start | bytes 393220
  1.8 5.1 %copy-start.5 = (bf16[512,128]{1,0:T(8,128)(2,1)S(1)}, bf16[512,128]{1,0:T(8,128)(2,1)}, u32[]{:S(2)}) copy-start(bf16[512,128]{1,0:T(8,128)(2,1)} %rest_3_.1) | copy-start | bytes 393220
  1.8 5.1 %copy-start.7 = (s32[5,512]{1,0:T(8,128)S(1)}, s32[5,512]{1,0:T(8,128)}, u32[]{:S(2)}) copy-start(s32[5,512]{1,0:T(8,128)} %rest_4_.1) | copy-start | bytes 30724
  1.8 5.1 %copy-start.8 = (s32[5,512]{1,0:T(8,128)S(1)}, s32[5,512]{1,0:T(8,128)}, u32[]{:S(2)}) copy-start(s32[5,512]{1,0:T(8,128)} %rest_5_.1) | copy-start | bytes 30724
  1.8 5.1 %copy-start.9 = (bf16[512,128]{1,0:T(8,128)(2,1)S(1)}, bf16[512,128]{1,0:T(8,128)(2,1)}, u32[]{:S(2)}) copy-start(bf16[512,128]{1,0:T(8,128)(2,1)} %w_enc_out) | copy-start | bytes 393220
  1.8 5.1 %copy-start.13 = (s32[5,128]{1,0:T(8,128)S(1)}, s32[5,128]{1,0:T(8,128)}, u32[]{:S(2)}) copy-start(s32[5,128]{1,0:T(8,128)} %proc_src.5) | copy-start | bytes 7684
  1.8 5.1 %copy-start.14 = (s32[5,128]{1,0:T(8,128)S(1)}, s32[5,128]{1,0:T(8,128)}, u32[]{:S(2)}) copy-start(s32[5,128]{1,0:T(8,128)} %proc_dst.5) | copy-start | bytes 7684
  1.9 5.1 %copy-start.15 = (bf16[128,227]{0,1:T(8,128)(2,1)S(1)}, bf16[128,227]{0,1:T(8,128)(2,1)}, u32[]{:S(2)}) copy-start(bf16[128,227]{0,1:T(8,128)(2,1)} %param.27) | copy-start | bytes 174340
  1.9 15.9 %all-to-all-start = ((bf16[4,483,128]{2,1,0:T(8,128)(2,1)}), bf16[4,483,128]{2,1,0:T(8,128)(2,1)S(1)}, u32[]{:S(2)}, u32[]{:S(2)}) async-start(bf16[4,483,128]{2,1,0:T(8,128)(2,1)} %pad_maximum_fusion), calls=%async_computation | async-start | bytes 999424 | tf_op jit(solution)/shard_map/all_to_all | solution.py:286
  7.0 37.8 %collective-permute-start = (bf16[1792,128]{1,0:T(8,128)(2,1)S(1)}, bf16[1792,128]{1,0:T(8,128)(2,1)S(1)}, u32[]{:S(2)}, u32[]{:S(2)}) collective-permute-start(bf16[1792,128]{1,0:T(8,128)(2,1)S(1)} %shard_map.174.b0), channel_id=1, source_target_pairs={{0,1},{1,2},{2,3},{3,0},{4,5},{5,6},{6,7},{7,4},{8,9},{9,10},{10,1... | collective-permute-start | bytes 1376264 | tf_op jit(solution)/shard_map/ppermute | solution.py:322
  10.4 34.4 %collective-permute-start.1 = (bf16[1792,128]{1,0:T(8,128)(2,1)S(1)}, bf16[1792,128]{1,0:T(8,128)(2,1)S(1)}, u32[]{:S(2)}, u32[]{:S(2)}) collective-permute-start(bf16[1792,128]{1,0:T(8,128)(2,1)S(1)} %shard_map.174.b0), channel_id=1, source_target_pairs={{0,2},{1,3},{2,0},{3,1},{4,6},{5,7},{6,4},{7,5},{8,10},{9,11},{10,... | collective-permute-start | bytes 1376264 | tf_op jit(solution)/shard_map/ppermute | solution.py:322
  14.7 30.1 %collective-permute-start.2 = (bf16[1792,128]{1,0:T(8,128)(2,1)S(1)}, bf16[1792,128]{1,0:T(8,128)(2,1)S(1)}, u32[]{:S(2)}, u32[]{:S(2)}) collective-permute-start(bf16[1792,128]{1,0:T(8,128)(2,1)S(1)} %shard_map.174.b0), channel_id=1, source_target_pairs={{0,3},{1,0},{2,1},{3,2},{4,7},{5,4},{6,5},{7,6},{8,11},{9,8},{10,9... | collective-permute-start | bytes 1376264 | tf_op jit(solution)/shard_map/ppermute | solution.py:322
  17.8 0.9 copy-start.4
  18.7 0.9 copy-start.6
  62.2 5.2 %copy-start.17 = (s32[1,1024]{1,0:T(1,128)S(1)}, s32[1,1024]{1,0:T(1,128)}, u32[]{:S(2)}) copy-start(s32[1,1024]{1,0:T(1,128)} %local_dst.3) | copy-start | bytes 12292
  67.4 0.7 copy-start.16
  92.9 9.0 %copy-start.10 = (bf16[512,128]{1,0:T(8,128)(2,1)S(1)}, bf16[512,128]{1,0:T(8,128)(2,1)}, u32[]{:S(2)}) copy-start(bf16[512,128]{1,0:T(8,128)(2,1)} %rest_0_.5) | copy-start | bytes 393220
  92.9 9.0 %copy-start.11 = (s32[5,512]{1,0:T(8,128)S(1)}, s32[5,512]{1,0:T(8,128)}, u32[]{:S(2)}) copy-start(s32[5,512]{1,0:T(8,128)} %dec_src.1) | copy-start | bytes 30724
  92.9 9.0 %copy-start.12 = (s32[5,512]{1,0:T(8,128)S(1)}, s32[5,512]{1,0:T(8,128)}, u32[]{:S(2)}) copy-start(s32[5,512]{1,0:T(8,128)} %dec_dst.1) | copy-start | bytes 30724

commit v7 on v6

--- a/solution.py
+++ b/solution.py
@@ -80,19 +80,14 @@
 
 
 def pre_kernel(
-    grid_state, big, w_es, w_ed, w_dd, enc_src, enc_dst, proc_src, proc_dst,
-    payload, enc_recv, dec_recv, latent, digits,
+    grid_state, big, w_es, enc_src, enc_dst, proc_src, proc_dst, payload, latent, digits,
 ):
     core = core_index()
     channels, nodes = grid_state.shape
-    grid_latent = silu(dot_first(grid_state[...], wide(big, enc_recv.shape[0], channels))).astype(BF16)
+    first = big.shape[1] - channels
+    grid_latent = silu(dot_first(grid_state[...], wide(big, first, channels))).astype(BF16)
     latent[...] = grid_latent
-    grid_normed = rms(grid_latent).astype(BF16)
-    dec_recv[...] = dot(grid_normed, w_dd[...]).astype(BF16)
-    payload[0:nodes, :] = dot(grid_normed, w_es[...]).astype(BF16)
-    mesh_count = enc_recv.shape[0]
-    mesh_normed = rms(wide(big, 0, mesh_count)).astype(BF16)
-    enc_recv[...] = dot(mesh_normed, w_ed[...]).astype(BF16)
+    payload[0:nodes, :] = dot(rms(grid_latent).astype(BF16), w_es[...]).astype(BF16)
     for t, table in enumerate((enc_src, enc_dst)):
         start = nodes + t * TILE
         payload[start : start + TILE, :] = code_table(digits, table, core, 0).astype(BF16)
@@ -127,13 +122,14 @@
 
 
 def enc_kernel(
-    pair, two, far, recv, enc_src, enc_dst,
+    pair, two, far, big, w_ed, enc_src, enc_dst,
     agg, proc_tab,
 ):
     core = core_index()
-    recv_count = recv.shape[0]
+    recv_count = agg.shape[1]
     send_count = pair.shape[1] - TABLES * TILE
-    recv_t = transposed(recv[...])
+    recv = dot(rms(wide(big, 0, recv_count)).astype(BF16), w_ed[...])
+    recv_t = recv.T.astype(BF16)
     arrivals = []
     for v, (block, offset, second) in enumerate(places(pair, two, far, core)):
         lists = [
@@ -238,20 +234,20 @@
     agg[...] = jnp.broadcast_to(total.T.astype(BF16)[None], agg.shape)
 
 
-def dec_kernel(pair, two, far, recv, dec_src, dec_dst, agg):
+def dec_kernel(pair, two, far, latent, w_dd, dec_src, dec_dst, agg):
     core = core_index()
-    recv_count = recv.shape[0]
+    recv_count = agg.shape[1]
     send_count = pair.shape[1] - 2 * TILE
-    recv_t = transposed(recv[...])
-    total = add_edges(
-        None, transposed(pair[core, 0:send_count, :]), recv_t, dec_src[2:3, :], dec_dst[2:3, :],
-        send_count, recv_count,
-    )
+    recv_t = dot(rms(latent[...]).astype(BF16), w_dd[...]).T.astype(BF16)
+    arrivals = [(pair.at[core], dec_src[2:3, :], dec_dst[2:3, :])]
     for block, offset, second in places(pair, two, far, core):
         src, dst = [
             flat(decode(block[start : start + TILE, :], offset, second), 0, 4)
             for start in (send_count, send_count + TILE)
         ]
+        arrivals.append((block, src, dst))
+    total = None
+    for block, src, dst in arrivals:
         total = add_edges(
             total, transposed(block[0:send_count, :]), recv_t, src, dst, send_count, recv_count
         )
@@ -316,20 +312,15 @@
     )
     early, w_enc_out = lax.optimization_barrier((early, w_enc_out))
     big = exchange(early)
-    soon = (grid_state.T, w_enc_src, w_enc_dst, w_dec_dst, enc_src, enc_dst, proc_src, proc_dst)
+    soon = (grid_state.T, w_enc_src, enc_src, enc_dst, proc_src, proc_dst)
     late = call(late_kernel, shape((late_rows, width)), w_enc_out, w_proc, w_out.T, *soon)
     blocks = [late] + [
         lax.ppermute(late, "chan", [(s, (s + k) % chans) for s in range(chans)]) for k in range(1, chans)
     ]
 
-    payload, recv, dec_recv, grid_latent = call(
+    payload, grid_latent = call(
         pre_kernel,
-        (
-            shape((grid_count + TABLES * TILE, width)),
-            shape((mesh_count, width)),
-            shape((grid_count, width)),
-            shape((grid_count, latent_width)),
-        ),
+        (shape((grid_count + TABLES * TILE, width)), shape((grid_count, latent_width))),
         soon[0], big, *soon[1:],
         scratch=[pltpu.VMEM((16, enc_src.shape[1]), F32)],
     )
@@ -337,7 +328,7 @@
     agg, proc_tab = call(
         enc_kernel,
         (shape((chans, mesh_count, width)), shape((4, 8, LANES), I32)),
-        pair, two, far, recv, enc_src, enc_dst,
+        pair, two, far, big, w_enc_dst, enc_src, enc_dst,
     )
     agg, *blocks = lax.optimization_barrier((agg, *blocks))
     state = big
@@ -361,7 +352,7 @@
     )
     pair, two, far = around(send)
     agg = call(
-        dec_kernel, shape((chans, grid_count, width)), pair, two, far, dec_recv, dec_src, dec_dst
+        dec_kernel, shape((chans, grid_count, width)), pair, two, far, grid_latent, w_dec_dst, dec_src, dec_dst
     )
     last = functools.partial(later_kernel, out_kernel, 3 * latent_width)
     return call(last, shape((channels, grid_count)), exchange(agg), grid_latent, *blocks).T

time: 132 us -> 130 us (0.985)
  local copies, waits for them, and re-layouts: 3.49 us -> 1.68 us
    unnamed x38 -> x34, local copies, waits for them, and re-layouts: 2.57 us -> 0.77 us
where the time goes in v7:
time: 130 us
  blocking collectives  101 us (78%)
  starting transfers between devices  15.7 us (12%)
  Pallas kernels  10.5 us (8%)
  local copies, waits for them, and re-layouts  1.68 us (1%)
    all_gather x8, blocking collectives, core_gather(): lax.all_gather(block, 'band', axis_index_groups=[[s, s + 1] for s in rang...  39.3 us
    all_to_all x4, blocking collectives, exchange(): return lax.all_to_all(copies, 'chan', 0, 0, tiled=True)  38.2 us
    all_gather x4, blocking collectives, around(): two = lax.all_gather(pair, 'band', axis_index_groups=sides)  23.1 us
    ppermute x3, starting transfers between devices, on_device(): lax.ppermute(late, 'chan', [(s, (s + k) % chans) for s in range(chans)])  10.8 us
    pallas_call x10, Pallas kernels, call(): pl.pallas_call(kernel, out_shape=out_shapes, in_specs=[pl.BlockSpec(memor...  10.5 us
    all_to_all x1, starting transfers between devices, exchange(): return lax.all_to_all(copies, 'chan', 0, 0, tiled=True)  4.99 us
  transfers between devices with their start and end apart: 4, of which 0 were waited for; matrix products, arithmetic and copies ran while one was open for 0% of the time, Pallas kernels for 2%

profile of v7, /device:TPU:1, one launch (start us, length us, event | category | flops | bytes accessed | tf_op | source)
XLA Modules:
  0.0 129.8 jit_solution(14737859954931998195)
XLA Ops:
  0.0 0.9 broadcast_in_dim.4
  0.9 0.8 pad_maximum_fusion
  1.8 5.0 %all-to-all-start = ((bf16[4,483,128]{2,1,0:T(8,128)(2,1)}), bf16[4,483,128]{2,1,0:T(8,128)(2,1)S(1)}, u32[]{:S(2)}, u32[]{:S(2)}) async-start(bf16[4,483,128]{2,1,0:T(8,128)(2,1)} %pad_maximum_fusion), calls=%async_computation | async-start | bytes 999424 | tf_op jit(solution)/shard_map/all_to_all | solution.py:282
  6.9 3.4 %collective-permute-start = (bf16[1792,128]{1,0:T(8,128)(2,1)S(1)}, bf16[1792,128]{1,0:T(8,128)(2,1)S(1)}, u32[]{:S(2)}, u32[]{:S(2)}) collective-permute-start(bf16[1792,128]{1,0:T(8,128)(2,1)S(1)} %shard_map.174.b0), channel_id=1, source_target_pairs={{0,1},{1,2},{2,3},{3,0},{4,5},{5,6},{6,7},{7,4},{8,9},{9,10},{10,1... | collective-permute-start | bytes 1376264 | tf_op jit(solution)/shard_map/ppermute | solution.py:318
  10.3 4.3 %collective-permute-start.1 = (bf16[1792,128]{1,0:T(8,128)(2,1)S(1)}, bf16[1792,128]{1,0:T(8,128)(2,1)S(1)}, u32[]{:S(2)}, u32[]{:S(2)}) collective-permute-start(bf16[1792,128]{1,0:T(8,128)(2,1)S(1)} %shard_map.174.b0), channel_id=1, source_target_pairs={{0,2},{1,3},{2,0},{3,1},{4,6},{5,7},{6,4},{7,5},{8,10},{9,11},{10,... | collective-permute-start | bytes 1376264 | tf_op jit(solution)/shard_map/ppermute | solution.py:318
  14.6 3.1 %collective-permute-start.2 = (bf16[1792,128]{1,0:T(8,128)(2,1)S(1)}, bf16[1792,128]{1,0:T(8,128)(2,1)S(1)}, u32[]{:S(2)}, u32[]{:S(2)}) collective-permute-start(bf16[1792,128]{1,0:T(8,128)(2,1)S(1)} %shard_map.174.b0), channel_id=1, source_target_pairs={{0,3},{1,0},{2,1},{3,2},{4,7},{5,4},{6,5},{7,6},{8,11},{9,8},{10,9... | collective-permute-start | bytes 1376264 | tf_op jit(solution)/shard_map/ppermute | solution.py:318
  17.8 0.8 shard_map.172
  18.6 8.3 %all-gather = bf16[1216,128]{1,0:T(8,128)(2,1)S(1)} all-gather(bf16[608,128]{1,0:T(8,128)(2,1)S(1)} %get-tuple-element.23), channel_id=2, replica_groups={{0,4},{8,12},{16,20},{24,28},{32,36},{40,44},{48,52},{56,60},{64,68},{7..., dimensions={0}, use_global_device_ids=true | all-gather | bytes 466944 | tf_op jit(solution)/shard_map/all_gather | solution.py:287
  26.8 7.3 %all-gather.1 = bf16[4,608,128]{2,1,0:T(8,128)(2,1)S(1)} all-gather(bf16[2,608,128]{2,1,0:T(8,128)(2,1)S(1)} %bitcast.17), channel_id=3, replica_groups={{4,8},{12,16},{20,24},{28,32},{36,40},{44,48},{52,56},{60,64},{68,72},{..., dimensions={0}, use_global_device_ids=true | all-gather | bytes 933888 | tf_op jit(solution)/shard_map/all_gather | solution.py:294
  34.2 7.3 %all-gather.2 = bf16[2,1,608,128]{3,2,1,0:T(8,128)(2,1)S(1)} all-gather(bf16[1,1,608,128]{3,2,1,0:T(8,128)(2,1)S(1)} %slice_select_fusion), channel_id=4, replica_groups={{0,4},{8,12},{16,20},{24,28},{32,36},{40,44},{48,52},{56,60},{64,68},{7..., dimensions={0}, use_global_device_ids=true | all-gather | bytes 466944 | tf_op jit(solution)/shard_map/all_gather | solution.py:287
  41.4 1.6 %shard_map.173 = (bf16[4,256,128]{2,1,0:T(8,128)(2,1)S(1)}, s32[4,8,128]{2,1,0:T(8,128)S(1)}) custom-call(bf16[2,608,128]{2,1,0:T(8,128)(2,1)S(1)} %bitcast.18, bf16[2,2,608,128]{3,2,1,0:T(8,128)(2,1)S(1)} %bitcast.16, bf16[2,608,128]{2,1,0:T(8,128)(2,1)S(1)} %bitcast.27, bf16[4,483,128]{2,1,0:T(8,128)(2,1)S(1)} %all-to-all-done.big.state, ...), custom_call_target="tpu_custom_call" | custom-call | tf_op jit(solution)/shard_map/pallas_call | solution.py:267
  43.1 8.8 %all_to_all.25.agg4 = bf16[4,256,128]{2,1,0:T(8,128)(2,1)S(1)} all-to-all(bf16[4,256,128]{2,1,0:T(8,128)(2,1)S(1)} %get-tuple-element.26), channel_id=1, replica_groups=mesh['band'=128,'chan'=4] {'chan'}, dimensions={0} | all-to-all | bytes 524288 | tf_op jit(solution)/shard_map/all_to_all | solution.py:282
  51.9 0.8 shard_map.175
  52.6 2.7 %all-gather.3 = bf16[512,128]{1,0:T(8,128)(2,1)S(1)} all-gather(bf16[256,128]{1,0:T(8,128)(2,1)S(1)} %get-tuple-element.31), channel_id=5, replica_groups={{0,4},{8,12},{16,20},{24,28},{32,36},{40,44},{48,52},{56,60},{64,68},{7..., dimensions={0}, use_global_device_ids=true | all-gather | bytes 196608 | tf_op jit(solution)/shard_map/all_gather | solution.py:287
  55.4 5.1 %all-gather.4 = bf16[4,256,128]{2,1,0:T(8,128)(2,1)S(1)} all-gather(bf16[2,256,128]{2,1,0:T(8,128)(2,1)S(1)} %bitcast.28), channel_id=6, replica_groups={{4,8},{12,16},{20,24},{28,32},{36,40},{44,48},{52,56},{60,64},{68,72},{..., dimensions={0}, use_global_device_ids=true | all-gather | bytes 393216 | tf_op jit(solution)/shard_map/all_gather | solution.py:294
  60.5 5.2 %all-gather.5 = bf16[2,1,256,128]{3,2,1,0:T(8,128)(2,1)S(1)} all-gather(bf16[1,1,256,128]{3,2,1,0:T(8,128)(2,1)S(1)} %slice_select_fusion.3), channel_id=7, replica_groups={{0,4},{8,12},{16,20},{24,28},{32,36},{40,44},{48,52},{56,60},{64,68},{7..., dimensions={0}, use_global_device_ids=true | all-gather | bytes 196608 | tf_op jit(solution)/shard_map/all_gather | solution.py:287
  65.7 0.7 copy-done.14
  66.4 1.1 shard_map.176
  67.5 8.8 %all_to_all.26.agg4 = bf16[4,256,128]{2,1,0:T(8,128)(2,1)S(1)} all-to-all(bf16[4,256,128]{2,1,0:T(8,128)(2,1)S(1)} %shard_map.176), channel_id=1, replica_groups=mesh['band'=128,'chan'=4] {'chan'}, dimensions={0} | all-to-all | bytes 524288 | tf_op jit(solution)/shard_map/all_to_all | solution.py:282
  76.3 0.8 shard_map.177
  77.1 2.7 %all-gather.6 = bf16[512,128]{1,0:T(8,128)(2,1)S(1)} all-gather(bf16[256,128]{1,0:T(8,128)(2,1)S(1)} %get-tuple-element.35), channel_id=8, replica_groups={{0,4},{8,12},{16,20},{24,28},{32,36},{40,44},{48,52},{56,60},{64,68},{7..., dimensions={0}, use_global_device_ids=true | all-gather | bytes 196608 | tf_op jit(solution)/shard_map/all_gather | solution.py:287
  79.8 5.1 %all-gather.7 = bf16[4,256,128]{2,1,0:T(8,128)(2,1)S(1)} all-gather(bf16[2,256,128]{2,1,0:T(8,128)(2,1)S(1)} %bitcast.30), channel_id=9, replica_groups={{4,8},{12,16},{20,24},{28,32},{36,40},{44,48},{52,56},{60,64},{68,72},{..., dimensions={0}, use_global_device_ids=true | all-gather | bytes 393216 | tf_op jit(solution)/shard_map/all_gather | solution.py:294
  84.9 5.2 %all-gather.8 = bf16[2,1,256,128]{3,2,1,0:T(8,128)(2,1)S(1)} all-gather(bf16[1,1,256,128]{3,2,1,0:T(8,128)(2,1)S(1)} %slice_select_fusion.2), channel_id=10, replica_groups={{0,4},{8,12},{16,20},{24,28},{32,36},{40,44},{48,52},{56,60},{64,68},{7..., dimensions={0}, use_global_device_ids=true | all-gather | bytes 196608 | tf_op jit(solution)/shard_map/all_gather | solution.py:287
  90.1 1.1 shard_map.178
  91.2 9.0 %all_to_all.27.agg4 = bf16[4,256,128]{2,1,0:T(8,128)(2,1)S(1)} all-to-all(bf16[4,256,128]{2,1,0:T(8,128)(2,1)S(1)} %shard_map.178), channel_id=1, replica_groups=mesh['band'=128,'chan'=4] {'chan'}, dimensions={0} | all-to-all | bytes 524288 | tf_op jit(solution)/shard_map/all_to_all | solution.py:282
  100.2 0.7 shard_map.179
  100.9 2.8 %all-gather.9 = bf16[640,128]{1,0:T(8,128)(2,1)S(1)} all-gather(bf16[320,128]{1,0:T(8,128)(2,1)S(1)} %shard_map.179), channel_id=11, replica_groups={{0,4},{8,12},{16,20},{24,28},{32,36},{40,44},{48,52},{56,60},{64,68},{7..., dimensions={0}, use_global_device_ids=true | all-gather | bytes 245760 | tf_op jit(solution)/shard_map/all_gather | solution.py:287
  103.6 5.7 %all-gather.10 = bf16[4,320,128]{2,1,0:T(8,128)(2,1)S(1)} all-gather(bf16[2,320,128]{2,1,0:T(8,128)(2,1)S(1)} %bitcast.25), channel_id=12, replica_groups={{4,8},{12,16},{20,24},{28,32},{36,40},{44,48},{52,56},{60,64},{68,72},{..., dimensions={0}, use_global_device_ids=true | all-gather | bytes 491520 | tf_op jit(solution)/shard_map/all_gather | solution.py:294
  109.4 5.1 %all-gather.11 = bf16[2,1,320,128]{3,2,1,0:T(8,128)(2,1)S(1)} all-gather(bf16[1,1,320,128]{3,2,1,0:T(8,128)(2,1)S(1)} %slice_select_fusion.1), channel_id=13, replica_groups={{0,4},{8,12},{16,20},{24,28},{32,36},{40,44},{48,52},{56,60},{64,68},{7..., dimensions={0}, use_global_device_ids=true | all-gather | bytes 245760 | tf_op jit(solution)/shard_map/all_gather | solution.py:287
  114.4 2.5 %shard_map.180 = bf16[4,512,128]{2,1,0:T(8,128)(2,1)S(1)} custom-call(bf16[2,320,128]{2,1,0:T(8,128)(2,1)S(1)} %bitcast.26, bf16[2,2,320,128]{3,2,1,0:T(8,128)(2,1)S(1)} %bitcast.20, bf16[2,320,128]{2,1,0:T(8,128)(2,1)S(1)} %bitcast.34, bf16[512,512]{1,0:T(8,128)(2,1)S(1)} %get-tuple-element.38.latent.state, bf16[512,128]{1,0:T(8,128)(2,1)S(1)} %copy-done.5, ...), custom_call_target="tpu_custom_call" | custom-call | tf_op jit(solution)/shard_map/pallas_call | solution.py:267
  116.9 11.6 %all_to_all.28.agg4 = bf16[4,512,128]{2,1,0:T(8,128)(2,1)S(1)} all-to-all(bf16[4,512,128]{2,1,0:T(8,128)(2,1)S(1)} %shard_map.180), channel_id=1, replica_groups=mesh['band'=128,'chan'=4] {'chan'}, dimensions={0} | all-to-all | bytes 1048576 | tf_op jit(solution)/shard_map/all_to_all | solution.py:282
  128.6 1.2 shard_map.181
  (43 shorter events, 0.2 us)
Async XLA Ops:
  0.0 0.9 copy-start.16
  0.9 5.9 %copy-start = (bf16[2,3,512,128]{3,2,1,0:T(8,128)(2,1)S(1)}, bf16[2,3,512,128]{3,2,1,0:T(8,128)(2,1)}, u32[]{:S(2)}) copy-start(bf16[2,3,512,128]{3,2,1,0:T(8,128)(2,1)} %rest_0_.4) | copy-start | bytes 2359300
  1.8 5.1 %copy-start.1 = (bf16[512,227]{0,1:T(8,128)(2,1)S(1)}, bf16[512,227]{0,1:T(8,128)(2,1)}, u32[]{:S(2)}) copy-start(bf16[512,227]{0,1:T(8,128)(2,1)} %param.18) | copy-start | bytes 697348
  1.8 5.1 %copy-start.2 = (bf16[512,128]{1,0:T(8,128)(2,1)S(1)}, bf16[512,128]{1,0:T(8,128)(2,1)}, u32[]{:S(2)}) copy-start(bf16[512,128]{1,0:T(8,128)(2,1)} %rest_1_.2) | copy-start | bytes 393220
  1.8 5.1 %copy-start.3 = (s32[5,512]{1,0:T(8,128)S(1)}, s32[5,512]{1,0:T(8,128)}, u32[]{:S(2)}) copy-start(s32[5,512]{1,0:T(8,128)} %rest_2_.2) | copy-start | bytes 30724
  1.8 5.1 %copy-start.4 = (s32[5,512]{1,0:T(8,128)S(1)}, s32[5,512]{1,0:T(8,128)}, u32[]{:S(2)}) copy-start(s32[5,512]{1,0:T(8,128)} %rest_3_.1) | copy-start | bytes 30724
  1.8 5.1 %copy-start.6 = (bf16[512,128]{1,0:T(8,128)(2,1)S(1)}, bf16[512,128]{1,0:T(8,128)(2,1)}, u32[]{:S(2)}) copy-start(bf16[512,128]{1,0:T(8,128)(2,1)} %w_enc_out) | copy-start | bytes 393220
  1.8 5.1 %copy-start.11 = (s32[5,128]{1,0:T(8,128)S(1)}, s32[5,128]{1,0:T(8,128)}, u32[]{:S(2)}) copy-start(s32[5,128]{1,0:T(8,128)} %proc_src.5) | copy-start | bytes 7684
  1.8 5.1 %copy-start.12 = (s32[5,128]{1,0:T(8,128)S(1)}, s32[5,128]{1,0:T(8,128)}, u32[]{:S(2)}) copy-start(s32[5,128]{1,0:T(8,128)} %proc_dst.5) | copy-start | bytes 7684
  1.8 5.1 %copy-start.13 = (bf16[128,227]{0,1:T(8,128)(2,1)S(1)}, bf16[128,227]{0,1:T(8,128)(2,1)}, u32[]{:S(2)}) copy-start(bf16[128,227]{0,1:T(8,128)(2,1)} %param.27) | copy-start | bytes 174340
  1.8 15.9 %all-to-all-start = ((bf16[4,483,128]{2,1,0:T(8,128)(2,1)}), bf16[4,483,128]{2,1,0:T(8,128)(2,1)S(1)}, u32[]{:S(2)}, u32[]{:S(2)}) async-start(bf16[4,483,128]{2,1,0:T(8,128)(2,1)} %pad_maximum_fusion), calls=%async_computation | async-start | bytes 999424 | tf_op jit(solution)/shard_map/all_to_all | solution.py:282
  6.9 36.1 %collective-permute-start = (bf16[1792,128]{1,0:T(8,128)(2,1)S(1)}, bf16[1792,128]{1,0:T(8,128)(2,1)S(1)}, u32[]{:S(2)}, u32[]{:S(2)}) collective-permute-start(bf16[1792,128]{1,0:T(8,128)(2,1)S(1)} %shard_map.174.b0), channel_id=1, source_target_pairs={{0,1},{1,2},{2,3},{3,0},{4,5},{5,6},{6,7},{7,4},{8,9},{9,10},{10,1... | collective-permute-start | bytes 1376264 | tf_op jit(solution)/shard_map/ppermute | solution.py:318
  10.3 32.7 %collective-permute-start.1 = (bf16[1792,128]{1,0:T(8,128)(2,1)S(1)}, bf16[1792,128]{1,0:T(8,128)(2,1)S(1)}, u32[]{:S(2)}, u32[]{:S(2)}) collective-permute-start(bf16[1792,128]{1,0:T(8,128)(2,1)S(1)} %shard_map.174.b0), channel_id=1, source_target_pairs={{0,2},{1,3},{2,0},{3,1},{4,6},{5,7},{6,4},{7,5},{8,10},{9,11},{10,... | collective-permute-start | bytes 1376264 | tf_op jit(solution)/shard_map/ppermute | solution.py:318
  14.6 28.4 %collective-permute-start.2 = (bf16[1792,128]{1,0:T(8,128)(2,1)S(1)}, bf16[1792,128]{1,0:T(8,128)(2,1)S(1)}, u32[]{:S(2)}, u32[]{:S(2)}) collective-permute-start(bf16[1792,128]{1,0:T(8,128)(2,1)S(1)} %shard_map.174.b0), channel_id=1, source_target_pairs={{0,3},{1,0},{2,1},{3,2},{4,7},{5,4},{6,5},{7,6},{8,11},{9,8},{10,9... | collective-permute-start | bytes 1376264 | tf_op jit(solution)/shard_map/ppermute | solution.py:318
  34.1 7.3 %copy-start.8 = (bf16[512,128]{1,0:T(8,128)(2,1)S(1)}, bf16[512,128]{1,0:T(8,128)(2,1)}, u32[]{:S(2)}) copy-start(bf16[512,128]{1,0:T(8,128)(2,1)} %w_ed.1) | copy-start | bytes 393220
  60.5 5.2 %copy-start.15 = (s32[1,1024]{1,0:T(1,128)S(1)}, s32[1,1024]{1,0:T(1,128)}, u32[]{:S(2)}) copy-start(s32[1,1024]{1,0:T(1,128)} %local_dst.3) | copy-start | bytes 12292
  65.7 0.7 copy-start.14
  91.2 9.0 %copy-start.7 = (bf16[512,128]{1,0:T(8,128)(2,1)S(1)}, bf16[512,128]{1,0:T(8,128)(2,1)}, u32[]{:S(2)}) copy-start(bf16[512,128]{1,0:T(8,128)(2,1)} %rest_0_.5) | copy-start | bytes 393220
  91.2 9.0 %copy-start.9 = (s32[5,512]{1,0:T(8,128)S(1)}, s32[5,512]{1,0:T(8,128)}, u32[]{:S(2)}) copy-start(s32[5,512]{1,0:T(8,128)} %dec_src.1) | copy-start | bytes 30724
  91.2 9.0 %copy-start.10 = (s32[5,512]{1,0:T(8,128)S(1)}, s32[5,512]{1,0:T(8,128)}, u32[]{:S(2)}) copy-start(s32[5,512]{1,0:T(8,128)} %dec_dst.1) | copy-start | bytes 30724
  109.3 5.1 %copy-start.5 = (bf16[512,128]{1,0:T(8,128)(2,1)S(1)}, bf16[512,128]{1,0:T(8,128)(2,1)}, u32[]{:S(2)}) copy-start(bf16[512,128]{1,0:T(8,128)(2,1)} %w_dd.1) | copy-start | bytes 393220

commit v8 on v7

--- a/solution.py
+++ b/solution.py
@@ -98,7 +98,8 @@
 
 def add_edges(total, send_t, recv_t, src, dst, send_count, recv_count):
     to = one_hot(dst, recv_count)
-    message = silu(dot(send_t, one_hot(src, send_count)) + dot(recv_t, to)).astype(BF16)
+    ends = jnp.concatenate([one_hot(src, send_count), to], axis=0)
+    message = silu(dot(jnp.concatenate([send_t, recv_t], axis=1), ends)).astype(BF16)
     part = dot_last(message, to)
     return part if total is None else total + part
 
@@ -122,12 +123,16 @@
 
 
 def enc_kernel(
-    pair, two, far, big, w_ed, enc_src, enc_dst,
-    agg, proc_tab,
+    pair, two, far, big, w_ed, enc_src, enc_dst, proc_src, proc_dst, local_src, local_dst,
+    agg, proc_tab, inner,
 ):
     core = core_index()
     recv_count = agg.shape[1]
     send_count = pair.shape[1] - TABLES * TILE
+    count = local_src.shape[1]
+    for i, (local, proc) in enumerate(((local_src, proc_src), (local_dst, proc_dst))):
+        inner[i : i + 1, 0:count] = local[...]
+        inner[i : i + 1, count:] = proc[2:3, :]
     recv = dot(rms(wide(big, 0, recv_count)).astype(BF16), w_ed[...])
     recv_t = recv.T.astype(BF16)
     arrivals = []
@@ -217,7 +222,7 @@
         recv[...] = dot(normed, turned(w_recv)).astype(BF16)
 
 
-def proc_kernel(pair, two, far, recv, local_src, local_dst, proc_src, proc_dst, tab, agg):
+def proc_kernel(pair, two, far, recv, inner, tab, agg):
     core = core_index()
     sib = 1 - core
     count = recv.shape[0]
@@ -228,9 +233,7 @@
         total = add_edges(
             total, transposed(block[...]), recv_t, lists[0:1, :], lists[1:2, :], count, count
         )
-    own_src = jnp.concatenate([local_src[...], proc_src[2:3, :]], axis=1)
-    own_dst = jnp.concatenate([local_dst[...], proc_dst[2:3, :]], axis=1)
-    total = add_edges(total, transposed(pair[core]), recv_t, own_src, own_dst, count, count)
+    total = add_edges(total, transposed(pair[core]), recv_t, inner[0:1, :], inner[1:2, :], count, count)
     agg[...] = jnp.broadcast_to(total.T.astype(BF16)[None], agg.shape)
 
 
@@ -325,10 +328,14 @@
         scratch=[pltpu.VMEM((16, enc_src.shape[1]), F32)],
     )
     pair, two, far = around(payload)
-    agg, proc_tab = call(
+    agg, proc_tab, inner = call(
         enc_kernel,
-        (shape((chans, mesh_count, width)), shape((4, 8, LANES), I32)),
-        pair, two, far, big, w_enc_dst, enc_src, enc_dst,
+        (
+            shape((chans, mesh_count, width)),
+            shape((4, 8, LANES), I32),
+            shape((2, local_src.shape[1] + proc_src.shape[1]), I32),
+        ),
+        pair, two, far, big, w_enc_dst, enc_src, enc_dst, proc_src, proc_dst, local_src, local_dst,
     )
     agg, *blocks = lax.optimization_barrier((agg, *blocks))
     state = big
@@ -342,7 +349,7 @@
         pair, two, far = around(send)
         agg = call(
             proc_kernel, shape((chans, mesh_count, width)), pair, two, far, recv,
-            local_src, local_dst, proc_src, proc_dst, proc_tab,
+            inner, proc_tab,
         )
     node = functools.partial(later_kernel, functools.partial(node_kernel, False), 2 * latent_width)
     send = call(

time: 130 us -> 130 us (level)
  no operation moved by 1% of the time
where the time goes in v8:
time: 130 us; the launch traced here: 129 us
  blocking collectives  101 us (78%)
  starting transfers between devices  15.8 us (12%)
  Pallas kernels  10.4 us (8%)
    all_gather x8, blocking collectives, core_gather(): lax.all_gather(block, 'band', axis_index_groups=[[s, s + 1] for s in rang...  39.3 us
    all_to_all x4, blocking collectives, exchange(): return lax.all_to_all(copies, 'chan', 0, 0, tiled=True)  38.2 us
    all_gather x4, blocking collectives, around(): two = lax.all_gather(pair, 'band', axis_index_groups=sides)  23.1 us
    ppermute x3, starting transfers between devices, on_device(): lax.ppermute(late, 'chan', [(s, (s + k) % chans) for s in range(chans)])  10.8 us
    pallas_call x10, Pallas kernels, call(): pl.pallas_call(kernel, out_shape=out_shapes, in_specs=[pl.BlockSpec(memor...  10.4 us
    all_to_all x1, starting transfers between devices, exchange(): return lax.all_to_all(copies, 'chan', 0, 0, tiled=True)  4.99 us
  transfers between devices with their start and end apart: 4, of which 0 were waited for; matrix products, arithmetic and copies ran while one was open for 0% of the time, Pallas kernels for 2%

profile of v8, /device:TPU:1, one launch (start us, length us, event | category | flops | bytes accessed | tf_op | source)
XLA Modules:
  0.0 129.0 jit_solution(14519208590929576123)
XLA Ops:
  0.0 0.9 broadcast_in_dim.4
  0.9 0.8 pad_maximum_fusion
  1.8 0.0 copy-start.11
  1.8 5.0 %all-to-all-start = ((bf16[4,483,128]{2,1,0:T(8,128)(2,1)}), bf16[4,483,128]{2,1,0:T(8,128)(2,1)S(1)}, u32[]{:S(2)}, u32[]{:S(2)}) async-start(bf16[4,483,128]{2,1,0:T(8,128)(2,1)} %pad_maximum_fusion), calls=%async_computation | async-start | bytes 999424 | tf_op jit(solution)/shard_map/all_to_all | solution.py:285
  6.9 3.4 %collective-permute-start = (bf16[1792,128]{1,0:T(8,128)(2,1)S(1)}, bf16[1792,128]{1,0:T(8,128)(2,1)S(1)}, u32[]{:S(2)}, u32[]{:S(2)}) collective-permute-start(bf16[1792,128]{1,0:T(8,128)(2,1)S(1)} %shard_map.174.b0), channel_id=1, source_target_pairs={{0,1},{1,2},{2,3},{3,0},{4,5},{5,6},{6,7},{7,4},{8,9},{9,10},{10,1... | collective-permute-start | bytes 1376264 | tf_op jit(solution)/shard_map/ppermute | solution.py:321
  10.3 4.3 %collective-permute-start.1 = (bf16[1792,128]{1,0:T(8,128)(2,1)S(1)}, bf16[1792,128]{1,0:T(8,128)(2,1)S(1)}, u32[]{:S(2)}, u32[]{:S(2)}) collective-permute-start(bf16[1792,128]{1,0:T(8,128)(2,1)S(1)} %shard_map.174.b0), channel_id=1, source_target_pairs={{0,2},{1,3},{2,0},{3,1},{4,6},{5,7},{6,4},{7,5},{8,10},{9,11},{10,... | collective-permute-start | bytes 1376264 | tf_op jit(solution)/shard_map/ppermute | solution.py:321
  14.6 3.1 %collective-permute-start.2 = (bf16[1792,128]{1,0:T(8,128)(2,1)S(1)}, bf16[1792,128]{1,0:T(8,128)(2,1)S(1)}, u32[]{:S(2)}, u32[]{:S(2)}) collective-permute-start(bf16[1792,128]{1,0:T(8,128)(2,1)S(1)} %shard_map.174.b0), channel_id=1, source_target_pairs={{0,3},{1,0},{2,1},{3,2},{4,7},{5,4},{6,5},{7,6},{8,11},{9,8},{10,9... | collective-permute-start | bytes 1376264 | tf_op jit(solution)/shard_map/ppermute | solution.py:321
  17.8 0.8 shard_map.172
  18.6 8.3 %all-gather = bf16[1216,128]{1,0:T(8,128)(2,1)S(1)} all-gather(bf16[608,128]{1,0:T(8,128)(2,1)S(1)} %get-tuple-element.24), channel_id=2, replica_groups={{0,4},{8,12},{16,20},{24,28},{32,36},{40,44},{48,52},{56,60},{64,68},{7..., dimensions={0}, use_global_device_ids=true | all-gather | bytes 466944 | tf_op jit(solution)/shard_map/all_gather | solution.py:290
  26.8 7.3 %all-gather.1 = bf16[4,608,128]{2,1,0:T(8,128)(2,1)S(1)} all-gather(bf16[2,608,128]{2,1,0:T(8,128)(2,1)S(1)} %bitcast.17), channel_id=3, replica_groups={{4,8},{12,16},{20,24},{28,32},{36,40},{44,48},{52,56},{60,64},{68,72},{..., dimensions={0}, use_global_device_ids=true | all-gather | bytes 933888 | tf_op jit(solution)/shard_map/all_gather | solution.py:297
  34.2 7.3 %all-gather.2 = bf16[2,1,608,128]{3,2,1,0:T(8,128)(2,1)S(1)} all-gather(bf16[1,1,608,128]{3,2,1,0:T(8,128)(2,1)S(1)} %slice_select_fusion), channel_id=4, replica_groups={{0,4},{8,12},{16,20},{24,28},{32,36},{40,44},{48,52},{56,60},{64,68},{7..., dimensions={0}, use_global_device_ids=true | all-gather | bytes 466944 | tf_op jit(solution)/shard_map/all_gather | solution.py:290
  41.5 1.5 %shard_map.173 = (bf16[4,256,128]{2,1,0:T(8,128)(2,1)S(1)}, s32[4,8,128]{2,1,0:T(8,128)S(1)}, s32[2,1152]{1,0:T(2,128)S(1)}) custom-call(bf16[2,608,128]{2,1,0:T(8,128)(2,1)S(1)} %bitcast.18, bf16[2,2,608,128]{3,2,1,0:T(8,128)(2,1)S(1)} %bitcast.16, bf16[2,608,128]{2,1,0:T(8,128)(2,1)S(1)} %bitcast.27, bf16[4,483,128]{2,1,0:T(8,128)(2,1)S(1)} %all-to-all-done.big.state, ...), custom_call_target="tpu_custom_call" | custom-call | tf_op jit(solution)/shard_map/pallas_call | solution.py:270
  43.1 8.8 %all_to_all.25.agg4 = bf16[4,256,128]{2,1,0:T(8,128)(2,1)S(1)} all-to-all(bf16[4,256,128]{2,1,0:T(8,128)(2,1)S(1)} %get-tuple-element.27), channel_id=1, replica_groups=mesh['band'=128,'chan'=4] {'chan'}, dimensions={0} | all-to-all | bytes 524288 | tf_op jit(solution)/shard_map/all_to_all | solution.py:285
  51.9 0.8 shard_map.175
  52.6 2.7 %all-gather.3 = bf16[512,128]{1,0:T(8,128)(2,1)S(1)} all-gather(bf16[256,128]{1,0:T(8,128)(2,1)S(1)} %get-tuple-element.32), channel_id=5, replica_groups={{0,4},{8,12},{16,20},{24,28},{32,36},{40,44},{48,52},{56,60},{64,68},{7..., dimensions={0}, use_global_device_ids=true | all-gather | bytes 196608 | tf_op jit(solution)/shard_map/all_gather | solution.py:290
  55.4 5.1 %all-gather.4 = bf16[4,256,128]{2,1,0:T(8,128)(2,1)S(1)} all-gather(bf16[2,256,128]{2,1,0:T(8,128)(2,1)S(1)} %bitcast.30), channel_id=6, replica_groups={{4,8},{12,16},{20,24},{28,32},{36,40},{44,48},{52,56},{60,64},{68,72},{..., dimensions={0}, use_global_device_ids=true | all-gather | bytes 393216 | tf_op jit(solution)/shard_map/all_gather | solution.py:297
  60.4 5.2 %all-gather.5 = bf16[2,1,256,128]{3,2,1,0:T(8,128)(2,1)S(1)} all-gather(bf16[1,1,256,128]{3,2,1,0:T(8,128)(2,1)S(1)} %slice_select_fusion.3), channel_id=7, replica_groups={{0,4},{8,12},{16,20},{24,28},{32,36},{40,44},{48,52},{56,60},{64,68},{7..., dimensions={0}, use_global_device_ids=true | all-gather | bytes 196608 | tf_op jit(solution)/shard_map/all_gather | solution.py:290
  65.7 1.1 shard_map.176
  66.8 8.8 %all_to_all.26.agg4 = bf16[4,256,128]{2,1,0:T(8,128)(2,1)S(1)} all-to-all(bf16[4,256,128]{2,1,0:T(8,128)(2,1)S(1)} %shard_map.176), channel_id=1, replica_groups=mesh['band'=128,'chan'=4] {'chan'}, dimensions={0} | all-to-all | bytes 524288 | tf_op jit(solution)/shard_map/all_to_all | solution.py:285
  75.6 0.8 shard_map.177
  76.3 2.7 %all-gather.6 = bf16[512,128]{1,0:T(8,128)(2,1)S(1)} all-gather(bf16[256,128]{1,0:T(8,128)(2,1)S(1)} %get-tuple-element.37), channel_id=8, replica_groups={{0,4},{8,12},{16,20},{24,28},{32,36},{40,44},{48,52},{56,60},{64,68},{7..., dimensions={0}, use_global_device_ids=true | all-gather | bytes 196608 | tf_op jit(solution)/shard_map/all_gather | solution.py:290
  79.1 5.1 %all-gather.7 = bf16[4,256,128]{2,1,0:T(8,128)(2,1)S(1)} all-gather(bf16[2,256,128]{2,1,0:T(8,128)(2,1)S(1)} %bitcast.28), channel_id=9, replica_groups={{4,8},{12,16},{20,24},{28,32},{36,40},{44,48},{52,56},{60,64},{68,72},{..., dimensions={0}, use_global_device_ids=true | all-gather | bytes 393216 | tf_op jit(solution)/shard_map/all_gather | solution.py:297
  84.2 5.2 %all-gather.8 = bf16[2,1,256,128]{3,2,1,0:T(8,128)(2,1)S(1)} all-gather(bf16[1,1,256,128]{3,2,1,0:T(8,128)(2,1)S(1)} %slice_select_fusion.2), channel_id=10, replica_groups={{0,4},{8,12},{16,20},{24,28},{32,36},{40,44},{48,52},{56,60},{64,68},{7..., dimensions={0}, use_global_device_ids=true | all-gather | bytes 196608 | tf_op jit(solution)/shard_map/all_gather | solution.py:290
  89.4 1.1 shard_map.178
  90.5 9.0 %all_to_all.27.agg4 = bf16[4,256,128]{2,1,0:T(8,128)(2,1)S(1)} all-to-all(bf16[4,256,128]{2,1,0:T(8,128)(2,1)S(1)} %shard_map.178), channel_id=1, replica_groups=mesh['band'=128,'chan'=4] {'chan'}, dimensions={0} | all-to-all | bytes 524288 | tf_op jit(solution)/shard_map/all_to_all | solution.py:285
  99.5 0.7 shard_map.179
  100.2 2.8 %all-gather.9 = bf16[640,128]{1,0:T(8,128)(2,1)S(1)} all-gather(bf16[320,128]{1,0:T(8,128)(2,1)S(1)} %shard_map.179), channel_id=11, replica_groups={{0,4},{8,12},{16,20},{24,28},{32,36},{40,44},{48,52},{56,60},{64,68},{7..., dimensions={0}, use_global_device_ids=true | all-gather | bytes 245760 | tf_op jit(solution)/shard_map/all_gather | solution.py:290
  102.9 5.7 %all-gather.10 = bf16[4,320,128]{2,1,0:T(8,128)(2,1)S(1)} all-gather(bf16[2,320,128]{2,1,0:T(8,128)(2,1)S(1)} %bitcast.25), channel_id=12, replica_groups={{4,8},{12,16},{20,24},{28,32},{36,40},{44,48},{52,56},{60,64},{68,72},{..., dimensions={0}, use_global_device_ids=true | all-gather | bytes 491520 | tf_op jit(solution)/shard_map/all_gather | solution.py:297
  108.6 5.1 %all-gather.11 = bf16[2,1,320,128]{3,2,1,0:T(8,128)(2,1)S(1)} all-gather(bf16[1,1,320,128]{3,2,1,0:T(8,128)(2,1)S(1)} %slice_select_fusion.1), channel_id=13, replica_groups={{0,4},{8,12},{16,20},{24,28},{32,36},{40,44},{48,52},{56,60},{64,68},{7..., dimensions={0}, use_global_device_ids=true | all-gather | bytes 245760 | tf_op jit(solution)/shard_map/all_gather | solution.py:290
  113.7 2.4 %shard_map.180 = bf16[4,512,128]{2,1,0:T(8,128)(2,1)S(1)} custom-call(bf16[2,320,128]{2,1,0:T(8,128)(2,1)S(1)} %bitcast.26, bf16[2,2,320,128]{3,2,1,0:T(8,128)(2,1)S(1)} %bitcast.20, bf16[2,320,128]{2,1,0:T(8,128)(2,1)S(1)} %bitcast.34, bf16[512,512]{1,0:T(8,128)(2,1)S(1)} %get-tuple-element.40.latent.state, bf16[512,128]{1,0:T(8,128)(2,1)S(1)} %copy-done.5, ...), custom_call_target="tpu_custom_call" | custom-call | tf_op jit(solution)/shard_map/pallas_call | solution.py:270
  116.2 11.6 %all_to_all.28.agg4 = bf16[4,512,128]{2,1,0:T(8,128)(2,1)S(1)} all-to-all(bf16[4,512,128]{2,1,0:T(8,128)(2,1)S(1)} %shard_map.180), channel_id=1, replica_groups=mesh['band'=128,'chan'=4] {'chan'}, dimensions={0} | all-to-all | bytes 1048576 | tf_op jit(solution)/shard_map/all_to_all | solution.py:285
  127.8 1.2 shard_map.181
  (43 shorter events, 0.2 us)
Async XLA Ops:
  0.0 0.9 copy-start.16
  0.9 5.9 %copy-start = (bf16[2,3,512,128]{3,2,1,0:T(8,128)(2,1)S(1)}, bf16[2,3,512,128]{3,2,1,0:T(8,128)(2,1)}, u32[]{:S(2)}) copy-start(bf16[2,3,512,128]{3,2,1,0:T(8,128)(2,1)} %rest_0_.4) | copy-start | bytes 2359300
  1.8 5.1 %copy-start.1 = (bf16[512,227]{0,1:T(8,128)(2,1)S(1)}, bf16[512,227]{0,1:T(8,128)(2,1)}, u32[]{:S(2)}) copy-start(bf16[512,227]{0,1:T(8,128)(2,1)} %param.18) | copy-start | bytes 697348
  1.8 5.1 %copy-start.2 = (bf16[512,128]{1,0:T(8,128)(2,1)S(1)}, bf16[512,128]{1,0:T(8,128)(2,1)}, u32[]{:S(2)}) copy-start(bf16[512,128]{1,0:T(8,128)(2,1)} %rest_1_.2) | copy-start | bytes 393220
  1.8 5.1 %copy-start.3 = (s32[5,512]{1,0:T(8,128)S(1)}, s32[5,512]{1,0:T(8,128)}, u32[]{:S(2)}) copy-start(s32[5,512]{1,0:T(8,128)} %rest_2_.2) | copy-start | bytes 30724
  1.8 5.1 %copy-start.4 = (s32[5,512]{1,0:T(8,128)S(1)}, s32[5,512]{1,0:T(8,128)}, u32[]{:S(2)}) copy-start(s32[5,512]{1,0:T(8,128)} %rest_3_.1) | copy-start | bytes 30724
  1.8 5.1 %copy-start.6 = (bf16[512,128]{1,0:T(8,128)(2,1)S(1)}, bf16[512,128]{1,0:T(8,128)(2,1)}, u32[]{:S(2)}) copy-start(bf16[512,128]{1,0:T(8,128)(2,1)} %w_enc_out) | copy-start | bytes 393220
  1.8 5.1 %copy-start.11 = (bf16[128,227]{0,1:T(8,128)(2,1)S(1)}, bf16[128,227]{0,1:T(8,128)(2,1)}, u32[]{:S(2)}) copy-start(bf16[128,227]{0,1:T(8,128)(2,1)} %param.27) | copy-start | bytes 174340
  1.8 5.1 %copy-start.12 = (s32[5,128]{1,0:T(8,128)S(1)}, s32[5,128]{1,0:T(8,128)}, u32[]{:S(2)}) copy-start(s32[5,128]{1,0:T(8,128)} %rest_4_.1) | copy-start | bytes 7684
  1.8 5.1 %copy-start.13 = (s32[5,128]{1,0:T(8,128)S(1)}, s32[5,128]{1,0:T(8,128)}, u32[]{:S(2)}) copy-start(s32[5,128]{1,0:T(8,128)} %rest_5_.1) | copy-start | bytes 7684
  1.8 15.9 %all-to-all-start = ((bf16[4,483,128]{2,1,0:T(8,128)(2,1)}), bf16[4,483,128]{2,1,0:T(8,128)(2,1)S(1)}, u32[]{:S(2)}, u32[]{:S(2)}) async-start(bf16[4,483,128]{2,1,0:T(8,128)(2,1)} %pad_maximum_fusion), calls=%async_computation | async-start | bytes 999424 | tf_op jit(solution)/shard_map/all_to_all | solution.py:285
  6.9 36.1 %collective-permute-start = (bf16[1792,128]{1,0:T(8,128)(2,1)S(1)}, bf16[1792,128]{1,0:T(8,128)(2,1)S(1)}, u32[]{:S(2)}, u32[]{:S(2)}) collective-permute-start(bf16[1792,128]{1,0:T(8,128)(2,1)S(1)} %shard_map.174.b0), channel_id=1, source_target_pairs={{0,1},{1,2},{2,3},{3,0},{4,5},{5,6},{6,7},{7,4},{8,9},{9,10},{10,1... | collective-permute-start | bytes 1376264 | tf_op jit(solution)/shard_map/ppermute | solution.py:321
  10.3 32.7 %collective-permute-start.1 = (bf16[1792,128]{1,0:T(8,128)(2,1)S(1)}, bf16[1792,128]{1,0:T(8,128)(2,1)S(1)}, u32[]{:S(2)}, u32[]{:S(2)}) collective-permute-start(bf16[1792,128]{1,0:T(8,128)(2,1)S(1)} %shard_map.174.b0), channel_id=1, source_target_pairs={{0,2},{1,3},{2,0},{3,1},{4,6},{5,7},{6,4},{7,5},{8,10},{9,11},{10,... | collective-permute-start | bytes 1376264 | tf_op jit(solution)/shard_map/ppermute | solution.py:321
  14.6 28.4 %collective-permute-start.2 = (bf16[1792,128]{1,0:T(8,128)(2,1)S(1)}, bf16[1792,128]{1,0:T(8,128)(2,1)S(1)}, u32[]{:S(2)}, u32[]{:S(2)}) collective-permute-start(bf16[1792,128]{1,0:T(8,128)(2,1)S(1)} %shard_map.174.b0), channel_id=1, source_target_pairs={{0,3},{1,0},{2,1},{3,2},{4,7},{5,4},{6,5},{7,6},{8,11},{9,8},{10,9... | collective-permute-start | bytes 1376264 | tf_op jit(solution)/shard_map/ppermute | solution.py:321
  34.1 7.3 %copy-start.8 = (bf16[512,128]{1,0:T(8,128)(2,1)S(1)}, bf16[512,128]{1,0:T(8,128)(2,1)}, u32[]{:S(2)}) copy-start(bf16[512,128]{1,0:T(8,128)(2,1)} %w_ed.1) | copy-start | bytes 393220
  34.2 7.3 %copy-start.14 = (s32[1,1024]{1,0:T(1,128)S(1)}, s32[1,1024]{1,0:T(1,128)}, u32[]{:S(2)}) copy-start(s32[1,1024]{1,0:T(1,128)} %local_src.1) | copy-start | bytes 12292
  34.2 7.3 %copy-start.15 = (s32[1,1024]{1,0:T(1,128)S(1)}, s32[1,1024]{1,0:T(1,128)}, u32[]{:S(2)}) copy-start(s32[1,1024]{1,0:T(1,128)} %local_dst.1) | copy-start | bytes 12292
  90.5 9.0 %copy-start.7 = (bf16[512,128]{1,0:T(8,128)(2,1)S(1)}, bf16[512,128]{1,0:T(8,128)(2,1)}, u32[]{:S(2)}) copy-start(bf16[512,128]{1,0:T(8,128)(2,1)} %rest_0_.5) | copy-start | bytes 393220
  90.5 9.0 %copy-start.9 = (s32[5,512]{1,0:T(8,128)S(1)}, s32[5,512]{1,0:T(8,128)}, u32[]{:S(2)}) copy-start(s32[5,512]{1,0:T(8,128)} %dec_src.1) | copy-start | bytes 30724
  90.5 9.0 %copy-start.10 = (s32[5,512]{1,0:T(8,128)S(1)}, s32[5,512]{1,0:T(8,128)}, u32[]{:S(2)}) copy-start(s32[5,512]{1,0:T(8,128)} %dec_dst.1) | copy-start | bytes 30724
  108.6 5.1 %copy-start.5 = (bf16[512,128]{1,0:T(8,128)(2,1)S(1)}, bf16[512,128]{1,0:T(8,128)(2,1)}, u32[]{:S(2)}) copy-start(bf16[512,128]{1,0:T(8,128)(2,1)} %w_dd.1) | copy-start | bytes 393220

commit v9 on v8

--- a/solution.py
+++ b/solution.py
@@ -36,6 +36,10 @@
 
 def dot_last(a, b):
     return lax.dot_general(a, b, (((1,), (1,)), ((), ())), preferred_element_type=F32)
+
+
+def flipped(weight, rows):
+    return lax.dot_general(weight, rows, (((0,), (1,)), ((), ())), preferred_element_type=F32)
 
 
 def wide(ref, start, size):
@@ -216,24 +220,26 @@
     def turned(weight):
         return jnp.concatenate([weight[columns_at(k), :] for k in range(CHANS)], axis=0)
 
-    send[0:count, :] = dot(normed, turned(w_send)).astype(BF16)
     if has_recv:
         new_state[...] = after
-        recv[...] = dot(normed, turned(w_recv)).astype(BF16)
+        send[...] = flipped(turned(w_send), normed).astype(BF16)
+        recv[...] = flipped(turned(w_recv), normed).astype(BF16)
+    else:
+        send[0:count, :] = dot(normed, turned(w_send)).astype(BF16)
 
 
 def proc_kernel(pair, two, far, recv, inner, tab, agg):
     core = core_index()
     sib = 1 - core
-    count = recv.shape[0]
-    recv_t = transposed(recv[...])
+    count = recv.shape[1]
+    recv_t = recv[...]
     total = None
     for v, block in enumerate((two.at[core, 0], two.at[core, 1], pair.at[sib], far.at[sib])):
         lists = tab[v]
         total = add_edges(
-            total, transposed(block[...]), recv_t, lists[0:1, :], lists[1:2, :], count, count
-        )
-    total = add_edges(total, transposed(pair[core]), recv_t, inner[0:1, :], inner[1:2, :], count, count)
+            total, block[...], recv_t, lists[0:1, :], lists[1:2, :], count, count
+        )
+    total = add_edges(total, pair[core], recv_t, inner[0:1, :], inner[1:2, :], count, count)
     agg[...] = jnp.broadcast_to(total.T.astype(BF16)[None], agg.shape)
 
 
@@ -343,7 +349,7 @@
         kernel = functools.partial(layer_kernel, layer)
         state, send, recv = call(
             functools.partial(later_kernel, kernel, layer * latent_width),
-            (shape((mesh_count, latent_width), F32), shape((mesh_count, width)), shape((mesh_count, width))),
+            (shape((mesh_count, latent_width), F32), shape((width, mesh_count)), shape((width, mesh_count))),
             exchange(agg), state, *blocks, w_proc,
         )
         pair, two, far = around(send)

time: 130 us -> 129 us (level)
  no operation moved by 1% of the time
where the time goes in v9:
time: 129 us
  blocking collectives  101 us (78%)
  starting transfers between devices  15.8 us (12%)
  Pallas kernels  10.3 us (8%)
    all_gather x8, blocking collectives, core_gather(): lax.all_gather(block, 'band', axis_index_groups=[[s, s + 1] for s in rang...  39.3 us
    all_to_all x4, blocking collectives, exchange(): return lax.all_to_all(copies, 'chan', 0, 0, tiled=True)  38.3 us
    all_gather x4, blocking collectives, around(): two = lax.all_gather(pair, 'band', axis_index_groups=sides)  23.1 us
    ppermute x3, starting transfers between devices, on_device(): lax.ppermute(late, 'chan', [(s, (s + k) % chans) for s in range(chans)])  10.8 us
    pallas_call x10, Pallas kernels, call(): pl.pallas_call(kernel, out_shape=out_shapes, in_specs=[pl.BlockSpec(memor...  10.3 us
    all_to_all x1, starting transfers between devices, exchange(): return lax.all_to_all(copies, 'chan', 0, 0, tiled=True)  4.99 us
  transfers between devices with their start and end apart: 4, of which 0 were waited for; matrix products, arithmetic and copies ran while one was open for 0% of the time, Pallas kernels for 2%

profile of v9, /device:TPU:1, one launch (start us, length us, event | category | flops | bytes accessed | tf_op | source)
XLA Modules:
  0.0 128.9 jit_solution(8839028008184440835)
XLA Ops:
  0.0 0.9 broadcast_in_dim.4
  0.9 0.8 pad_maximum_fusion
  1.8 0.0 copy-start.11
  1.8 5.0 %all-to-all-start = ((bf16[4,483,128]{2,1,0:T(8,128)(2,1)}), bf16[4,483,128]{2,1,0:T(8,128)(2,1)S(1)}, u32[]{:S(2)}, u32[]{:S(2)}) async-start(bf16[4,483,128]{2,1,0:T(8,128)(2,1)} %pad_maximum_fusion), calls=%async_computation | async-start | bytes 999424 | tf_op jit(solution)/shard_map/all_to_all | solution.py:291
  6.9 3.4 %collective-permute-start = (bf16[1792,128]{1,0:T(8,128)(2,1)S(1)}, bf16[1792,128]{1,0:T(8,128)(2,1)S(1)}, u32[]{:S(2)}, u32[]{:S(2)}) collective-permute-start(bf16[1792,128]{1,0:T(8,128)(2,1)S(1)} %shard_map.174.b0), channel_id=1, source_target_pairs={{0,1},{1,2},{2,3},{3,0},{4,5},{5,6},{6,7},{7,4},{8,9},{9,10},{10,1... | collective-permute-start | bytes 1376264 | tf_op jit(solution)/shard_map/ppermute | solution.py:327
  10.3 4.3 %collective-permute-start.1 = (bf16[1792,128]{1,0:T(8,128)(2,1)S(1)}, bf16[1792,128]{1,0:T(8,128)(2,1)S(1)}, u32[]{:S(2)}, u32[]{:S(2)}) collective-permute-start(bf16[1792,128]{1,0:T(8,128)(2,1)S(1)} %shard_map.174.b0), channel_id=1, source_target_pairs={{0,2},{1,3},{2,0},{3,1},{4,6},{5,7},{6,4},{7,5},{8,10},{9,11},{10,... | collective-permute-start | bytes 1376264 | tf_op jit(solution)/shard_map/ppermute | solution.py:327
  14.6 3.1 %collective-permute-start.2 = (bf16[1792,128]{1,0:T(8,128)(2,1)S(1)}, bf16[1792,128]{1,0:T(8,128)(2,1)S(1)}, u32[]{:S(2)}, u32[]{:S(2)}) collective-permute-start(bf16[1792,128]{1,0:T(8,128)(2,1)S(1)} %shard_map.174.b0), channel_id=1, source_target_pairs={{0,3},{1,0},{2,1},{3,2},{4,7},{5,4},{6,5},{7,6},{8,11},{9,8},{10,9... | collective-permute-start | bytes 1376264 | tf_op jit(solution)/shard_map/ppermute | solution.py:327
  17.8 0.8 shard_map.172
  18.6 8.3 %all-gather = bf16[1216,128]{1,0:T(8,128)(2,1)S(1)} all-gather(bf16[608,128]{1,0:T(8,128)(2,1)S(1)} %get-tuple-element.24), channel_id=2, replica_groups={{0,4},{8,12},{16,20},{24,28},{32,36},{40,44},{48,52},{56,60},{64,68},{7..., dimensions={0}, use_global_device_ids=true | all-gather | bytes 466944 | tf_op jit(solution)/shard_map/all_gather | solution.py:296
  26.8 7.3 %all-gather.1 = bf16[4,608,128]{2,1,0:T(8,128)(2,1)S(1)} all-gather(bf16[2,608,128]{2,1,0:T(8,128)(2,1)S(1)} %bitcast.17), channel_id=3, replica_groups={{4,8},{12,16},{20,24},{28,32},{36,40},{44,48},{52,56},{60,64},{68,72},{..., dimensions={0}, use_global_device_ids=true | all-gather | bytes 933888 | tf_op jit(solution)/shard_map/all_gather | solution.py:303
  34.2 7.3 %all-gather.2 = bf16[2,1,608,128]{3,2,1,0:T(8,128)(2,1)S(1)} all-gather(bf16[1,1,608,128]{3,2,1,0:T(8,128)(2,1)S(1)} %slice_select_fusion), channel_id=4, replica_groups={{0,4},{8,12},{16,20},{24,28},{32,36},{40,44},{48,52},{56,60},{64,68},{7..., dimensions={0}, use_global_device_ids=true | all-gather | bytes 466944 | tf_op jit(solution)/shard_map/all_gather | solution.py:296
  41.5 1.5 %shard_map.173 = (bf16[4,256,128]{2,1,0:T(8,128)(2,1)S(1)}, s32[4,8,128]{2,1,0:T(8,128)S(1)}, s32[2,1152]{1,0:T(2,128)S(1)}) custom-call(bf16[2,608,128]{2,1,0:T(8,128)(2,1)S(1)} %bitcast.18, bf16[2,2,608,128]{3,2,1,0:T(8,128)(2,1)S(1)} %bitcast.16, bf16[2,608,128]{2,1,0:T(8,128)(2,1)S(1)} %bitcast.27, bf16[4,483,128]{2,1,0:T(8,128)(2,1)S(1)} %all-to-all-done.big.state, ...), custom_call_target="tpu_custom_call" | custom-call | tf_op jit(solution)/shard_map/pallas_call | solution.py:276
  43.1 8.8 %all_to_all.25.agg4 = bf16[4,256,128]{2,1,0:T(8,128)(2,1)S(1)} all-to-all(bf16[4,256,128]{2,1,0:T(8,128)(2,1)S(1)} %get-tuple-element.27), channel_id=1, replica_groups=mesh['band'=128,'chan'=4] {'chan'}, dimensions={0} | all-to-all | bytes 524288 | tf_op jit(solution)/shard_map/all_to_all | solution.py:291
  51.9 0.8 shard_map.175
  52.7 2.7 %all-gather.3 = bf16[256,256]{1,0:T(8,128)(2,1)S(1)} all-gather(bf16[128,256]{1,0:T(8,128)(2,1)S(1)} %get-tuple-element.32), channel_id=5, replica_groups={{0,4},{8,12},{16,20},{24,28},{32,36},{40,44},{48,52},{56,60},{64,68},{7..., dimensions={0}, use_global_device_ids=true | all-gather | bytes 196608 | tf_op jit(solution)/shard_map/all_gather | solution.py:296
  55.4 5.1 %all-gather.4 = bf16[4,128,256]{2,1,0:T(8,128)(2,1)S(1)} all-gather(bf16[2,128,256]{2,1,0:T(8,128)(2,1)S(1)} %bitcast.30), channel_id=6, replica_groups={{4,8},{12,16},{20,24},{28,32},{36,40},{44,48},{52,56},{60,64},{68,72},{..., dimensions={0}, use_global_device_ids=true | all-gather | bytes 393216 | tf_op jit(solution)/shard_map/all_gather | solution.py:303
  60.5 5.2 %all-gather.5 = bf16[2,1,128,256]{3,2,1,0:T(8,128)(2,1)S(1)} all-gather(bf16[1,1,128,256]{3,2,1,0:T(8,128)(2,1)S(1)} %slice_select_fusion.3), channel_id=7, replica_groups={{0,4},{8,12},{16,20},{24,28},{32,36},{40,44},{48,52},{56,60},{64,68},{7..., dimensions={0}, use_global_device_ids=true | all-gather | bytes 196608 | tf_op jit(solution)/shard_map/all_gather | solution.py:296
  65.7 1.0 shard_map.176
  66.7 8.8 %all_to_all.26.agg4 = bf16[4,256,128]{2,1,0:T(8,128)(2,1)S(1)} all-to-all(bf16[4,256,128]{2,1,0:T(8,128)(2,1)S(1)} %shard_map.176), channel_id=1, replica_groups=mesh['band'=128,'chan'=4] {'chan'}, dimensions={0} | all-to-all | bytes 524288 | tf_op jit(solution)/shard_map/all_to_all | solution.py:291
  75.6 0.8 shard_map.177
  76.4 2.7 %all-gather.6 = bf16[256,256]{1,0:T(8,128)(2,1)S(1)} all-gather(bf16[128,256]{1,0:T(8,128)(2,1)S(1)} %get-tuple-element.37), channel_id=8, replica_groups={{0,4},{8,12},{16,20},{24,28},{32,36},{40,44},{48,52},{56,60},{64,68},{7..., dimensions={0}, use_global_device_ids=true | all-gather | bytes 196608 | tf_op jit(solution)/shard_map/all_gather | solution.py:296
  79.1 5.1 %all-gather.7 = bf16[4,128,256]{2,1,0:T(8,128)(2,1)S(1)} all-gather(bf16[2,128,256]{2,1,0:T(8,128)(2,1)S(1)} %bitcast.28), channel_id=9, replica_groups={{4,8},{12,16},{20,24},{28,32},{36,40},{44,48},{52,56},{60,64},{68,72},{..., dimensions={0}, use_global_device_ids=true | all-gather | bytes 393216 | tf_op jit(solution)/shard_map/all_gather | solution.py:303
  84.2 5.2 %all-gather.8 = bf16[2,1,128,256]{3,2,1,0:T(8,128)(2,1)S(1)} all-gather(bf16[1,1,128,256]{3,2,1,0:T(8,128)(2,1)S(1)} %slice_select_fusion.2), channel_id=10, replica_groups={{0,4},{8,12},{16,20},{24,28},{32,36},{40,44},{48,52},{56,60},{64,68},{7..., dimensions={0}, use_global_device_ids=true | all-gather | bytes 196608 | tf_op jit(solution)/shard_map/all_gather | solution.py:296
  89.4 1.0 shard_map.178
  90.4 9.0 %all_to_all.27.agg4 = bf16[4,256,128]{2,1,0:T(8,128)(2,1)S(1)} all-to-all(bf16[4,256,128]{2,1,0:T(8,128)(2,1)S(1)} %shard_map.178), channel_id=1, replica_groups=mesh['band'=128,'chan'=4] {'chan'}, dimensions={0} | all-to-all | bytes 524288 | tf_op jit(solution)/shard_map/all_to_all | solution.py:291
  99.4 0.7 shard_map.179
  100.1 2.7 %all-gather.9 = bf16[640,128]{1,0:T(8,128)(2,1)S(1)} all-gather(bf16[320,128]{1,0:T(8,128)(2,1)S(1)} %shard_map.179), channel_id=11, replica_groups={{0,4},{8,12},{16,20},{24,28},{32,36},{40,44},{48,52},{56,60},{64,68},{7..., dimensions={0}, use_global_device_ids=true | all-gather | bytes 245760 | tf_op jit(solution)/shard_map/all_gather | solution.py:296
  102.8 5.7 %all-gather.10 = bf16[4,320,128]{2,1,0:T(8,128)(2,1)S(1)} all-gather(bf16[2,320,128]{2,1,0:T(8,128)(2,1)S(1)} %bitcast.25), channel_id=12, replica_groups={{4,8},{12,16},{20,24},{28,32},{36,40},{44,48},{52,56},{60,64},{68,72},{..., dimensions={0}, use_global_device_ids=true | all-gather | bytes 491520 | tf_op jit(solution)/shard_map/all_gather | solution.py:303
  108.6 5.1 %all-gather.11 = bf16[2,1,320,128]{3,2,1,0:T(8,128)(2,1)S(1)} all-gather(bf16[1,1,320,128]{3,2,1,0:T(8,128)(2,1)S(1)} %slice_select_fusion.1), channel_id=13, replica_groups={{0,4},{8,12},{16,20},{24,28},{32,36},{40,44},{48,52},{56,60},{64,68},{7..., dimensions={0}, use_global_device_ids=true | all-gather | bytes 245760 | tf_op jit(solution)/shard_map/all_gather | solution.py:296
  113.7 2.4 %shard_map.180 = bf16[4,512,128]{2,1,0:T(8,128)(2,1)S(1)} custom-call(bf16[2,320,128]{2,1,0:T(8,128)(2,1)S(1)} %bitcast.26, bf16[2,2,320,128]{3,2,1,0:T(8,128)(2,1)S(1)} %bitcast.20, bf16[2,320,128]{2,1,0:T(8,128)(2,1)S(1)} %bitcast.34, bf16[512,512]{1,0:T(8,128)(2,1)S(1)} %get-tuple-element.40.latent.state, bf16[512,128]{1,0:T(8,128)(2,1)S(1)} %copy-done.5, ...), custom_call_target="tpu_custom_call" | custom-call | tf_op jit(solution)/shard_map/pallas_call | solution.py:276
  116.1 11.6 %all_to_all.28.agg4 = bf16[4,512,128]{2,1,0:T(8,128)(2,1)S(1)} all-to-all(bf16[4,512,128]{2,1,0:T(8,128)(2,1)S(1)} %shard_map.180), channel_id=1, replica_groups=mesh['band'=128,'chan'=4] {'chan'}, dimensions={0} | all-to-all | bytes 1048576 | tf_op jit(solution)/shard_map/all_to_all | solution.py:291
  127.7 1.2 shard_map.181
  (43 shorter events, 0.2 us)
Async XLA Ops:
  0.0 0.9 copy-start.16
  0.9 5.9 %copy-start = (bf16[2,3,512,128]{3,2,1,0:T(8,128)(2,1)S(1)}, bf16[2,3,512,128]{3,2,1,0:T(8,128)(2,1)}, u32[]{:S(2)}) copy-start(bf16[2,3,512,128]{3,2,1,0:T(8,128)(2,1)} %rest_0_.4) | copy-start | bytes 2359300
  1.8 5.1 %copy-start.1 = (bf16[512,227]{0,1:T(8,128)(2,1)S(1)}, bf16[512,227]{0,1:T(8,128)(2,1)}, u32[]{:S(2)}) copy-start(bf16[512,227]{0,1:T(8,128)(2,1)} %param.18) | copy-start | bytes 697348
  1.8 5.1 %copy-start.2 = (bf16[512,128]{1,0:T(8,128)(2,1)S(1)}, bf16[512,128]{1,0:T(8,128)(2,1)}, u32[]{:S(2)}) copy-start(bf16[512,128]{1,0:T(8,128)(2,1)} %rest_1_.2) | copy-start | bytes 393220
  1.8 5.1 %copy-start.3 = (s32[5,512]{1,0:T(8,128)S(1)}, s32[5,512]{1,0:T(8,128)}, u32[]{:S(2)}) copy-start(s32[5,512]{1,0:T(8,128)} %rest_2_.2) | copy-start | bytes 30724
  1.8 5.1 %copy-start.4 = (s32[5,512]{1,0:T(8,128)S(1)}, s32[5,512]{1,0:T(8,128)}, u32[]{:S(2)}) copy-start(s32[5,512]{1,0:T(8,128)} %rest_3_.1) | copy-start | bytes 30724
  1.8 5.1 %copy-start.6 = (bf16[512,128]{1,0:T(8,128)(2,1)S(1)}, bf16[512,128]{1,0:T(8,128)(2,1)}, u32[]{:S(2)}) copy-start(bf16[512,128]{1,0:T(8,128)(2,1)} %w_enc_out) | copy-start | bytes 393220
  1.8 5.1 %copy-start.11 = (bf16[128,227]{0,1:T(8,128)(2,1)S(1)}, bf16[128,227]{0,1:T(8,128)(2,1)}, u32[]{:S(2)}) copy-start(bf16[128,227]{0,1:T(8,128)(2,1)} %param.27) | copy-start | bytes 174340
  1.8 5.1 %copy-start.12 = (s32[5,128]{1,0:T(8,128)S(1)}, s32[5,128]{1,0:T(8,128)}, u32[]{:S(2)}) copy-start(s32[5,128]{1,0:T(8,128)} %rest_4_.1) | copy-start | bytes 7684
  1.8 5.1 %copy-start.13 = (s32[5,128]{1,0:T(8,128)S(1)}, s32[5,128]{1,0:T(8,128)}, u32[]{:S(2)}) copy-start(s32[5,128]{1,0:T(8,128)} %rest_5_.1) | copy-start | bytes 7684
  1.8 15.9 %all-to-all-start = ((bf16[4,483,128]{2,1,0:T(8,128)(2,1)}), bf16[4,483,128]{2,1,0:T(8,128)(2,1)S(1)}, u32[]{:S(2)}, u32[]{:S(2)}) async-start(bf16[4,483,128]{2,1,0:T(8,128)(2,1)} %pad_maximum_fusion), calls=%async_computation | async-start | bytes 999424 | tf_op jit(solution)/shard_map/all_to_all | solution.py:291
  6.9 36.1 %collective-permute-start = (bf16[1792,128]{1,0:T(8,128)(2,1)S(1)}, bf16[1792,128]{1,0:T(8,128)(2,1)S(1)}, u32[]{:S(2)}, u32[]{:S(2)}) collective-permute-start(bf16[1792,128]{1,0:T(8,128)(2,1)S(1)} %shard_map.174.b0), channel_id=1, source_target_pairs={{0,1},{1,2},{2,3},{3,0},{4,5},{5,6},{6,7},{7,4},{8,9},{9,10},{10,1... | collective-permute-start | bytes 1376264 | tf_op jit(solution)/shard_map/ppermute | solution.py:327
  10.3 32.7 %collective-permute-start.1 = (bf16[1792,128]{1,0:T(8,128)(2,1)S(1)}, bf16[1792,128]{1,0:T(8,128)(2,1)S(1)}, u32[]{:S(2)}, u32[]{:S(2)}) collective-permute-start(bf16[1792,128]{1,0:T(8,128)(2,1)S(1)} %shard_map.174.b0), channel_id=1, source_target_pairs={{0,2},{1,3},{2,0},{3,1},{4,6},{5,7},{6,4},{7,5},{8,10},{9,11},{10,... | collective-permute-start | bytes 1376264 | tf_op jit(solution)/shard_map/ppermute | solution.py:327
  14.6 28.4 %collective-permute-start.2 = (bf16[1792,128]{1,0:T(8,128)(2,1)S(1)}, bf16[1792,128]{1,0:T(8,128)(2,1)S(1)}, u32[]{:S(2)}, u32[]{:S(2)}) collective-permute-start(bf16[1792,128]{1,0:T(8,128)(2,1)S(1)} %shard_map.174.b0), channel_id=1, source_target_pairs={{0,3},{1,0},{2,1},{3,2},{4,7},{5,4},{6,5},{7,6},{8,11},{9,8},{10,9... | collective-permute-start | bytes 1376264 | tf_op jit(solution)/shard_map/ppermute | solution.py:327
  34.1 7.3 %copy-start.8 = (bf16[512,128]{1,0:T(8,128)(2,1)S(1)}, bf16[512,128]{1,0:T(8,128)(2,1)}, u32[]{:S(2)}) copy-start(bf16[512,128]{1,0:T(8,128)(2,1)} %w_ed.1) | copy-start | bytes 393220
  34.2 7.3 %copy-start.14 = (s32[1,1024]{1,0:T(1,128)S(1)}, s32[1,1024]{1,0:T(1,128)}, u32[]{:S(2)}) copy-start(s32[1,1024]{1,0:T(1,128)} %local_src.1) | copy-start | bytes 12292
  34.2 7.3 %copy-start.15 = (s32[1,1024]{1,0:T(1,128)S(1)}, s32[1,1024]{1,0:T(1,128)}, u32[]{:S(2)}) copy-start(s32[1,1024]{1,0:T(1,128)} %local_dst.1) | copy-start | bytes 12292
  90.4 9.0 %copy-start.7 = (bf16[512,128]{1,0:T(8,128)(2,1)S(1)}, bf16[512,128]{1,0:T(8,128)(2,1)}, u32[]{:S(2)}) copy-start(bf16[512,128]{1,0:T(8,128)(2,1)} %rest_0_.5) | copy-start | bytes 393220
  90.4 9.0 %copy-start.9 = (s32[5,512]{1,0:T(8,128)S(1)}, s32[5,512]{1,0:T(8,128)}, u32[]{:S(2)}) copy-start(s32[5,512]{1,0:T(8,128)} %dec_src.1) | copy-start | bytes 30724
  90.4 9.0 %copy-start.10 = (s32[5,512]{1,0:T(8,128)S(1)}, s32[5,512]{1,0:T(8,128)}, u32[]{:S(2)}) copy-start(s32[5,512]{1,0:T(8,128)} %dec_dst.1) | copy-start | bytes 30724
  108.6 5.1 %copy-start.5 = (bf16[512,128]{1,0:T(8,128)(2,1)S(1)}, bf16[512,128]{1,0:T(8,128)(2,1)}, u32[]{:S(2)}) copy-start(bf16[512,128]{1,0:T(8,128)(2,1)} %w_dd.1) | copy-start | bytes 393220
